TPU v7x, 32 devices: a whole 2x2x4 slice. The times are simulated.
32 devices in a mesh: dp: 8 (over z, y), tensor: 4 (over x, core).
Axes of the slice: x: 2, y: 2, z: 4, core: 2. Of those that a mesh axis runs over, the one named last changes fastest.
Arguments:
- token_ids: int32 [16, 512], P('dp'), may hold values from 0 to 30719
- labels: int32 [16, 512], P('dp'), may hold values 0 or 1
- lengths: int32 [16], P('dp'), may hold values from 128 to 512, as said below
- pair_index: int32 [16], replicated, may hold values from 0 to 15, each once
- embed_table: float32 [31232, 1024], P(('dp', 'tensor')), may hold values from -0.12 to 0.12
- table_first: float32 [31232, 1024], P(('dp', 'tensor')), may hold values from -9.1552734e-05 to 9.1552734e-05
- table_second: float32 [31232, 1024], P(('dp', 'tensor')), may hold values from 5.2470448e-11 to 2.0988179e-10
- vectors: float32 [27650], replicated
- vector_first: float32 [27650], replicated, may hold values from -0.0007324219 to 0.0007324219
- vector_second: float32 [27650], replicated, may hold values from 1.1193695e-09 to 4.477478e-09
- in_proj: float32 [2, 4, 3, 4, 256, 256], P(None, None, None, 'tensor', 'dp'), may hold values from -0.1875 to 0.1875
- out_proj: float32 [2, 4, 4, 256, 256], P(None, 'tensor', None, 'dp'), may hold values from -3 to 3
- up_proj: float32 [2, 4, 16, 256, 256], P(None, None, 'tensor', 'dp'), may hold values from -0.1875 to 0.1875
- down_proj: float32 [2, 16, 4, 256, 256], P(None, 'tensor', None, 'dp'), may hold values from -0.09375 to 0.09375
- stats_left: float32 [4, 8, 12, 256, 256], P('tensor', 'dp')
- stats_right: float32 [4, 8, 12, 256, 256], P('tensor', 'dp')
- root_left: float32 [4, 8, 12, 256, 256], P('tensor', 'dp')
- root_right: float32 [4, 8, 12, 256, 256], P('tensor', 'dp')
Outputs:
- loss: float32 [3], replicated
- grad_norm: float32 [], replicated
- new_in_proj: float32 [2, 4, 3, 4, 256, 256], P(None, None, None, 'tensor', 'dp')
- new_out_proj: float32 [2, 4, 4, 256, 256], P(None, 'tensor', None, 'dp')
- new_up_proj: float32 [2, 4, 16, 256, 256], P(None, None, 'tensor', 'dp')
- new_down_proj: float32 [2, 16, 4, 256, 256], P(None, 'tensor', None, 'dp')
- grad_in_proj: float32 [2, 4, 3, 4, 256, 256], P(None, None, None, 'tensor', 'dp')
- grad_out_proj: float32 [2, 4, 4, 256, 256], P(None, 'tensor', None, 'dp')
- grad_up_proj: float32 [2, 4, 16, 256, 256], P(None, None, 'tensor', 'dp')
- grad_down_proj: float32 [2, 16, 4, 256, 256], P(None, 'tensor', None, 'dp')
- new_stats_left: float32 [4, 8, 12, 256, 256], P('tensor', 'dp')
- new_stats_right: float32 [4, 8, 12, 256, 256], P('tensor', 'dp')
- new_table: float32 [31232, 1024], P(('dp', 'tensor'))
- new_table_first: float32 [31232, 1024], P(('dp', 'tensor'))
- new_table_second: float32 [31232, 1024], P(('dp', 'tensor'))
- new_vectors: float32 [27650], replicated
- new_vector_first: float32 [27650], replicated
- new_vector_second: float32 [27650], replicated
- grad_layer_vectors: float32 [24576], replicated
Inputs may be any that keep to these rules, and one draw needn't show every extreme that they name: `lengths`: the last sequence uses all 512 slots.
All inputs are finite; a program needn't handle non-finite values. No bound on the sum of `labels` on one device may be relied on, other than what follows from the above.
Results may differ from a plain program's by a relative error of at most 0.0085.
Values may be sent and summed in bfloat16 or wider, within the bound.
No kernel may reach another device: no remote copies, remote signals or barrier semaphores. Data moves between devices by JAX's collectives and lax.ppermute only.
A program may use at most 320 MiB of HBM per device.

v0:
```python
from functools import partial

import jax
import jax.numpy as jnp
from jax import lax
from jax.sharding import PartitionSpec as P

D = 1024
HD = 64
FF = 4096
VOCAB = 30720
STEP = 10


PRECISE = lax.Precision.HIGHEST
EPS_NORM = 1e-05
EPS_UNIT = 1e-06
CLIP_NORM = 1.0
BETA_ONE = 0.9
BETA_TWO = 0.999
ADAM_EPS = 1e-08
STAT_DECAY = 0.95
RATE_TABLE = 0.06
RATE_VECTOR = 0.5
RATE_MATRIX = 0.5
RATE_OUT = 4.0
DECAY_TABLE = 0.01
DECAY_MATRIX = 0.01
CON_WEIGHT = 16.0
MASK_FILL = -1000000000.0


def for_sending(array):

    def short(part):
        return part.astype(jnp.bfloat16) if part.dtype == jnp.float32 else part

    return jax.tree.map(short, array)


def layer_norm(values, gain, shift):
    centre = values - jnp.mean(values, axis=-1, keepdims=True)
    spread_sq = jnp.mean(centre * centre, axis=-1, keepdims=True)
    return centre * lax.rsqrt(spread_sq + EPS_NORM) * gain + shift


def norm_back(values, gain, shift, upstream):
    ignored, pull = jax.vjp(layer_norm, values, gain, shift)
    return pull(upstream)


def contrast(pooled, log_scale, pair_index):
    unit_rows = pooled * lax.rsqrt(jnp.sum(pooled * pooled, axis=-1, keepdims=True) + EPS_UNIT)
    partner = jnp.take(unit_rows, pair_index, axis=0)
    logits = jnp.exp(log_scale) * jnp.dot(unit_rows, partner.T, precision=PRECISE)
    matched = jnp.diagonal(logits)
    by_rows = jax.nn.logsumexp(logits, axis=1) - matched
    by_cols = jax.nn.logsumexp(logits, axis=0) - matched
    return 0.5 * (jnp.mean(by_rows) + jnp.mean(by_cols))


def adamw(weight, first, second, grad, rate, decay):
    first = BETA_ONE * first + (1 - BETA_ONE) * grad
    second = BETA_TWO * second + (1 - BETA_TWO) * grad * grad
    fixed_first = first / (1 - BETA_ONE**STEP)
    fixed_second = second / (1 - BETA_TWO**STEP)
    return (
        weight - rate * (fixed_first / (jnp.sqrt(fixed_second) + ADAM_EPS) + decay * weight),
        first,
        second,
    )


def collect(values):
    return lax.all_gather(values, "tensor", axis=0, tiled=True)


def spread(values):
    return lax.psum_scatter(
        values.astype(jnp.bfloat16), "tensor", scatter_dimension=0, tiled=True
    ).astype(jnp.float32)


def collect_grad(values):
    return lax.all_gather(values, "tensor", axis=0, tiled=True)


def spread_grad(values):
    return lax.psum_scatter(
        values.astype(jnp.bfloat16), "tensor", scatter_dimension=0, tiled=True
    ).astype(jnp.float32)


def column_sum(values):
    return jnp.sum(values.astype(jnp.float32), axis=0)


def fetch_weights(in_proj, out_proj, up_proj, down_proj, layer_no, again):
    in_layer = in_proj[layer_no]
    row_blocks = in_layer.shape[0]
    pieces = (
        in_layer.reshape((row_blocks * 3,) + in_layer.shape[2:]),
        out_proj[layer_no],
        up_proj[layer_no],
        down_proj[layer_no],
    )
    pieces = tuple((member.astype(jnp.bfloat16) for member in pieces))
    if again:
        whole = jax.tree.map(
            lambda part, own: part.astype(own.dtype),
            lax.all_gather(for_sending(pieces), "dp", axis=2, tiled=True),
            pieces,
        )
    else:
        whole = jax.tree.map(
            lambda part, own: part.astype(own.dtype),
            lax.all_gather(for_sending(pieces), "dp", axis=2, tiled=True),
            pieces,
        )
    return (whole[0].reshape((row_blocks, 3) + whole[0].shape[1:]), whole[1], whole[2], whole[3])


def scores_of(queries, keys_in, keys_live):
    scores = jnp.einsum(
        "sqhe,skhe->shqk", queries, keys_in, preferred_element_type=jnp.float32
    ) * queries.shape[-1] ** (-0.5)
    return jnp.where(keys_live[:, None, None, :], scores, MASK_FILL)


def layer_forward(residual, weights, pieces, keys_live, head_shape):
    w_in, w_out, w_up, w_down = weights
    bias_q, bias_v, bias_up, bias_out, bias_down, gain_one, shift_one, gain_two, shift_two = pieces
    row_blocks, three_way, local_blocks, block_size, ignored = w_in.shape
    gathered = collect(residual.astype(jnp.bfloat16))
    tokens = gathered.shape[0]
    projected = jnp.einsum(
        "tai,ajcib->tjcb",
        gathered.reshape(tokens, row_blocks, block_size),
        w_in,
        preferred_element_type=jnp.float32,
    ).reshape(tokens, 3, -1)
    queries = (projected[:, 0] + bias_q).astype(jnp.bfloat16)
    keys_in = projected[:, 1].astype(jnp.bfloat16)
    values_in = (projected[:, 2] + bias_v).astype(jnp.bfloat16)
    scores = scores_of(queries.reshape(head_shape), keys_in.reshape(head_shape), keys_live)
    highest = jnp.max(scores, axis=-1, keepdims=True)
    log_total = highest + jnp.log(jnp.sum(jnp.exp(scores - highest), axis=-1, keepdims=True))
    weights_low = jnp.exp(scores - log_total).astype(jnp.bfloat16)
    mixed = jnp.einsum(
        "shqk,skhe->sqhe",
        weights_low,
        values_in.reshape(head_shape),
        preferred_element_type=jnp.float32,
    )
    mixed = mixed.astype(jnp.bfloat16).reshape(tokens, local_blocks, block_size)
    branch = (
        spread(
            jnp.einsum("tai,acib->tcb", mixed, w_out, preferred_element_type=jnp.float32).reshape(
                tokens, -1
            )
        )
        + bias_out
    )
    middle = layer_norm(residual + branch, gain_one, shift_one)
    spread_mid = collect(middle.astype(jnp.bfloat16))
    hidden_pre = (
        jnp.einsum(
            "tai,acib->tcb",
            spread_mid.reshape(tokens, row_blocks, block_size),
            w_up,
            preferred_element_type=jnp.float32,
        ).reshape(tokens, -1)
        + bias_up
    )
    hidden_act = jax.nn.gelu(hidden_pre, approximate=False).astype(jnp.bfloat16)
    fed_out = (
        spread(
            jnp.einsum(
                "tai,acib->tcb",
                hidden_act.reshape(tokens, -1, block_size),
                w_down,
                preferred_element_type=jnp.float32,
            ).reshape(tokens, -1)
        )
        + bias_down
    )
    kept_values = (
        residual,
        branch,
        middle,
        fed_out,
        gathered,
        queries,
        keys_in,
        values_in,
        log_total,
        mixed,
        spread_mid,
        hidden_pre,
        hidden_act,
    )
    return (layer_norm(middle + fed_out, gain_two, shift_two), kept_values)


def attend_back(d_mixed, queries, keys_in, values_in, log_total, keys_live):
    scores = scores_of(queries, keys_in, keys_live)
    weights = jnp.exp(scores - log_total)
    d_values = jnp.einsum(
        "shqk,sqhe->skhe", weights.astype(jnp.bfloat16), d_mixed, preferred_element_type=jnp.float32
    )
    d_weights = jnp.einsum(
        "sqhe,skhe->shqk", d_mixed, values_in, preferred_element_type=jnp.float32
    )
    d_scores = (
        weights * (d_weights - jnp.sum(weights * d_weights, axis=-1, keepdims=True))
    ).astype(jnp.bfloat16)
    scale_by = queries.shape[-1] ** (-0.5)
    d_queries = (
        jnp.einsum("shqk,skhe->sqhe", d_scores, keys_in, preferred_element_type=jnp.float32)
        * scale_by
    )
    d_keys = (
        jnp.einsum("shqk,sqhe->skhe", d_scores, queries, preferred_element_type=jnp.float32)
        * scale_by
    )
    row_count = queries.shape[0] * queries.shape[1]
    return tuple(
        (
            member.reshape(row_count, -1).astype(jnp.bfloat16)
            for member in (d_queries, d_keys, d_values)
        )
    )


def layer_backward(upstream, kept_values, weights, pieces, keys_live, head_shape):
    (
        residual,
        branch,
        middle,
        fed_out,
        gathered,
        queries,
        keys_in,
        values_in,
        log_total,
        mixed,
        spread_mid,
        hidden_pre,
        hidden_act,
    ) = kept_values
    w_in, w_out, w_up, w_down = weights
    bias_q, bias_v, bias_up, bias_out, bias_down, gain_one, shift_one, gain_two, shift_two = pieces
    row_blocks, three_way, local_blocks, block_size, ignored = w_in.shape
    tokens = gathered.shape[0]
    d_second, d_gain_two, d_shift_two = norm_back(middle + fed_out, gain_two, shift_two, upstream)
    d_fed = d_second.astype(jnp.bfloat16)
    d_fed_all = collect_grad(d_fed).reshape(tokens, row_blocks, block_size)
    d_act = jnp.einsum(
        "tcb,acib->tai", d_fed_all, w_down, preferred_element_type=jnp.float32
    ).reshape(tokens, -1)
    d_w_down = jnp.einsum(
        "tai,tcb->acib",
        hidden_act.reshape(tokens, -1, block_size),
        d_fed_all,
        preferred_element_type=jnp.float32,
    )
    ignored_out, gelu_pull = jax.vjp(partial(jax.nn.gelu, approximate=False), hidden_pre)
    d_pre = gelu_pull(d_act)[0].astype(jnp.bfloat16)
    d_up_in = jnp.einsum(
        "tcb,acib->tai",
        d_pre.reshape(tokens, -1, block_size),
        w_up,
        preferred_element_type=jnp.float32,
    ).reshape(tokens, -1)
    d_w_up = jnp.einsum(
        "tai,tcb->acib",
        spread_mid.reshape(tokens, row_blocks, block_size),
        d_pre.reshape(tokens, -1, block_size),
        preferred_element_type=jnp.float32,
    )
    d_middle = d_second + spread_grad(d_up_in)
    d_first, d_gain_one, d_shift_one = norm_back(residual + branch, gain_one, shift_one, d_middle)
    d_branch = d_first.astype(jnp.bfloat16)
    d_branch_all = collect_grad(d_branch).reshape(tokens, row_blocks, block_size)
    d_mixed = jnp.einsum(
        "tcb,acib->tai", d_branch_all, w_out, preferred_element_type=jnp.float32
    ).astype(jnp.bfloat16)
    d_w_out = jnp.einsum("tai,tcb->acib", mixed, d_branch_all, preferred_element_type=jnp.float32)
    d_queries, d_keys, d_values = attend_back(
        d_mixed.reshape(head_shape),
        queries.reshape(head_shape),
        keys_in.reshape(head_shape),
        values_in.reshape(head_shape),
        log_total,
        keys_live,
    )
    d_proj = jnp.stack([d_queries, d_keys, d_values], axis=1).reshape(
        tokens, 3, local_blocks, block_size
    )
    d_in = jnp.einsum("tjcb,ajcib->tai", d_proj, w_in, preferred_element_type=jnp.float32).reshape(
        tokens, -1
    )
    d_w_in = jnp.einsum(
        "tai,tjcb->ajcib",
        gathered.reshape(tokens, row_blocks, block_size),
        d_proj,
        preferred_element_type=jnp.float32,
    )
    d_residual = d_first + spread_grad(d_in)
    bias_grads = (
        column_sum(d_queries),
        column_sum(d_values),
        column_sum(d_pre),
        column_sum(d_branch),
        column_sum(d_fed),
        d_gain_one,
        d_shift_one,
        d_gain_two,
        d_shift_two,
    )
    return (d_residual, (d_w_in, d_w_out, d_w_up, d_w_down), bias_grads)


def shards(
    token_ids,
    labels,
    lengths,
    pair_index,
    embed_table,
    table_first,
    table_second,
    vectors,
    vector_first,
    vector_second,
    in_proj,
    out_proj,
    up_proj,
    down_proj,
    stats_left,
    stats_right,
    root_left,
    root_right,
):
    seq_dev, seq_slots = token_ids.shape
    layers = in_proj.shape[0]
    tensor_ranks = lax.axis_size("tensor")
    owners = lax.axis_size("dp")
    tensor_rank = lax.axis_index("tensor")
    owner_rank = lax.axis_index("dp")
    per_layer = 8 * D + FF
    tail_at = layers * per_layer
    local_width = D // tensor_ranks
    local_hidden = FF // tensor_ranks
    group_rows = seq_dev * seq_slots
    local_rows = group_rows // tensor_ranks
    first_row = tensor_rank * local_rows
    my_rows = first_row + jnp.arange(local_rows)
    my_sequence = my_rows // seq_slots
    my_length = jnp.take(lengths, my_sequence)
    counted = (my_rows % seq_slots < my_length).astype(jnp.float32)
    my_labels = lax.dynamic_slice_in_dim(labels.reshape(-1), first_row, local_rows).astype(
        jnp.float32
    )
    keys_live = jnp.arange(seq_slots)[None, :] < lengths[:, None]
    head_shape = (seq_dev, seq_slots, local_width // HD, HD)
    shard_rows = embed_table.shape[0]
    gathered_table = lax.all_gather(embed_table.astype(jnp.bfloat16), "dp", axis=0, tiled=True)
    gathered_rows = gathered_table.shape[0]

    def locate(row_index):
        owner_block = row_index // shard_rows
        inside = owner_block % tensor_ranks == tensor_rank
        return (inside, owner_block // tensor_ranks * shard_rows + row_index % shard_rows)

    def lookup(inside, at_row):
        picked = jnp.take(gathered_table, jnp.where(inside, at_row, 0), axis=0).astype(jnp.float32)
        return jnp.where(inside[:, None], picked, 0.0)

    token_in, token_at = locate(token_ids.reshape(-1))
    place_in, place_at = locate(VOCAB + jnp.arange(group_rows) % seq_slots)
    embedded = spread(lookup(token_in, token_at) + lookup(place_in, place_at))

    def pieces_of(layer_no):
        base_at = layer_no * per_layer
        bias_q = lax.dynamic_slice_in_dim(vectors, base_at + tensor_rank * local_width, local_width)
        bias_v = lax.dynamic_slice_in_dim(
            vectors, base_at + D + tensor_rank * local_width, local_width
        )
        bias_up = lax.dynamic_slice_in_dim(
            vectors, base_at + 2 * D + tensor_rank * local_hidden, local_hidden
        )
        others = vectors[base_at + 2 * D + FF : base_at + per_layer].reshape(6, D)
        return (bias_q, bias_v, bias_up) + tuple(others)

    gain_embed = vectors[tail_at : tail_at + D]
    shift_embed = vectors[tail_at + D : tail_at + 2 * D]
    head_weight = vectors[tail_at + 2 * D : tail_at + 3 * D]
    residual = layer_norm(embedded, gain_embed, shift_embed)
    kept_all = []
    weights_all = []
    for layer_no in range(layers):
        weights = fetch_weights(in_proj, out_proj, up_proj, down_proj, layer_no, False)
        residual, kept_values = layer_forward(
            residual, weights, pieces_of(layer_no), keys_live, head_shape
        )
        kept_all.append(kept_values)
        weights_all.append(weights)
    logits_tok = jnp.dot(residual, head_weight, precision=PRECISE) + vectors[tail_at + 3 * D]
    bce_part = jnp.sum(counted * (jax.nn.softplus(logits_tok) - my_labels * logits_tok))
    count_part = jnp.sum(counted)
    token_weight = counted / my_length.astype(jnp.float32)
    chooser = (my_sequence[None, :] == jnp.arange(seq_dev)[:, None]).astype(
        jnp.float32
    ) * token_weight[None, :]
    pool_all = lax.all_gather(
        jnp.dot(chooser, residual, precision=PRECISE), ("dp", "tensor"), axis=0, tiled=True
    )
    pooled = jnp.sum(pool_all.reshape(owners, tensor_ranks, seq_dev, D), axis=1).reshape(-1, D)

    def contrast_loss(pooled_in, log_scale):
        return CON_WEIGHT * pooled_in.shape[0] * contrast(pooled_in, log_scale, pair_index)

    scaled_con, con_pull = jax.vjp(contrast_loss, pooled, vectors[tail_at + 3 * D + 1])
    d_pooled, d_scale = con_pull(jnp.ones_like(scaled_con))
    d_logit = counted * (jax.nn.sigmoid(logits_tok) - my_labels)
    global_sequence = owner_rank * seq_dev + my_sequence
    upstream = d_logit[:, None] * head_weight[None, :] + token_weight[:, None] * jnp.take(
        d_pooled, global_sequence, axis=0
    )
    d_head_weight = jnp.dot(d_logit, residual, precision=PRECISE)
    d_head_bias = jnp.sum(d_logit)
    leader = jnp.logical_and(owner_rank == 0, tensor_rank == 0).astype(jnp.float32)
    layer_grads = [None] * layers
    bias_parts = [None] * layers
    for layer_no in reversed(range(layers)):
        weights = fetch_weights(in_proj, out_proj, up_proj, down_proj, layer_no, True)
        upstream, matrix_parts, bias_parts[layer_no] = layer_backward(
            upstream, kept_all[layer_no], weights, pieces_of(layer_no), keys_live, head_shape
        )
        grad_in_local = matrix_parts[0]
        layer_grads[layer_no] = (
            lax.psum_scatter(
                grad_in_local.reshape((-1,) + grad_in_local.shape[2:]),
                "dp",
                scatter_dimension=2,
                tiled=True,
            ),
            lax.psum_scatter(matrix_parts[1], "dp", scatter_dimension=2, tiled=True),
            lax.psum_scatter(matrix_parts[2], "dp", scatter_dimension=2, tiled=True),
            lax.psum_scatter(matrix_parts[3], "dp", scatter_dimension=2, tiled=True),
        )
    d_embed, d_gain_embed, d_shift_embed = norm_back(embedded, gain_embed, shift_embed, upstream)
    d_rows = collect_grad(d_embed.astype(jnp.bfloat16)).astype(jnp.float32)
    table_grad = jnp.zeros(gathered_table.shape, jnp.float32)
    table_grad = table_grad.at[jnp.where(token_in, token_at, gathered_rows)].add(
        d_rows, mode="drop"
    )
    table_grad = table_grad.at[jnp.where(place_in, place_at, gathered_rows)].add(
        d_rows, mode="drop"
    )
    table_shard = lax.psum_scatter(table_grad, "dp", scatter_dimension=0, tiled=True)

    def placed(piece, offset):
        return lax.dynamic_update_slice(jnp.zeros((per_layer,), jnp.float32), piece, (offset,))

    vector_rows = []
    for layer_no in range(layers):
        grad_items = bias_parts[layer_no]
        layer_row = (
            placed(grad_items[0], tensor_rank * local_width)
            + placed(grad_items[1], D + tensor_rank * local_width)
            + placed(grad_items[2], 2 * D + tensor_rank * local_hidden)
        )
        layer_row = layer_row + jnp.concatenate(
            [jnp.zeros((2 * D + FF,), jnp.float32)] + list(grad_items[3:])
        )
        vector_rows.append(layer_row)
    vector_grad = jnp.concatenate(
        vector_rows
        + [d_gain_embed, d_shift_embed, d_head_weight, jnp.stack([d_head_bias, leader * d_scale])]
    )
    matrices = (in_proj, out_proj, up_proj, down_proj)
    matrix_grads = [
        jnp.stack([layer_grads[layer_no][kind_no] for layer_no in range(layers)]).reshape(
            matrices[kind_no].shape
        )
        for kind_no in range(4)
    ]
    squares = jnp.sum(table_shard * table_shard)
    for member in matrix_grads:
        squares = squares + jnp.sum(member * member)
    vector_total, square_total, bce_total, count_total = lax.psum(
        (vector_grad, squares, bce_part, count_part), ("dp", "tensor")
    )
    grad_norm = jnp.sqrt(square_total + jnp.sum(vector_total * vector_total))
    factor = CLIP_NORM / jnp.maximum(grad_norm, CLIP_NORM)
    clipped = [member * factor for member in matrix_grads]
    slot_count = stats_left.shape[2]
    block_size = in_proj.shape[-1]
    rows_per = block_size // owners
    flat_blocks = jnp.concatenate(
        [member.reshape(-1, rows_per, block_size) for member in clipped], axis=0
    )
    block_count = flat_blocks.shape[0]
    padded = jnp.concatenate(
        [
            flat_blocks,
            jnp.zeros((slot_count * owners - block_count, rows_per, block_size), jnp.float32),
        ],
        axis=0,
    )
    outgoing = padded.reshape(slot_count, owners, rows_per, block_size).transpose(1, 0, 2, 3)
    arrived = lax.all_to_all(
        outgoing.astype(jnp.bfloat16), "dp", split_axis=0, concat_axis=0, tiled=True
    ).astype(outgoing.dtype)
    whole_blocks = arrived.transpose(1, 0, 2, 3).reshape(slot_count, block_size, block_size)
    left_stat = stats_left.reshape(whole_blocks.shape)
    right_stat = stats_right.reshape(whole_blocks.shape)
    left_root = root_left.reshape(whole_blocks.shape)
    right_root = root_right.reshape(whole_blocks.shape)
    new_left = STAT_DECAY * left_stat + (1 - STAT_DECAY) * jnp.einsum(
        "sij,skj->sik", whole_blocks, whole_blocks, precision=PRECISE
    )
    new_right = STAT_DECAY * right_stat + (1 - STAT_DECAY) * jnp.einsum(
        "sji,sjk->sik", whole_blocks, whole_blocks, precision=PRECISE
    )
    direction = jnp.einsum(
        "sij,sjk->sik",
        jnp.einsum("sij,sjk->sik", left_root, whole_blocks, precision=PRECISE),
        right_root,
        precision=PRECISE,
    )
    returned = lax.all_to_all(
        direction.reshape(slot_count, owners, rows_per, block_size)
        .transpose(1, 0, 2, 3)
        .astype(jnp.bfloat16),
        "dp",
        split_axis=0,
        concat_axis=0,
        tiled=True,
    ).astype(jnp.float32)
    mine_back = returned.transpose(1, 0, 2, 3).reshape(slot_count * owners, rows_per, block_size)[
        :block_count
    ]
    new_weights = []
    begin_at = 0
    rates = (RATE_MATRIX, RATE_OUT, RATE_MATRIX, RATE_MATRIX)
    for weight, grad_part, rate in zip(matrices, clipped, rates):
        span_of = grad_part.size // (rows_per * block_size)
        update = mine_back[begin_at : begin_at + span_of].reshape(weight.shape)
        new_weights.append(weight - rate * (update + DECAY_MATRIX * weight))
        begin_at = begin_at + span_of
    clipped_vectors = vector_total * factor
    new_table, table_one, table_two = adamw(
        embed_table, table_first, table_second, table_shard * factor, RATE_TABLE, DECAY_TABLE
    )
    new_vectors, vector_one, vector_two = adamw(
        vectors, vector_first, vector_second, clipped_vectors, RATE_VECTOR, 0.0
    )
    loss = jnp.stack([bce_total, count_total, scaled_con])
    return (
        loss,
        grad_norm,
        new_weights[0],
        new_weights[1],
        new_weights[2],
        new_weights[3],
        clipped[0],
        clipped[1],
        clipped[2],
        clipped[3],
        new_left.reshape(stats_left.shape),
        new_right.reshape(stats_right.shape),
        new_table,
        table_one,
        table_two,
        new_vectors,
        vector_one,
        vector_two,
        clipped_vectors[:tail_at],
    )


def solution(mesh):
    placed = (
        P("dp", None),
        P("dp", None),
        P("dp"),
        P(),
        P(("dp", "tensor"), None),
        P(("dp", "tensor"), None),
        P(("dp", "tensor"), None),
        P(),
        P(),
        P(),
        P(None, None, None, "tensor", "dp", None),
        P(None, "tensor", None, "dp", None),
        P(None, None, "tensor", "dp", None),
        P(None, "tensor", None, "dp", None),
        P("tensor", "dp", None, None, None),
        P("tensor", "dp", None, None, None),
        P("tensor", "dp", None, None, None),
        P("tensor", "dp", None, None, None),
    )
    return jax.shard_map(
        shards,
        mesh=mesh,
        in_specs=placed,
        out_specs=(
            P(),
            P(),
            P(None, None, None, "tensor", "dp", None),
            P(None, "tensor", None, "dp", None),
            P(None, None, "tensor", "dp", None),
            P(None, "tensor", None, "dp", None),
            P(None, None, None, "tensor", "dp", None),
            P(None, "tensor", None, "dp", None),
            P(None, None, "tensor", "dp", None),
            P(None, "tensor", None, "dp", None),
            P("tensor", "dp", None, None, None),
            P("tensor", "dp", None, None, None),
            P(("dp", "tensor"), None),
            P(("dp", "tensor"), None),
            P(("dp", "tensor"), None),
            P(),
            P(),
            P(),
            P(),
        ),
        check_vma=False,
    )
```

profile of v0, /device:TPU:0, one launch (start us, length us, event | category | flops | bytes accessed | tf_op | source)
XLA Modules:
  0.0 2942.4 jit_solution(3162660148218701697)
XLA Ops:
  12.5 219.5 %all-gather.24.cloned.1.call-done = bf16[7808,1024]{1,0:T(8,128)(2,1)} async-done(((bf16[976,1024]{1,0:T(8,128)(2,1)}), bf16[7808,1024]{1,0:T(8,128)(2,1)}) %all-gather.24.cloned.1.call-update) | async-done | bytes 15990800 | tf_op jit(solution)/shard_map/all_gather | solution.py:367
  232.0 13.6 gather_fusion.3
  245.6 13.6 gather_fusion.4
  264.0 29.0 reduce-scatter.13.cloned.1.call-done
  302.5 34.0 %all-gather = bf16[1,1,4,256,256]{4,3,2,1,0:T(8,128)(2,1)} all-gather(bf16[1,1,4,32,256]{4,3,2,1,0:T(8,128)(2,1)S(1)} %get-tuple-element.196), channel_id=2, replica_groups=mesh['dp'=8,'tensor'=4] {'dp'}, dimensions={3}, use_global_device_ids=true | all-gather | bytes 589824 | tf_op jit(solution)/shard_map/all_gather | solution.py:117
  343.2 24.8 all-gather.28.cloned.1.call-done
  407.8 25.8 reduce-scatter.15.cloned.1.call-done
  439.9 45.6 %all-gather.48.cloned.1.call-done = bf16[1,4,4,256,256]{4,3,2,1,0:T(8,128)(2,1)} async-done(((bf16[1,4,4,32,256]{4,3,2,1,0:T(8,128)(2,1)}), bf16[1,4,4,256,256]{4,3,2,1,0:T(8,128)(2,1)}) %all-gather.48.cloned.1.call-update) | async-done | bytes 2097168 | tf_op jit(solution)/shard_map/all_gather | solution.py:117
  489.6 46.4 %all-gather.50.cloned.1.call-done = bf16[1,4,4,256,256]{4,3,2,1,0:T(8,128)(2,1)} async-done(((bf16[1,4,4,32,256]{4,3,2,1,0:T(8,128)(2,1)}), bf16[1,4,4,256,256]{4,3,2,1,0:T(8,128)(2,1)}) %all-gather.50.cloned.1.call-update) | async-done | bytes 2097168 | tf_op jit(solution)/shard_map/all_gather | solution.py:117
  540.2 19.1 all-gather.30.cloned.1.call-done
  559.3 14.8 multiply_convert_fusion.3
  579.8 30.9 %reduce-scatter.17.cloned.1.call-done = bf16[256,1024]{1,0:T(8,128)(2,1)} async-done(((bf16[1024,1024]{1,0:T(8,128)(2,1)}), bf16[256,1024]{1,0:T(8,128)(2,1)}) %reduce-scatter.17.cloned.1.call-update) | async-done | bytes 524304 | tf_op jit(solution)/shard_map/reduce_scatter | solution.py:79
  615.3 34.6 %all-gather.3 = bf16[1,1,4,256,256]{4,3,2,1,0:T(8,128)(2,1)} all-gather(bf16[1,1,4,32,256]{4,3,2,1,0:T(8,128)(2,1)S(1)} %get-tuple-element.195), channel_id=5, replica_groups=mesh['dp'=8,'tensor'=4] {'dp'}, dimensions={3}, use_global_device_ids=true | all-gather | bytes 589824 | tf_op jit(solution)/shard_map/all_gather | solution.py:117
  651.9 7.4 all-gather.34.cloned.1.call-done
  659.3 24.4 all-gather.32.cloned.1.call-done
  720.5 29.8 %reduce-scatter.19.cloned.1.call-done = bf16[256,1024]{1,0:T(8,128)(2,1)} async-done(((bf16[1024,1024]{1,0:T(8,128)(2,1)}), bf16[256,1024]{1,0:T(8,128)(2,1)}) %reduce-scatter.19.cloned.1.call-update) | async-done | bytes 524304 | tf_op jit(solution)/shard_map/reduce_scatter | solution.py:79
  754.2 47.6 %all-gather.52.cloned.1.call-done = bf16[1,4,4,256,256]{4,3,2,1,0:T(8,128)(2,1)} async-done(((bf16[1,4,4,32,256]{4,3,2,1,0:T(8,128)(2,1)}), bf16[1,4,4,256,256]{4,3,2,1,0:T(8,128)(2,1)}) %all-gather.52.cloned.1.call-update) | async-done | bytes 2097168 | tf_op jit(solution)/shard_map/all_gather | solution.py:117
  805.9 46.3 %all-gather.54.cloned.1.call-done = bf16[1,4,4,256,256]{4,3,2,1,0:T(8,128)(2,1)} async-done(((bf16[1,4,4,32,256]{4,3,2,1,0:T(8,128)(2,1)}), bf16[1,4,4,256,256]{4,3,2,1,0:T(8,128)(2,1)}) %all-gather.54.cloned.1.call-update) | async-done | bytes 2097168 | tf_op jit(solution)/shard_map/all_gather | solution.py:117
  856.3 19.0 all-gather.36.cloned.1.call-done
  875.3 14.8 multiply_convert_fusion.2
  899.4 27.4 reduce-scatter.21.cloned.1.call-done
  933.5 41.3 %all-gather.6 = f32[32,2,1024]{2,1,0:T(2,128)S(1)} all-gather(f32[1,2,1024]{2,1,0:T(2,128)S(1)} %convolution_bitcast_fusion.10), channel_id=1, replica_groups=mesh['dp'=8,'tensor'=4] {'dp','tensor'}, dimensions={0}, use_global_device_ids=true | all-gather | bytes 270336 | tf_op jit(solution)/shard_map/all_gather | solution.py:415
  994.6 14.1 all-gather.38.cloned.1.call-done
  1008.7 8.4 convert_reduce_fusion
  1022.2 31.5 %reduce-scatter.23.cloned.1.call-done = bf16[256,1024]{1,0:T(8,128)(2,1)} async-done(((bf16[1024,1024]{1,0:T(8,128)(2,1)}), bf16[256,1024]{1,0:T(8,128)(2,1)}) %reduce-scatter.23.cloned.1.call-update) | async-done | bytes 524304 | tf_op jit(solution)/shard_map/reduce_scatter | solution.py:89
  1063.1 19.8 all-gather.40.cloned.1.call-done
  1095.2 6.5 convert_reduce_fusion.5
  1138.9 31.5 %reduce-scatter.25.cloned.1.call-done = bf16[256,1024]{1,0:T(8,128)(2,1)} async-done(((bf16[1024,1024]{1,0:T(8,128)(2,1)}), bf16[256,1024]{1,0:T(8,128)(2,1)}) %reduce-scatter.25.cloned.1.call-update) | async-done | bytes 524304 | tf_op jit(solution)/shard_map/reduce_scatter | solution.py:89
  1181.7 18.0 all-gather.42.cloned.1.call-done
  1199.7 8.4 convert_reduce_fusion.1
  1213.3 31.5 %reduce-scatter.27.cloned.1.call-done = bf16[256,1024]{1,0:T(8,128)(2,1)} async-done(((bf16[1024,1024]{1,0:T(8,128)(2,1)}), bf16[256,1024]{1,0:T(8,128)(2,1)}) %reduce-scatter.27.cloned.1.call-update) | async-done | bytes 524304 | tf_op jit(solution)/shard_map/reduce_scatter | solution.py:89
  1254.7 20.0 all-gather.44.cloned.1.call-done
  1287.1 6.5 convert_reduce_fusion.9
  1330.7 31.5 %reduce-scatter.29.cloned.1.call-done = bf16[256,1024]{1,0:T(8,128)(2,1)} async-done(((bf16[1024,1024]{1,0:T(8,128)(2,1)}), bf16[256,1024]{1,0:T(8,128)(2,1)}) %reduce-scatter.29.cloned.1.call-update) | async-done | bytes 524304 | tf_op jit(solution)/shard_map/reduce_scatter | solution.py:89
  1401.5 6.6 convolution_bitcast_fusion
  1413.7 6.6 convolution_bitcast_fusion.2
  1440.8 6.6 convolution_bitcast_fusion.1
  1453.1 6.6 convolution_bitcast_fusion.3
  1472.1 22.2 scatter_custom_fusion.2
  1494.4 30.5 %scatter_custom_fusion.3 = f32[7808,1024]{1,0:T(8,128)} fusion(f32[7808,1024]{1,0:T(8,128)} %scatter_custom_fusion.2, s32[1024]{0:T(1024)S(1)} %bitcast.603, bf16[1024,1024]{1,0:T(8,128)(2,1)} %all-gather.46.cloned.1.call-done), kind=kCustom, calls=%fused_computation.26 | custom fusion | flops 2097152 | bytes 34078720 | tf_op jit(solution)/shard_map/scatter-add | solution.py:458
  1528.4 69.7 %reduce-scatter.35.cloned.1.call-done = f32[12,1,32,256]{3,2,0,1:T(8,128)} async-done(((f32[12,1,256,256]{3,2,0,1:T(8,128)}), f32[12,1,32,256]{3,2,0,1:T(8,128)}) %reduce-scatter.35.cloned.1.call-update) | async-done | bytes 393232 | tf_op jit(solution)/shard_map/reduce_scatter | solution.py:442
  1598.1 79.0 %reduce-scatter.33.cloned.1.call-done = f32[12,1,32,256]{3,2,0,1:T(8,128)} async-done(((f32[12,1,256,256]{3,2,0,1:T(8,128)}), f32[12,1,32,256]{3,2,0,1:T(8,128)}) %reduce-scatter.33.cloned.1.call-update) | async-done | bytes 393232 | tf_op jit(solution)/shard_map/reduce_scatter | solution.py:442
  1679.0 578.9 %all-reduce.13.cloned.1.call-done = (f32[1,4,256,256]{3,1,0,2:T(4,128)}, f32[1,4,256,256]{3,1,0,2:T(4,128)}, f32[4,4,256,256]{3,1,0,2:T(4,128)}, f32[4,4,256,256...) async-done(((f32[1,4,256,256]{3,1,0,2:T(4,128)}, f32[1,4,256,256]{3,1,0,2:T(4,128)}, f32[4,4,256,256]{3,1,0,2:T(4,128)}, ...) | async-done | bytes 18874384
  2269.7 509.1 %reduce-scatter.31.cloned.1.call-done = f32[976,1024]{1,0:T(8,128)} async-done(((f32[7808,1024]{1,0:T(8,128)}), f32[976,1024]{1,0:T(8,128)}) %reduce-scatter.31.cloned.1.call-update) | async-done | bytes 3997712 | tf_op jit(solution)/shard_map/reduce_scatter | solution.py:461
  2785.8 39.6 %all-reduce.6 = (f32[1]{0:T(128)}, f32[1]{0:T(128)}, f32[]{:T(128)}) all-reduce(f32[1]{0:T(128)} %bitcast.42, f32[1]{0:T(128)} %bitcast.41, f32[]{:T(128)S(6)} %add.920), channel_id=1, replica_groups=mesh['dp'=8,'tensor'=4] {'dp','tensor'}, use_global_device_ids=true, to_apply=%region_22.24 | all-reduce | flops 3 | bytes 24 | tf_op jit(solution)/shard_map/psum | solution.py:492
  2841.9 34.3 %all-to-all-done = bf16[8,12,32,256]{3,2,1,0:T(8,128)(2,1)} async-done(((bf16[8,12,32,256]{3,2,1,0:T(8,128)(2,1)}), bf16[8,12,32,256]{3,2,1,0:T(8,128)(2,1)}, u32[]{:S(2)}, u32[]{:S(2)}) %all-to-all-start) | async-done | bytes 1572896 | tf_op jit(solution)/shard_map/all_to_all | solution.py:513
  2893.9 10.4 multiply_subtract_fusion
  2909.5 16.6 all-to-all-done.1
  (578 shorter events, 462.5 us)
Async XLA Ops:
  7.2 2871.7 %copy-start = (f32[1,1,12,256,256]{4,3,2,1,0:T(8,128)S(1)}, f32[1,1,12,256,256]{4,3,2,1,0:T(8,128)}, u32[]{:S(2)}) copy-start(f32[1,1,12,256,256]{4,3,2,1,0:T(8,128)} %param.36) | copy-start | bytes 9437188
  7.2 224.8 %all-gather.24.cloned.1.call-start = ((), (), s32[]{:S(2)}) async-start(), calls=%async_computation.14 | async-start | bytes 17989632 | tf_op jit(solution)/shard_map/all_gather | solution.py:367
  11.2 281.8 %reduce-scatter.13.cloned.1.call-start = ((), (), s32[]{:S(2)}) async-start(), calls=%async_computation.15 | async-start | bytes 2621440 | tf_op jit(solution)/shard_map/reduce_scatter | solution.py:79
  263.2 39.3 %copy-start.44 = (f32[2,1,4,32,256]{4,3,2,1,0:T(8,128)S(1)}, f32[2,1,4,32,256]{4,3,2,1,0:T(8,128)}, u32[]{:S(2)}) copy-start(f32[2,1,4,32,256]{4,3,2,1,0:T(8,128)} %param.31) | copy-start | bytes 786436
  263.2 76.1 %all-gather.26.cloned.1.call-start = ((), (), s32[]{:S(2)}) async-start(), calls=%async_computation.16 | async-start | bytes 2621440 | tf_op jit(solution)/shard_map/all_gather | solution.py:75
  264.0 346.8 %copy-start.47 = (f32[1024]{0:T(1024)}, f32[1024]{0:T(1024)S(1)}, u32[]{:S(2)}) copy-start(f32[1024]{0:T(1024)S(1)} %get-tuple-element.215) | copy-start | bytes 12292
  264.0 346.8 %copy-start.51 = (f32[1024]{0:T(1024)}, f32[1024]{0:T(1024)S(1)}, u32[]{:S(2)}) copy-start(f32[1024]{0:T(1024)S(1)} %get-tuple-element.214) | copy-start | bytes 12292
  264.0 346.8 %copy-start.53 = (f32[1024]{0:T(1024)}, f32[1024]{0:T(1024)S(1)}, u32[]{:S(2)}) copy-start(f32[1024]{0:T(1024)S(1)} %get-tuple-element.213) | copy-start | bytes 12292
  264.0 346.8 %copy-start.65 = (f32[1024]{0:T(1024)}, f32[1024]{0:T(1024)S(1)}, u32[]{:S(2)}) copy-start(f32[1024]{0:T(1024)S(1)} %get-tuple-element.212) | copy-start | bytes 12292
  294.2 316.6 %copy-start.60 = (f32[256]{0:T(256)}, f32[256]{0:T(256)S(1)}, u32[]{:S(2)}) copy-start(f32[256]{0:T(256)S(1)} %broadcast_multiply_fusion.10) | copy-start | bytes 3076
  296.1 314.7 %copy-start.63 = (f32[256]{0:T(256)}, f32[256]{0:T(256)S(1)}, u32[]{:S(2)}) copy-start(f32[256]{0:T(256)S(1)} %fusion.187) | copy-start | bytes 3076
  298.2 69.8 %all-gather.28.cloned.1.call-start = ((), (), s32[]{:S(2)}) async-start(), calls=%async_computation.17 | async-start | bytes 1769472 | tf_op jit(solution)/shard_map/all_gather | solution.py:117
  300.2 133.3 %reduce-scatter.15.cloned.1.call-start = ((), (), s32[]{:S(2)}) async-start(), calls=%async_computation.18 | async-start | bytes 2621440 | tf_op jit(solution)/shard_map/reduce_scatter | solution.py:79
  301.7 89.0 %copy-start.69 = (f32[4,64]{1,0:T(4,128)}, f32[4,64]{1,0:T(4,128)S(1)}, u32[]{:S(2)}) copy-start(f32[4,64]{1,0:T(4,128)S(1)} %add.839) | copy-start | bytes 3076
  302.5 93.6 %copy-start.82 = (f32[4,64]{1,0:T(4,128)}, f32[4,64]{1,0:T(4,128)S(1)}, u32[]{:S(2)}) copy-start(f32[4,64]{1,0:T(4,128)S(1)} %add.835) | copy-start | bytes 3076
  403.2 82.3 %all-gather.48.cloned.1.call-start = ((), (), s32[]{:S(2)}) async-start(), calls=%async_computation.39 | async-start | bytes 2359296 | tf_op jit(solution)/shard_map/all_gather | solution.py:117
  405.6 130.5 %all-gather.50.cloned.1.call-start = ((), (), s32[]{:S(2)}) async-start(), calls=%async_computation.40 | async-start | bytes 2359296 | tf_op jit(solution)/shard_map/all_gather | solution.py:117
  407.8 151.5 %all-gather.30.cloned.1.call-start = ((), (), s32[]{:S(2)}) async-start(), calls=%async_computation.19 | async-start | bytes 2621440 | tf_op jit(solution)/shard_map/all_gather | solution.py:75
  435.2 175.6 %copy-start.71 = (f32[256]{0:T(256)}, f32[256]{0:T(256)S(1)}, u32[]{:S(2)}) copy-start(f32[256]{0:T(256)S(1)} %broadcast_multiply_fusion.9) | copy-start | bytes 3076
  437.0 103.2 %copy-start.90 = (f32[256]{0:T(256)}, f32[256]{0:T(256)S(1)}, u32[]{:S(2)}) copy-start(f32[256]{0:T(256)S(1)} %multiply_reduce_fusion.16) | copy-start | bytes 3076
  437.0 173.8 %copy-start.80 = (f32[256]{0:T(256)}, f32[256]{0:T(256)S(1)}, u32[]{:S(2)}) copy-start(f32[256]{0:T(256)S(1)} %fusion.188) | copy-start | bytes 3076
  439.8 170.9 %reduce-scatter.17.cloned.1.call-start = ((), (), s32[]{:S(2)}) async-start(), calls=%async_computation.20 | async-start | bytes 2621440 | tf_op jit(solution)/shard_map/reduce_scatter | solution.py:79
  485.5 73.8 %copy-start.93 = (f32[1024]{0:T(1024)S(1)}, f32[1024]{0:T(1024)}, u32[]{:S(2)}) copy-start(f32[1024]{0:T(1024)} %get-tuple-element.210) | copy-start | bytes 12292
  579.2 80.1 %all-gather.34.cloned.1.call-start = ((), (), s32[]{:S(2)}) async-start(), calls=%async_computation.22 | async-start | bytes 1769472 | tf_op jit(solution)/shard_map/all_gather | solution.py:117
  579.8 103.9 %all-gather.32.cloned.1.call-start = ((), (), s32[]{:S(2)}) async-start(), calls=%async_computation.21 | async-start | bytes 2621440 | tf_op jit(solution)/shard_map/all_gather | solution.py:75
  615.0 135.3 %reduce-scatter.19.cloned.1.call-start = ((), (), s32[]{:S(2)}) async-start(), calls=%async_computation.23 | async-start | bytes 2621440 | tf_op jit(solution)/shard_map/reduce_scatter | solution.py:79
  716.6 36.5 %copy-start.73 = (f32[1024]{0:T(1024)S(1)}, f32[1024]{0:T(1024)}, u32[]{:S(2)}) copy-start(f32[1024]{0:T(1024)} %get-tuple-element.204) | copy-start | bytes 12292
  718.7 83.1 %all-gather.52.cloned.1.call-start = ((), (), s32[]{:S(2)}) async-start(), calls=%async_computation.41 | async-start | bytes 2359296 | tf_op jit(solution)/shard_map/all_gather | solution.py:117
  719.5 132.7 %all-gather.54.cloned.1.call-start = ((), (), s32[]{:S(2)}) async-start(), calls=%async_computation.42 | async-start | bytes 2359296 | tf_op jit(solution)/shard_map/all_gather | solution.py:117
  720.0 155.2 %all-gather.36.cloned.1.call-start = ((), (), s32[]{:S(2)}) async-start(), calls=%async_computation.24 | async-start | bytes 2621440 | tf_op jit(solution)/shard_map/all_gather | solution.py:75
  754.2 172.6 %reduce-scatter.21.cloned.1.call-start = ((), (), s32[]{:S(2)}) async-start(), calls=%async_computation.25 | async-start | bytes 2621440 | tf_op jit(solution)/shard_map/reduce_scatter | solution.py:79
  801.8 73.5 %copy-start.95 = (f32[1024]{0:T(1024)S(1)}, f32[1024]{0:T(1024)}, u32[]{:S(2)}) copy-start(f32[1024]{0:T(1024)} %get-tuple-element.203) | copy-start | bytes 12292
  895.2 113.5 %all-gather.38.cloned.1.call-start = ((), (), s32[]{:S(2)}) async-start(), calls=%async_computation.26 | async-start | bytes 2621440 | tf_op jit(solution)/shard_map/all_gather | solution.py:85
  989.8 64.0 %reduce-scatter.23.cloned.1.call-start = ((), (), s32[]{:S(2)}) async-start(), calls=%async_computation.27 | async-start | bytes 2621440 | tf_op jit(solution)/shard_map/reduce_scatter | solution.py:89
  1022.2 60.8 %all-gather.40.cloned.1.call-start = ((), (), s32[]{:S(2)}) async-start(), calls=%async_computation.28 | async-start | bytes 2621440 | tf_op jit(solution)/shard_map/all_gather | solution.py:85
  1060.2 110.2 %reduce-scatter.25.cloned.1.call-start = ((), (), s32[]{:S(2)}) async-start(), calls=%async_computation.29 | async-start | bytes 2621440 | tf_op jit(solution)/shard_map/reduce_scatter | solution.py:89
  1138.9 60.8 %all-gather.42.cloned.1.call-start = ((), (), s32[]{:S(2)}) async-start(), calls=%async_computation.30 | async-start | bytes 2621440 | tf_op jit(solution)/shard_map/all_gather | solution.py:85
  1176.9 67.9 %reduce-scatter.27.cloned.1.call-start = ((), (), s32[]{:S(2)}) async-start(), calls=%async_computation.31 | async-start | bytes 2621440 | tf_op jit(solution)/shard_map/reduce_scatter | solution.py:89
  1213.2 61.5 %all-gather.44.cloned.1.call-start = ((), (), s32[]{:S(2)}) async-start(), calls=%async_computation.32 | async-start | bytes 2621440 | tf_op jit(solution)/shard_map/all_gather | solution.py:85
  1252.0 110.3 %reduce-scatter.29.cloned.1.call-start = ((), (), s32[]{:S(2)}) async-start(), calls=%async_computation.33 | async-start | bytes 2621440 | tf_op jit(solution)/shard_map/reduce_scatter | solution.py:89
  1330.7 141.5 %all-gather.46.cloned.1.call-start = ((), (), s32[]{:S(2)}) async-start(), calls=%async_computation.34 | async-start | bytes 2621440 | tf_op jit(solution)/shard_map/all_gather | solution.py:85
  1367.4 159.4 %all-reduce.11.cloned.1.call-start = ((), (), s32[]{:S(2)}) async-start(), calls=%async_computation.38 | async-start | bytes 229376 | tf_op jit(solution)/shard_map/psum | solution.py:492
  1373.5 224.6 %reduce-scatter.35.cloned.1.call-start = ((), (), s32[]{:S(2)}) async-start(), calls=%async_computation.37 | async-start | bytes 3538944 | tf_op jit(solution)/shard_map/reduce_scatter | solution.py:442
  1382.9 294.2 %reduce-scatter.33.cloned.1.call-start = ((), (), s32[]{:S(2)}) async-start(), calls=%async_computation.36 | async-start | bytes 3538944 | tf_op jit(solution)/shard_map/reduce_scatter | solution.py:442
  1392.1 865.8 %all-reduce.13.cloned.1.call-start = ((), (), s32[]{:S(2)}) async-start(), calls=%async_computation.43 | async-start | bytes 37748736
  1471.3 1307.5 %reduce-scatter.31.cloned.1.call-start = ((), (), s32[]{:S(2)}) async-start(), calls=%async_computation.35 | async-start | bytes 35979264 | tf_op jit(solution)/shard_map/reduce_scatter | solution.py:461
  2834.8 41.4 %all-to-all-start = ((bf16[8,12,32,256]{3,2,1,0:T(8,128)(2,1)}), bf16[8,12,32,256]{3,2,1,0:T(8,128)(2,1)}, u32[]{:S(2)}, u32[]{:S(2)}) async-start(bf16[8,12,32,256]{3,2,1,0:T(8,128)(2,1)} %bitcast.519), calls=%async_computation.12 | async-start | bytes 3145728 | tf_op jit(solution)/shard_map/all_to_all | solution.py:513
  2885.4 40.7 %all-to-all-start.1 = ((bf16[8,12,32,256]{3,2,1,0:T(8,128)(2,1)}), bf16[8,12,32,256]{3,2,1,0:T(8,128)(2,1)}, u32[]{:S(2)}, u32[]{:S(2)}) async-start(bf16[8,12,32,256]{3,2,1,0:T(8,128)(2,1)} %bitcast.518), calls=%async_computation.13 | async-start | bytes 3145728 | tf_op jit(solution)/shard_map/all_to_all | solution.py:533
  (93 other events, 1011.8 us)
Sparse Core Ops, SparseCore 0:
  11.3 220.6 all-gather.23
  263.3 29.5 reduce-scatter.12
  298.3 22.5 all-gather.25
  323.8 44.1 all-gather.27
  403.3 30.2 reduce-scatter.14
  436.2 49.2 all-gather.47
  488.3 47.7 all-gather.49
  538.2 21.0 all-gather.29
  579.3 31.4 reduce-scatter.16
  613.6 45.6 all-gather.33
  661.5 22.1 all-gather.31
  718.8 31.4 reduce-scatter.18
  752.5 49.2 all-gather.51
  804.4 47.7 all-gather.53
  854.2 21.0 all-gather.35
  895.3 31.4 reduce-scatter.20
  989.9 18.6 all-gather.37
  1022.3 31.4 reduce-scatter.22
  1060.3 22.5 all-gather.39
  1139.0 31.4 reduce-scatter.24
  1177.0 22.5 all-gather.41
  1213.3 31.4 reduce-scatter.26
  1252.1 22.5 all-gather.43
  1330.8 31.4 reduce-scatter.28
  1367.6 22.6 all-gather.45
  1397.1 120.6 all-reduce.10
  1522.3 75.7 reduce-scatter.34
  1602.7 74.3 reduce-scatter.32
  1684.4 573.3 all-reduce.12
  2262.1 516.6 reduce-scatter.30
where the time goes:
time: 2950 us; the launch traced here: 2940 us
  waiting for transfers between devices  2130 us (72%)
  local copies, waits for them, and re-layouts  265 us (9%)
  matrix products  192 us (7%)
  other arithmetic  168 us (6%)
  blocking collectives  149 us (5%)
    unnamed x31, waiting for transfers between devices  581 us
    reduce_scatter x1, waiting for transfers between devices, shards(): lax.psum_scatter(table_grad, 'dp', scatter_dimension=0, tiled=True)  509 us
    all_gather x1, waiting for transfers between devices, shards(): lax.all_gather(embed_table.astype(jnp.bfloat16), 'dp', axis=0, tiled=True)  219 us
    all_gather x6, waiting for transfers between devices, fetch_weights(): lax.all_gather(for_sending(pieces), 'dp', axis=2, tiled=True)  218 us
    reduce_scatter x2, waiting for transfers between devices, shards(): lax.psum_scatter(grad_in_local.reshape((-1,) + grad_in_local.shape[2:]),...  149 us
    reduce_scatter x5, waiting for transfers between devices, spread(): lax.psum_scatter(values.astype(jnp.bfloat16), 'tensor', scatter_dimension...  143 us
    reduce_scatter x4, waiting for transfers between devices, spread_grad(): lax.psum_scatter(values.astype(jnp.bfloat16), 'tensor', scatter_dimension...  126 us
    all_gather x5, waiting for transfers between devices, collect_grad(): return lax.all_gather(values, 'tensor', axis=0, tiled=True)  71.9 us
  transfers between devices with their start and end apart: 32, of which 29 were waited for; matrix products, arithmetic and copies ran while one was open for 9% of the time, Pallas kernels for 0%

commit v1 on v0

v1 whole, which is shorter than its diff:
```python
import math

import jax
import jax.numpy as jnp
from jax import lax
from jax.experimental import pallas as pl
from jax.experimental.pallas import tpu as pltpu
from jax.sharding import Mesh
from jax.sharding import PartitionSpec as P

D = 1024
HD = 64
FF = 4096
VOCAB = 30720
STEP = 10


PRECISE = lax.Precision.HIGHEST
EPS_NORM = 1e-05
EPS_UNIT = 1e-06
CLIP_NORM = 1.0
BETA_ONE = 0.9
BETA_TWO = 0.999
ADAM_EPS = 1e-08
STAT_DECAY = 0.95
RATE_TABLE = 0.06
RATE_VECTOR = 0.5
RATE_MATRIX = 0.5
RATE_OUT = 4.0
DECAY_TABLE = 0.01
DECAY_MATRIX = 0.01
CON_WEIGHT = 16.0
MASK_FILL = -1000000000.0

BF = jnp.bfloat16
F32 = jnp.float32
GROUP = ("dp", "x")
EVERY = ("dp", "x", "core")
ROW_SLOTS = 24


def layer_norm(values, gain, shift):
    centre = values - jnp.mean(values, axis=-1, keepdims=True)
    spread_sq = jnp.mean(centre * centre, axis=-1, keepdims=True)
    return centre * lax.rsqrt(spread_sq + EPS_NORM) * gain + shift


def norm_back(values, gain, shift, upstream):
    ignored, pull = jax.vjp(layer_norm, values, gain, shift)
    return pull(upstream)


def contrast(pooled, log_scale, pair_index):
    unit_rows = pooled * lax.rsqrt(jnp.sum(pooled * pooled, axis=-1, keepdims=True) + EPS_UNIT)
    partner = jnp.take(unit_rows, pair_index, axis=0)
    logits = jnp.exp(log_scale) * jnp.dot(unit_rows, partner.T, precision=PRECISE)
    matched = jnp.diagonal(logits)
    by_rows = jax.nn.logsumexp(logits, axis=1) - matched
    by_cols = jax.nn.logsumexp(logits, axis=0) - matched
    return 0.5 * (jnp.mean(by_rows) + jnp.mean(by_cols))


def adamw(weight, first, second, grad, rate, decay):
    first = BETA_ONE * first + (1 - BETA_ONE) * grad
    second = BETA_TWO * second + (1 - BETA_TWO) * grad * grad
    fixed_first = first / (1 - BETA_ONE**STEP)
    fixed_second = second / (1 - BETA_TWO**STEP)
    return (
        weight - rate * (fixed_first / (jnp.sqrt(fixed_second) + ADAM_EPS) + decay * weight),
        first,
        second,
    )


def from_peer(values, axis, mask=1):
    size = lax.axis_size(axis)
    return lax.ppermute(values, axis, [(at, at ^ mask) for at in range(size)])


def peers():
    found = []
    for axis in ("core", "x", "dp"):
        mask = 1
        while mask < lax.axis_size(axis):
            found.append((axis, mask))
            mask = mask * 2
    return found


def routes():
    masks = [1]
    while masks[-1] * 2 < lax.axis_size("dp"):
        masks.append(masks[-1] * 2)
    across = [("x", 1)]
    near = [("dp", masks[0])]
    far = [("dp", mask) for mask in masks[1:]]
    return (
        across + near + far,
        near + across + far,
        across + far + near,
        near + far + across,
    )


def scatter_sum(parts, route):
    masks = sorted((mask for axis, mask in route if axis == "dp"), reverse=True)
    left = [("dp", mask) for mask in masks] + [("x", 1)]
    parts = parts.reshape((2,) * len(left) + parts.shape[-2:])
    for axis, mask in route:
        dim = left.index((axis, mask))
        left.pop(dim)
        bit = lax.axis_index(axis) // mask % 2
        keep = lax.dynamic_index_in_dim(parts, bit, dim, keepdims=False)
        away = lax.dynamic_index_in_dim(parts, 1 - bit, dim, keepdims=False)
        parts = keep + from_peer(away, axis, mask)
    return parts


def sum_over_all(values):
    for axis, mask in peers():
        values = values + from_peer(values, axis, mask)
    return values


def gather_small(values, steps=()):
    mask = 1
    while mask < lax.axis_size("dp"):
        steps = steps + (("dp", mask),)
        mask = mask * 2
    for axis, mask in steps:
        other = from_peer(values, axis, mask)
        first = lax.axis_index(axis) // mask % 2 == 0
        values = jnp.where(
            first,
            jnp.concatenate([values, other], axis=0),
            jnp.concatenate([other, values], axis=0),
        )
    return values


def tree():
    count = lax.axis_size("dp") * lax.axis_size("x")
    holders = [count - 1]
    steps = []
    mask = 1
    while mask < count:
        steps.append([(at, at ^ mask) for at in holders])
        holders = holders + [at ^ mask for at in holders]
        mask = mask * 2
    return steps


def from_last(parts):
    at = lax.axis_index("dp") * lax.axis_size("x") + lax.axis_index("x")
    last = lax.axis_size("core") - 1
    value = jnp.where(lax.axis_index("core") == last, parts[last], from_peer(parts[0], "core"))
    for step in tree():
        found = lax.ppermute(value, GROUP, step)
        reached = jnp.any(at == jnp.array([there for here, there in step]))
        value = jnp.where(reached, found, value)
    return value


def to_last(value):
    total = value.astype(F32)
    for step in reversed(tree()):
        back = [(there, here) for here, there in step]
        total = total + lax.ppermute(total.astype(BF), GROUP, back).astype(F32)
    return jnp.concatenate([from_peer(total.astype(BF), "core").astype(F32), total], axis=0)


def collect(values):
    return jnp.concatenate([values, from_peer(values, "core")], axis=0)


def spread(values):
    half = values.shape[0] // 2
    return values[:half] + from_peer(values[half:].astype(BF), "core").astype(F32)


def column_sum(values):
    return jnp.sum(values.astype(F32), axis=0)


def fetch(pieces):
    low = pieces.astype(BF)
    whole = lax.all_gather(low, GROUP, axis=0, tiled=False)
    return whole.reshape((lax.axis_size("dp"), lax.axis_size("x")) + low.shape)


def fetch_layer(in_proj, out_proj, up_proj, down_proj, layer_no):
    rows, width = in_proj.shape[-2:]
    row_blocks = in_proj.shape[1]
    feed = up_proj.shape[2]
    pieces = [
        in_proj[layer_no].reshape(row_blocks, 3, rows, width).transpose(1, 0, 2, 3),
        out_proj[layer_no].reshape(1, row_blocks, rows, width),
        up_proj[layer_no].reshape(row_blocks, feed, rows, width),
        down_proj[layer_no].reshape(feed, row_blocks, rows, width),
    ]
    all_of = fetch(jnp.concatenate(pieces, axis=0))
    of_x = (1, all_of.shape[1], 0)
    second = (3, row_blocks, 0)
    return (
        (all_of, {"x": of_x, "low": (2, 3, 0), "high": second}),
        (all_of, {"x": of_x, "low": second, "high": (2, 1, 3)}),
        (all_of, {"x": of_x, "low": second, "high": (2, row_blocks, 4)}),
        (all_of, {"x": of_x, "low": second, "high": (2, feed, 4 + row_blocks)}),
    )


def wide():
    return pltpu.CompilerParams(vmem_limit_bytes=48 * 1024 * 1024)


def whole(shape):
    return pl.BlockSpec(shape, lambda step: (0,) * len(shape))


def columns_of(ref, at, width):
    if len(ref.shape) == 2:
        return ref[:, at * width : (at + 1) * width]
    per = ref.shape[2] // width
    return ref[at // per, :, at % per * width : (at % per + 1) * width]


def joined_rows(weights):
    if weights.shape[-2] % 16 == 0:
        return weights
    owners, ranks, first, second, rows, width = weights.shape
    moved = weights.transpose(1, 2, 3, 0, 4, 5)
    return moved.reshape(1, ranks, first, second, owners * rows, width)


def rows_product(left, weights, dims, over, across, outs, finish, by_column=()):
    weights = joined_rows(weights)
    owners, rows, width = weights.shape[0], weights.shape[4], weights.shape[5]
    side = owners * rows
    turned = "low" in over
    steps = 1
    for name in across:
        steps = steps * dims[name][1]
    tokens = left.shape[-2]
    block_sizes = [1] * 6
    block_sizes[0], block_sizes[4], block_sizes[5] = owners, rows, width
    for name in over:
        block_sizes[dims[name][0]] = dims[name][1]
    terms = [()]
    for name in over:
        terms = [term + (at,) for term in terms for at in range(dims[name][1])]

    def kernel(*refs):
        left_ref, weights_ref = refs[:2]
        total = None
        for number, term in enumerate(terms):
            at = [0] * 3
            for name, place in zip(over, term):
                at[dims[name][0] - 1] = place
            block = weights_ref[(slice(None),) + tuple(at)].reshape(side, width)
            part = columns_of(left_ref, number, side)
            contract = (((1,), (1 if turned else 0,)), ((), ()))
            term_out = lax.dot_general(part, block, contract, preferred_element_type=F32)
            total = term_out if total is None else total + term_out
        last_in = 2 + len(by_column)
        results = finish(total, *[ref[...] for ref in refs[2:last_in]])
        for ref, result in zip(refs[last_in:], results):
            ref[...] = result.astype(ref.dtype).reshape(ref.shape)

    def weights_at(step):
        place = [0] * 6
        for name in reversed(across):
            place[dims[name][0]] = dims[name][2] + lax.rem(step, dims[name][1])
            step = lax.div(step, dims[name][1])
        for name in over:
            place[dims[name][0]] = dims[name][2] // dims[name][1]
        return tuple(place)

    out_shapes = []
    out_specs = []
    for apart, dtype in outs:
        if apart == 1:
            out_shapes.append(jax.ShapeDtypeStruct((tokens, steps * side), dtype))
            out_specs.append(pl.BlockSpec((tokens, side), lambda step: (0, step)))
        else:
            per = steps // apart
            out_shapes.append(jax.ShapeDtypeStruct((apart, tokens, per * side), dtype))
            out_specs.append(
                pl.BlockSpec(
                    (1, tokens, side),
                    lambda step, per=per: (lax.div(step, per), 0, lax.rem(step, per)),
                )
            )
    work = steps * len(terms) * side * width
    return pl.pallas_call(
        kernel,
        grid=(steps,),
        in_specs=[whole(left.shape), pl.BlockSpec(tuple(block_sizes), weights_at)]
        + [
            pl.BlockSpec((member.shape[0], side), lambda step: (0, step)) for member in by_column
        ],
        out_specs=out_specs,
        out_shape=out_shapes,
        compiler_params=wide(),
        cost_estimate=pl.CostEstimate(
            flops=2 * tokens * work, bytes_accessed=2 * work + 2 * left.size, transcendentals=0
        ),
    )(left, weights, *by_column)


def block_grads(left, right, ranks, high, low, side, x_on_left):
    def kernel(left_ref, right_ref, out_ref):
        step = pl.program_id(0)
        for at in range(ranks if x_on_left else 1):
            begin = pl.multiple_of((at * high + step) * side, side)
            part = left_ref[:, pl.ds(begin, side)]
            for low_at in range(low):
                for rank in range(1 if x_on_left else ranks):
                    if x_on_left:
                        number, target = low_at, at
                    elif len(right_ref.shape) == 3:
                        number, target = low_at * ranks + rank, rank
                    else:
                        number, target = rank * low + low_at, rank
                    block = columns_of(right_ref, number, side)
                    out_ref[low_at, target] = lax.dot_general(
                        part, block, (((0,), (0,)), ((), ())), preferred_element_type=F32
                    ).astype(BF)

    return pl.pallas_call(
        kernel,
        grid=(high,),
        in_specs=[whole(left.shape), whole(right.shape)],
        out_specs=pl.BlockSpec((low, ranks, side, side), lambda step: (step, 0, 0, 0)),
        out_shape=jax.ShapeDtypeStruct((high * low, ranks, side, side), BF),
        compiler_params=wide(),
        cost_estimate=pl.CostEstimate(
            flops=2 * left.shape[-2] * high * low * ranks * side * side,
            bytes_accessed=2 * high * low * ranks * side * side,
            transcendentals=0,
        ),
    )(left, right)


PAIR = 2 * HD


def halves(values):
    lane = lax.broadcasted_iota(jnp.int32, values.shape, 1)
    nothing = jnp.zeros_like(values)
    return jnp.where(lane < HD, values, nothing), jnp.where(lane < HD, nothing, values)


def dot_nt(left, right):
    return lax.dot_general(left, right, (((1,), (1,)), ((), ())), preferred_element_type=F32)


def dot_nn(left, right):
    return lax.dot_general(left, right, (((1,), (0,)), ((), ())), preferred_element_type=F32)


def dot_tn(left, right):
    return lax.dot_general(left, right, (((0,), (0,)), ((), ())), preferred_element_type=F32)


def softmax_of(queries, keys_in, live):
    scores = dot_nt(queries, keys_in) * HD ** (-0.5)
    scores = jnp.where(live > 0, scores, MASK_FILL)
    grown = jnp.exp(scores - jnp.max(scores, axis=-1, keepdims=True))
    return grown / jnp.sum(grown, axis=-1, keepdims=True)


def attend_kernel(live_ref, qkv_ref, mixed_ref):
    live = live_ref[0]
    query_heads = halves(qkv_ref[0])
    value_heads = halves(qkv_ref[2])
    total = None
    for query, value in zip(query_heads, value_heads):
        weights = softmax_of(query, qkv_ref[1], live).astype(BF)
        part = dot_nn(weights, value)
        total = part if total is None else total + part
    mixed_ref[...] = total.astype(BF)


def attend_back_kernel(live_ref, qkv_ref, d_mixed_ref, d_qkv_ref):
    live = live_ref[0]
    query_heads = halves(qkv_ref[0])
    key_heads = halves(qkv_ref[1])
    d_heads = halves(d_mixed_ref[...])
    d_query = d_key = d_value = 0.0
    for query, key, d_out in zip(query_heads, key_heads, d_heads):
        weights = softmax_of(query, qkv_ref[1], live)
        d_value = d_value + dot_tn(weights.astype(BF), d_out)
        d_weights = dot_nt(d_out, qkv_ref[2])
        d_scores = weights * (
            d_weights - jnp.sum(weights * d_weights, axis=-1, keepdims=True)
        )
        d_scores = d_scores.astype(BF)
        d_query = d_query + dot_nn(d_scores, key)
        d_key = d_key + dot_tn(d_scores, query)
    scale_by = HD ** (-0.5)
    d_qkv_ref[0] = (d_query * scale_by).astype(BF)
    d_qkv_ref[1] = (d_key * scale_by).astype(BF)
    d_qkv_ref[2] = d_value.astype(BF)


def attend(qkv, live, d_mixed=None):
    seqs, slots = live.shape
    width = qkv.shape[2]
    pairs = width // PAIR
    mixed_spec = pl.BlockSpec((slots, PAIR), lambda seq, pair: (seq, pair))
    qkv_spec = pl.BlockSpec((3, slots, PAIR), lambda seq, pair: (0, seq, pair))
    specs = [pl.BlockSpec((1, 1, slots), lambda seq, pair: (seq, 0, 0)), qkv_spec]
    operands = [live.astype(F32).reshape(seqs, 1, slots), qkv]
    if d_mixed is None:
        out_spec, out_shape = mixed_spec, jax.ShapeDtypeStruct(qkv.shape[1:], BF)
        body, products = attend_kernel, 2
    else:
        specs.append(mixed_spec)
        operands.append(d_mixed)
        out_spec, out_shape = qkv_spec, jax.ShapeDtypeStruct(qkv.shape, BF)
        body, products = attend_back_kernel, 5
    return pl.pallas_call(
        body,
        grid=(seqs, pairs),
        in_specs=specs,
        out_specs=out_spec,
        out_shape=out_shape,
        compiler_params=wide(),
        cost_estimate=pl.CostEstimate(
            flops=2 * products * seqs * slots * slots * width * 2,
            bytes_accessed=2 * qkv.size * 2,
            transcendentals=seqs * slots * slots * width // HD,
        ),
    )(*operands)


def product(left, right):
    return jnp.dot(left, right, preferred_element_type=F32)


def product_tn(left, right):
    return lax.dot_general(left, right, (((0,), (0,)), ((), ())), preferred_element_type=F32)


def same(total):
    return (total,)


def plus(total, bias):
    return (total + bias,)


ROOT_HALF = 0.5**0.5
DENSITY = (2 * math.pi) ** (-0.5)


def plus_gelu(total, bias):
    total = total + bias
    return (total, total * (1.0 + lax.erf(total * ROOT_HALF)) * 0.5)


def times_gelu_slope(total, before):
    slope = 0.5 * (1.0 + lax.erf(before * ROOT_HALF)) + before * (
        DENSITY * jnp.exp(-0.5 * before * before)
    )
    return (total * slope,)


def layer_forward(residual, weights, pieces, keys_live):
    w_in, w_out, w_up, w_down = weights
    bias_q, bias_v, bias_up, bias_out, bias_down, gain_one, shift_one, gain_two, shift_two = pieces
    gathered = collect(residual.astype(BF))
    bias_in = jnp.concatenate([bias_q, jnp.zeros_like(bias_q), bias_v]).reshape(1, -1)
    (qkv,) = rows_product(
        gathered, *w_in, ("high",), ("low", "x"), [(3, BF)], plus, [bias_in]
    )
    mixed = attend(qkv, keys_live)
    (mixed_out,) = rows_product(mixed, *w_out, ("x", "high"), ("low",), [(1, F32)], same)
    first_in = residual + (spread(mixed_out) + bias_out)
    middle = layer_norm(first_in, gain_one, shift_one)
    spread_mid = collect(middle.astype(BF))
    hidden_pre, hidden_act = rows_product(
        spread_mid,
        *w_up,
        ("high",),
        ("x", "low"),
        [(1, F32), (1, BF)],
        plus_gelu,
        [bias_up.reshape(1, -1)],
    )
    (fed_out,) = rows_product(hidden_act, *w_down, ("x", "high"), ("low",), [(1, F32)], same)
    second_in = middle + (spread(fed_out) + bias_down)
    kept_values = (
        first_in,
        second_in,
        gathered,
        qkv,
        mixed,
        spread_mid,
        hidden_pre,
        hidden_act,
    )
    return (layer_norm(second_in, gain_two, shift_two), kept_values)


def layer_backward(upstream, kept_values, weights, pieces, keys_live):
    (
        first_in,
        second_in,
        gathered,
        qkv,
        mixed,
        spread_mid,
        hidden_pre,
        hidden_act,
    ) = kept_values
    w_in, w_out, w_up, w_down = weights
    gain_one, shift_one, gain_two, shift_two = pieces[5:]
    ranks, side = w_in[1]["x"][1], w_in[0].shape[-1]
    row_blocks, feed = w_in[1]["high"][1], w_up[1]["low"][1]
    d_second, d_gain_two, d_shift_two = norm_back(second_in, gain_two, shift_two, upstream)
    d_fed = d_second.astype(BF)
    d_fed_all = collect(d_fed)
    parts = block_grads(hidden_act, d_fed_all, ranks, feed, row_blocks, side, True)
    d_fed_all, parts = lax.optimization_barrier((d_fed_all, parts))
    yield "down", parts
    (d_pre,) = rows_product(
        d_fed_all, *w_down, ("low",), ("x", "high"), [(1, BF)], times_gelu_slope, [hidden_pre]
    )
    parts = block_grads(spread_mid, d_pre, ranks, row_blocks, feed, side, False)
    d_pre, parts = lax.optimization_barrier((d_pre, parts))
    yield "up", parts
    (d_up_in,) = rows_product(d_pre, *w_up, ("x", "low"), ("high",), [(1, F32)], same)
    d_middle = d_second + spread(d_up_in)
    d_first, d_gain_one, d_shift_one = norm_back(first_in, gain_one, shift_one, d_middle)
    d_branch = d_first.astype(BF)
    d_branch_all = collect(d_branch)
    parts = block_grads(mixed, d_branch_all, ranks, 1, row_blocks, side, True)
    d_branch_all, parts = lax.optimization_barrier((d_branch_all, parts))
    yield "out", parts
    (d_mixed,) = rows_product(d_branch_all, *w_out, ("low",), ("x", "high"), [(1, BF)], same)
    d_qkv = attend(qkv, keys_live, d_mixed)
    parts = block_grads(gathered, d_qkv, ranks, row_blocks, 3, side, False)
    d_qkv, parts = lax.optimization_barrier((d_qkv, parts))
    yield "in", parts
    (d_in,) = rows_product(d_qkv, *w_in, ("low", "x"), ("high",), [(1, F32)], same)
    d_residual = d_first + spread(d_in)
    bias_grads = (
        column_sum(d_qkv[0]),
        column_sum(d_qkv[2]),
        column_sum(d_pre),
        column_sum(d_branch),
        column_sum(d_fed),
        d_gain_one,
        d_shift_one,
        d_gain_two,
        d_shift_two,
    )
    yield "rest", (d_residual, bias_grads)


def shards(
    token_ids,
    labels,
    lengths,
    pair_index,
    embed_table,
    table_first,
    table_second,
    vectors,
    vector_first,
    vector_second,
    in_proj,
    out_proj,
    up_proj,
    down_proj,
    stats_left,
    stats_right,
    root_left,
    root_right,
):
    seq_dev, seq_slots = token_ids.shape
    layers = in_proj.shape[0]
    owners = lax.axis_size("dp")
    ranks = lax.axis_size("x")
    cores = lax.axis_size("core")
    devices = owners * ranks * cores
    owner_rank = lax.axis_index("dp")
    rank = lax.axis_index("x")
    core = lax.axis_index("core")
    device = (owner_rank * ranks + rank) * cores + core
    per_layer = 8 * D + FF
    tail_at = layers * per_layer
    block_size = in_proj.shape[-1]
    rows_per = in_proj.shape[-2]
    row_blocks = in_proj.shape[1]
    feed_blocks = up_proj.shape[2]
    slot_count = stats_left.shape[2]
    seqs = seq_dev // ranks
    group_rows = seqs * seq_slots
    local_rows = group_rows // cores

    def mine(values):
        return lax.dynamic_slice_in_dim(
            values.reshape(-1), rank * group_rows + core * local_rows, local_rows
        )

    my_rows = core * local_rows + jnp.arange(local_rows)
    my_sequence = rank * seqs + my_rows // seq_slots
    my_length = jnp.take(lengths, my_sequence)
    counted = (my_rows % seq_slots < my_length).astype(F32)
    my_labels = mine(labels).astype(F32)
    turned = (jnp.arange(group_rows) + core * local_rows) % group_rows
    keys_live = (turned % seq_slots < jnp.take(lengths, rank * seqs + turned // seq_slots)).reshape(
        seqs, seq_slots
    )

    shard_rows = embed_table.shape[0]
    all_ids = gather_small(token_ids).reshape(-1)
    last_base = VOCAB - (devices - 1) * shard_rows
    by_device = all_ids.reshape(devices, local_rows)
    holder = by_device // shard_rows
    earlier = jnp.arange(local_rows)[None, :] < jnp.arange(local_rows)[:, None]
    turn = jnp.sum(
        ((holder[:, :, None] == holder[:, None, :]) & earlier[None]).astype(jnp.int32), axis=2
    )
    rounds = jnp.max(turn) // ROW_SLOTS + 1
    own_index = by_device - device * shard_rows
    my_holder = lax.dynamic_index_in_dim(holder, device, 0, keepdims=False)
    my_turn = lax.dynamic_index_in_dim(turn, device, 0, keepdims=False)

    def plan(round_no):
        first = round_no * ROW_SLOTS
        here = (holder == device)[:, None, :] & (
            turn[:, None, :] - first == jnp.arange(ROW_SLOTS)[None, :, None]
        )
        row_of_slot = jnp.sum(jnp.where(here, own_index[:, None, :] + 1, 0), axis=2).reshape(-1)
        inside = (my_turn >= first) & (my_turn < first + ROW_SLOTS)
        my_slot = jnp.where(inside, my_holder * ROW_SLOTS + my_turn - first, -1)
        slot_of_token = (jnp.arange(devices * ROW_SLOTS)[:, None] == my_slot[None, :]).astype(BF)
        return row_of_slot, slot_of_token

    def exchange(filled):
        return lax.all_to_all(filled, EVERY, split_axis=0, concat_axis=0, tiled=True)

    def fetch_rows(round_no):
        row_of_slot, slot_of_token = plan(round_no)
        filled = jnp.take(embed_table, jnp.maximum(row_of_slot - 1, 0), axis=0).astype(BF)
        return product_tn(slot_of_token, exchange(filled))

    def return_rows(round_no, grads):
        row_of_slot, slot_of_token = plan(round_no)
        reached = exchange(product(slot_of_token, grads).astype(BF))
        picker = (row_of_slot[None, :] == 1 + jnp.arange(shard_rows)[:, None]).astype(BF)
        return product(picker, reached)

    def full_rows():
        table = lax.all_gather(embed_table.astype(BF), "dp", axis=0, tiled=True)
        tensor_ranks = ranks * cores

        def lookup(row_index):
            block_at = row_index // shard_rows
            inside = block_at % tensor_ranks == rank * cores + core
            at_row = block_at // tensor_ranks * shard_rows + row_index % shard_rows
            picked = jnp.take(table, jnp.where(inside, at_row, 0), axis=0)
            return jnp.where(inside[:, None], picked, jnp.zeros((), BF))

        rows = lookup(token_ids.reshape(-1))
        rows = rows + lookup(VOCAB + jnp.arange(rows.shape[0]) % seq_slots)
        return lax.psum_scatter(rows, ("x", "core"), scatter_dimension=0, tiled=True).astype(F32)

    places_last = last_base >= 0 and local_rows * cores == seq_slots
    if places_last:
        token_rows = lax.fori_loop(
            1, rounds, lambda at, rows: rows + fetch_rows(at), fetch_rows(0)
        )
        place_rows = from_last(
            [
                embed_table[last_base + at * local_rows : last_base + (at + 1) * local_rows].astype(BF)
                for at in range(cores)
            ]
        )
        embedded = token_rows + place_rows.astype(F32)
    else:
        embedded = full_rows()

    def by_rank(base_at, width):
        return jnp.concatenate(
            [
                lax.dynamic_slice_in_dim(vectors, base_at + (at * cores + core) * width, width)
                for at in range(ranks)
            ]
        )

    head_width = D // (ranks * cores)
    feed_width = FF // (ranks * cores)

    def pieces_of(layer_no):
        base_at = layer_no * per_layer
        others = vectors[base_at + 2 * D + FF : base_at + per_layer].reshape(6, D)
        return (
            by_rank(base_at, head_width),
            by_rank(base_at + D, head_width),
            by_rank(base_at + 2 * D, feed_width),
        ) + tuple(others)

    gain_embed = vectors[tail_at : tail_at + D]
    shift_embed = vectors[tail_at + D : tail_at + 2 * D]
    head_weight = vectors[tail_at + 2 * D : tail_at + 3 * D]
    residual = layer_norm(embedded, gain_embed, shift_embed)
    kept_all = []
    weights_all = []
    for layer_no in range(layers):
        weights = fetch_layer(in_proj, out_proj, up_proj, down_proj, layer_no)
        residual, kept_values = layer_forward(
            residual, weights, pieces_of(layer_no), keys_live
        )
        kept_all.append(kept_values)
        weights_all.append(weights)

    logits_tok = jnp.dot(residual, head_weight, precision=PRECISE) + vectors[tail_at + 3 * D]
    bce_part = jnp.sum(counted * (jax.nn.softplus(logits_tok) - my_labels * logits_tok))
    count_part = jnp.sum(counted)
    token_weight = counted / my_length.astype(F32)
    here_sequence = my_rows // seq_slots
    chooser = (here_sequence[None, :] == jnp.arange(seqs)[:, None]).astype(F32) * token_weight[None, :]
    pooled_here = jnp.dot(chooser, residual, precision=PRECISE)
    pooled = gather_small(pooled_here + from_peer(pooled_here, "core"), (("x", 1),))
    global_sequence = owner_rank * seq_dev + my_sequence

    def contrast_loss(pooled_in, log_scale):
        return CON_WEIGHT * pooled_in.shape[0] * contrast(pooled_in, log_scale, pair_index)

    scaled_con, con_pull = jax.vjp(contrast_loss, pooled, vectors[tail_at + 3 * D + 1])
    d_pooled, d_scale = con_pull(jnp.ones_like(scaled_con))
    d_logit = counted * (jax.nn.sigmoid(logits_tok) - my_labels)
    upstream = d_logit[:, None] * head_weight[None, :] + token_weight[:, None] * jnp.take(
        d_pooled, global_sequence, axis=0
    )
    d_head_weight = jnp.dot(d_logit, residual, precision=PRECISE)
    d_head_bias = jnp.sum(d_logit)
    leader = (device == 0).astype(F32)

    counts = {
        "in": row_blocks * 3,
        "out": row_blocks,
        "up": row_blocks * feed_blocks,
        "down": feed_blocks * row_blocks,
    }
    starts = {}
    begin_at = 0
    for name in ("in", "out", "up", "down"):
        starts[name] = begin_at
        begin_at = begin_at + layers * counts[name]
    block_count = begin_at
    ready = {}
    summed = {}

    def send_ready(offload):
        taken = []
        for slot in range(slot_count):
            numbers = range(slot * owners, min((slot + 1) * owners, block_count))
            if slot not in summed and all(number in ready for number in numbers):
                taken.append(slot)
        if offload and len(taken) > 0:
            array = ready[taken[0] * owners][0]
            array = array.reshape((len(taken), owners * ranks) + array.shape[2:])
            array = array.transpose(1, 0, 2, 3).reshape((-1,) + array.shape[2:])
            arrived = lax.psum_scatter(array, GROUP, scatter_dimension=0, tiled=True)
            for at, slot in enumerate(taken):
                summed[slot] = arrived[at]
            return
        for slot in taken:
            numbers = range(slot * owners, (slot + 1) * owners)
            members = []
            at = 0
            while at < owners:
                number = numbers[at]
                if number >= block_count:
                    members.append(jnp.zeros((owners - at, ranks, block_size, block_size), BF))
                    break
                array, offset = ready[number]
                span = 1
                while at + span < owners and ready.get(number + span, (None, 0))[0] is array:
                    span = span + 1
                members.append(array[offset : offset + span])
                at = at + span
            joined = jnp.concatenate(members, axis=0) if len(members) > 1 else members[0]
            summed[slot] = scatter_sum(joined, routes()[slot % 4])

    early = {("down", layers - 1), ("up", layers - 1), ("down", layers - 2)}
    bias_parts = [None] * layers
    for layer_no in reversed(range(layers)):
        for name, value in layer_backward(
            upstream,
            kept_all[layer_no],
            weights_all[layer_no],
            pieces_of(layer_no),
            keys_live,
        ):
            if name == "rest":
                upstream, bias_parts[layer_no] = value
                continue
            first = starts[name] + layer_no * counts[name]
            for at in range(counts[name]):
                ready[first + at] = (value, at)
            whole_slots = first % owners == 0 and counts[name] % owners == 0
            send_ready(whole_slots and (name, layer_no) in early)

    d_embed, d_gain_embed, d_shift_embed = norm_back(embedded, gain_embed, shift_embed, upstream)
    d_embed = d_embed.astype(BF)

    if places_last:
        table_shard = lax.fori_loop(
            1, rounds, lambda at, total: total + return_rows(at, d_embed), return_rows(0, d_embed)
        )
        place_grads = to_last(d_embed)
        table_shard = table_shard.at[last_base : last_base + seq_slots].add(
            jnp.where(device == devices - 1, place_grads, 0.0)
        )
    else:
        d_rows = lax.all_gather(d_embed, EVERY, axis=0, tiled=True)
        held = device * shard_rows + jnp.arange(shard_rows)
        all_places = VOCAB + jnp.arange(all_ids.shape[0]) % seq_slots
        picker = (all_ids[None, :] == held[:, None]).astype(BF) + (
            all_places[None, :] == held[:, None]
        ).astype(BF)
        table_shard = product(picker, d_rows)

    def placed(piece, base_at, width):
        row = jnp.zeros((ranks * cores * width,), F32)
        for at in range(ranks):
            row = lax.dynamic_update_slice(
                row, piece[at * width : (at + 1) * width], ((at * cores + core) * width,)
            )
        return row

    vector_rows = []
    for layer_no in range(layers):
        grad_items = bias_parts[layer_no]
        vector_rows.append(placed(grad_items[0], 0, head_width))
        vector_rows.append(placed(grad_items[1], 0, head_width))
        vector_rows.append(placed(grad_items[2], 0, feed_width))
        vector_rows.extend(grad_items[3:])
    vector_grad = jnp.concatenate(
        vector_rows
        + [d_gain_embed, d_shift_embed, d_head_weight, jnp.stack([d_head_bias, leader * d_scale])]
    )
    vector_total = sum_over_all(jnp.concatenate([vector_grad, jnp.stack([bce_part, count_part])]))
    offloaded = {
        starts[name] // owners + (layer_no * counts[name]) // owners + at
        for name, layer_no in early
        for at in range(counts[name] // owners)
    }
    order = [slot for slot in summed if slot not in offloaded] + [
        slot for slot in summed if slot in offloaded
    ]
    summed[order[0]], vector_total = lax.optimization_barrier((summed[order[0]], vector_total))
    bce_total, count_total = vector_total[-2], vector_total[-1]
    vector_total = vector_total[:-2]

    blocks_low = jnp.stack([summed[slot] for slot in range(slot_count)])
    blocks = blocks_low.astype(F32)
    squares = jnp.sum(table_shard * table_shard) + jnp.sum(blocks * blocks)
    square_total = sum_over_all(squares.reshape(1, 1))[0, 0]
    grad_norm = jnp.sqrt(square_total + jnp.sum(vector_total * vector_total))
    factor = CLIP_NORM / jnp.maximum(grad_norm, CLIP_NORM)

    left_root = root_left.reshape(blocks.shape)
    right_root = root_right.reshape(blocks.shape)
    returned = [None] * slot_count
    per_send = max(1, slot_count // 3)
    for begin_at in range(0, slot_count, per_send):
        taken = sorted(order[begin_at : begin_at + per_send])
        some = jnp.stack([summed[slot] for slot in taken])

        def roots(array):
            return jnp.stack([array[slot] for slot in taken])

        direction = jnp.einsum(
            "sij,sjk->sik",
            jnp.einsum(
                "sij,sjk->sik", roots(left_root), some.astype(F32), precision=lax.Precision.HIGH
            ),
            roots(right_root),
            precision=lax.Precision.HIGH,
        )
        both = jnp.stack([some, direction.astype(BF)])
        outgoing = both.reshape(2, len(taken), owners, rows_per, block_size).transpose(2, 0, 1, 3, 4)
        back = lax.all_to_all(outgoing, "dp", split_axis=0, concat_axis=0, tiled=True)
        for at, slot in enumerate(taken):
            returned[slot] = back[:, :, at]
    mine_back = (
        jnp.stack(returned)
        .transpose(2, 0, 1, 3, 4)
        .reshape(2, slot_count * owners, rows_per, block_size)[:, :block_count]
        .astype(F32)
        * factor
    )
    square_of = factor * factor * (1 - STAT_DECAY)
    new_left = STAT_DECAY * stats_left.reshape(blocks.shape) + square_of * jnp.einsum(
        "sij,skj->sik", blocks_low, blocks_low, preferred_element_type=F32
    )
    new_right = STAT_DECAY * stats_right.reshape(blocks.shape) + square_of * jnp.einsum(
        "sji,sjk->sik", blocks_low, blocks_low, preferred_element_type=F32
    )
    matrices = (in_proj, out_proj, up_proj, down_proj)
    new_weights = []
    clipped = []
    begin_at = 0
    rates = (RATE_MATRIX, RATE_OUT, RATE_MATRIX, RATE_MATRIX)
    for weight, rate in zip(matrices, rates):
        span_of = weight.size // (rows_per * block_size)
        part = mine_back[:, begin_at : begin_at + span_of].reshape((2,) + weight.shape)
        clipped.append(part[0])
        new_weights.append(weight - rate * (part[1] + DECAY_MATRIX * weight))
        begin_at = begin_at + span_of
    clipped_vectors = vector_total * factor
    new_table, table_one, table_two = adamw(
        embed_table, table_first, table_second, table_shard * factor, RATE_TABLE, DECAY_TABLE
    )
    new_vectors, vector_one, vector_two = adamw(
        vectors, vector_first, vector_second, clipped_vectors, RATE_VECTOR, 0.0
    )
    loss = jnp.stack([bce_total, count_total, scaled_con])
    return (
        loss,
        grad_norm,
        new_weights[0],
        new_weights[1],
        new_weights[2],
        new_weights[3],
        clipped[0],
        clipped[1],
        clipped[2],
        clipped[3],
        new_left.reshape(stats_left.shape),
        new_right.reshape(stats_right.shape),
        new_table,
        table_one,
        table_two,
        new_vectors,
        vector_one,
        vector_two,
        clipped_vectors[:tail_at],
    )


def solution(mesh):
    owners, tensor_ranks = mesh.shape["dp"], mesh.shape["tensor"]
    split = Mesh(mesh.devices.reshape(owners, tensor_ranks // 2, 2), EVERY)
    both = ("x", "core")
    placed = (
        P("dp", None),
        P("dp", None),
        P("dp"),
        P(),
        P(EVERY, None),
        P(EVERY, None),
        P(EVERY, None),
        P(),
        P(),
        P(),
        P(None, None, None, both, "dp", None),
        P(None, both, None, "dp", None),
        P(None, None, both, "dp", None),
        P(None, both, None, "dp", None),
        P(both, "dp", None, None, None),
        P(both, "dp", None, None, None),
        P(both, "dp", None, None, None),
        P(both, "dp", None, None, None),
    )
    matrices = placed[10:14]
    return jax.shard_map(
        shards,
        mesh=split,
        in_specs=placed,
        out_specs=(P(), P())
        + matrices
        + matrices
        + placed[14:16]
        + placed[4:7]
        + (P(), P(), P(), P()),
        check_vma=False,
    )
```

time: 2950 us -> 1020 us (0.35)
  waiting for transfers between devices: 2130 us -> 471 us
  local copies, waits for them, and re-layouts: 265 us -> 91.3 us
  matrix products: 192 us -> 28.1 us
  blocking collectives: 149 us -> 0 us
  Pallas kernels: 0 us -> 142 us
  starting transfers between devices: 12.1 us -> 142 us
  other arithmetic: 168 us -> 106 us
    reduce_scatter x12 -> x3, waiting for transfers between devices: 927 us -> 0.01 us  [send_ready(): arrived = lax.psum_scatter(array, GROUP, scatter_dimension=0, tiled=True)]
    unnamed x31 -> x5, waiting for transfers between devices: 581 us -> 0.08 us
    all_gather x16 -> x2, waiting for transfers between devices: 572 us -> 141 us  [fetch(): whole = lax.all_gather(low, GROUP, axis=0, tiled=False)]
    ppermute x0 -> x68, waiting for transfers between devices: none -> 257 us  [the longest x60 193 us: from_peer(): return lax.ppermute(values, axis, [(at, at ^ mask) for at in range(size)])]
    dot_general x41 -> x12, matrix products: 188 us -> 22.9 us  [the longest x2 6.48 us: product(): return jnp.dot(left, right, preferred_element_type=F32)]
    pallas_call x0 -> x28, Pallas kernels: none -> 142 us  [the longest x16 84.3 us: rows_product(): pl.pallas_call(kernel, grid=(steps,), in_specs=[whole(left.shape), pl.Blo...]
    all_gather x3 -> x0, blocking collectives: 110 us -> none  [the longest x2 68.6 us: fetch_weights(): lax.all_gather(for_sending(pieces), 'dp', axis=2, tiled=True)]
    ppermute x0 -> x68, starting transfers between devices: none -> 98.4 us  [the longest x60 86.2 us: from_peer(): return lax.ppermute(values, axis, [(at, at ^ mask) for at in range(size)])]
  transfers between devices with their start and end apart: 32 -> 78, of which waited for: 29 -> 40; matrix products, arithmetic and copies ran while one was open for 9% -> 17% of each run, Pallas kernels for 0% -> 11%
where the time goes in v1:
time: 1020 us; the launch traced here: 1010 us
  waiting for transfers between devices  471 us (46%)
  starting transfers between devices  142 us (14%)
  Pallas kernels  142 us (14%)
  other arithmetic  106 us (10%)
  local copies, waits for them, and re-layouts  91.3 us (9%)
  matrix products  28.1 us (3%)
  between operations  28.1 us (3%)
    ppermute x60, waiting for transfers between devices, from_peer(): return lax.ppermute(values, axis, [(at, at ^ mask) for at in range(size)])  193 us
    all_gather x2, waiting for transfers between devices, fetch(): whole = lax.all_gather(low, GROUP, axis=0, tiled=False)  141 us
    ppermute x60, starting transfers between devices, from_peer(): return lax.ppermute(values, axis, [(at, at ^ mask) for at in range(size)])  86.2 us
    pallas_call x16, Pallas kernels, rows_product(): pl.pallas_call(kernel, grid=(steps,), in_specs=[whole(left.shape), pl.Blo...  84.3 us
    ppermute x4, waiting for transfers between devices, from_last(): found = lax.ppermute(value, GROUP, step)  64.1 us
    all_to_all x2, waiting for transfers between devices, exchange(): lax.all_to_all(filled, EVERY, split_axis=0, concat_axis=0, tiled=True)  57.7 us
    pallas_call x4, Pallas kernels, attend(): pl.pallas_call(body, grid=(seqs, pairs), in_specs=specs, out_specs=out_sp...  33.7 us
    all_to_all x3, starting transfers between devices, shards(): lax.all_to_all(outgoing, 'dp', split_axis=0, concat_axis=0, tiled=True)  27.8 us
  transfers between devices with their start and end apart: 78, of which 40 were waited for; matrix products, arithmetic and copies ran while one was open for 17% of the time, Pallas kernels for 11%

profile of v1, /device:TPU:0, one launch (start us, length us, event | category | flops | bytes accessed | tf_op | source)
XLA Modules:
  0.0 1009.4 jit_solution(10846800915882362002)
XLA Ops:
  28.9 6.7 gather_fusion.1
  38.5 6.7 all-to-all-start.2
  56.7 57.7 %all-to-all-done.2 = bf16[32,24,1024]{2,1,0:T(8,128)(2,1)} async-done(((bf16[32,24,1024]{2,1,0:T(8,128)(2,1)}), bf16[32,24,1024]{2,1,0:T(8,128)(2,1)}, u32[]{:S(2)}, u32[]{:S(2)}) %all-to-all-start.2) | async-done | bytes 1572896 | tf_op jit(solution)/shard_map/all_to_all | solution.py:644
  116.4 64.1 %collective-permute-done.7 = bf16[256,1024]{1,0:T(8,128)(2,1)} collective-permute-done((bf16[256,1024]{1,0:T(8,128)(2,1)}, bf16[256,1024]{1,0:T(8,128)(2,1)}, u32[]{:S(2)}, u32[]{:S(2)}) %collective-permute-start.7) | collective-permute-done | bytes 524320 | tf_op jit(solution)/shard_map/ppermute | solution.py:158
  185.6 29.2 %all-gather.3.cloned.1.call-done = bf16[16,12,4,32,256]{4,3,2,1,0:T(8,128)(2,1)} async-done(((bf16[1,12,4,32,256]{4,3,2,1,0:T(8,128)(2,1)}), bf16[16,12,4,32,256]{4,3,2,1,0:T(8,128)(2,1)}) %all-gather.3.cloned.1.call-update) | async-done | bytes 12582928 | tf_op jit(solution)/shard_map/all_gather | solution.py:187
  214.8 5.2 shard_map.357.qkv_ref
  219.9 6.6 shard_map.358.refs_0_.left_ref
  236.0 8.6 shard_map.360
  244.5 5.6 shard_map.361
  255.3 112.2 %all-gather.5.cloned.1.call-done = bf16[16,12,4,32,256]{4,3,2,1,0:T(8,128)(2,1)} async-done(((bf16[1,12,4,32,256]{4,3,2,1,0:T(8,128)(2,1)}), bf16[16,12,4,32,256]{4,3,2,1,0:T(8,128)(2,1)}) %all-gather.5.cloned.1.call-update) | async-done | bytes 12582928 | tf_op jit(solution)/shard_map/all_gather | solution.py:187
  367.6 5.2 shard_map.362.qkv_ref
  372.8 6.6 shard_map.363.refs_0_.left_ref
  389.5 8.5 shard_map.365
  398.0 5.1 shard_map.366
  442.9 4.3 shard_map.367
  447.2 4.7 copy.144
  455.6 8.0 shard_map.368.right_ref.refs_0_
  463.6 4.3 shard_map.369
  467.9 4.6 copy.142
  472.6 5.5 shard_map.370
  497.9 10.3 %shard_map.373.right_ref.refs_0_ = bf16[3,512,512]{2,1,0:T(8,128)(2,1)S(1)} custom-call(f32[1,1,512]{2,1,0:T(1,128)S(1)} %compare_convert_fusion.live_ref, bf16[3,512,512]{2,1,0:T(8,128)(2,1)S(1)} %copy-done.24, bf16[512,512]{1,0:T(8,128)(2,1)S(1)} %shard_map.372.d_mixed_ref), custom_call_target="tpu_custom_call" | custom-call | flops 2684354560 | bytes 3145728 | tf_op jit(solution)/shard_map/pallas_call | solution.py:422
  510.7 5.0 shard_map.375
  522.5 4.4 shard_map.376
  526.9 7.9 shard_map.377.right_ref.refs_0_
  548.3 4.9 shard_map.379
  554.2 11.1 %collective-permute-done.24 = bf16[2,2,2,256,256]{4,3,2,1,0:T(8,128)(2,1)} collective-permute-done((bf16[2,2,2,256,256]{4,3,2,1,0:T(8,128)(2,1)S(1)}, bf16[2,2,2,256,256]{4,3,2,1,0:T(8,128)(2,1)}, u32[]{:S(2)}, u32[]{:S(2)}) %collective-permute-start.24) | collective-permute-done | bytes 1048608 | tf_op jit(solution)/shard_map/ppermute | solution.py:77
  576.4 8.5 collective-permute-done.25
  589.2 13.5 %collective-permute-done.26 = bf16[2,256,256]{2,1,0:T(8,128)(2,1)S(1)} collective-permute-done((bf16[2,256,256]{2,1,0:T(8,128)(2,1)S(1)}, bf16[2,256,256]{2,1,0:T(8,128)(2,1)S(1)}, u32[]{:S(2)}, u32[]{:S(2)}) %collective-permute-start.26) | collective-permute-done | bytes 262176 | tf_op jit(solution)/shard_map/ppermute | solution.py:77
  602.8 6.7 collective-permute-done.27
  612.6 10.3 %shard_map.382.right_ref.refs_0_ = bf16[3,512,512]{2,1,0:T(8,128)(2,1)S(1)} custom-call(f32[1,1,512]{2,1,0:T(1,128)S(1)} %compare_convert_fusion.live_ref, bf16[3,512,512]{2,1,0:T(8,128)(2,1)S(1)} %copy-done.22, bf16[512,512]{1,0:T(8,128)(2,1)S(1)} %shard_map.381.d_mixed_ref), custom_call_target="tpu_custom_call" | custom-call | flops 2684354560 | bytes 3145728 | tf_op jit(solution)/shard_map/pallas_call | solution.py:422
  650.1 10.6 %collective-permute-done.60 = bf16[2,2,256,256]{3,2,1,0:T(8,128)(2,1)S(1)} collective-permute-done((bf16[2,2,256,256]{3,2,1,0:T(8,128)(2,1)S(1)}, bf16[2,2,256,256]{3,2,1,0:T(8,128)(2,1)S(1)}, u32[]{:S(2)}, u32[]{:S(2)}) %collective-permute-start.60) | collective-permute-done | bytes 524320 | tf_op jit(solution)/shard_map/ppermute | solution.py:77
  679.0 4.5 collective-permute-done.34
  694.0 27.1 %collective-permute-done.35 = f32[27652]{0:T(1024)S(1)} collective-permute-done((f32[27652]{0:T(1024)S(1)}, f32[27652]{0:T(1024)S(1)}, u32[]{:S(2)}, u32[]{:S(2)}) %collective-permute-start.35) | collective-permute-done | bytes 110640 | tf_op jit(solution)/shard_map/ppermute | solution.py:77
  740.9 14.4 %collective-permute-done.37 = f32[27652]{0:T(1024)S(1)} collective-permute-done((f32[27652]{0:T(1024)S(1)}, f32[27652]{0:T(1024)S(1)}, u32[]{:S(2)}, u32[]{:S(2)}) %collective-permute-start.37) | collective-permute-done | bytes 110640 | tf_op jit(solution)/shard_map/ppermute | solution.py:77
  756.0 5.7 collective-permute-done.52
  763.9 9.3 collective-permute-done.48
  776.3 9.2 all-to-all-start.3
  793.8 34.5 %collective-permute-done.45 = bf16[2,256,256]{2,1,0:T(8,128)(2,1)S(1)} collective-permute-done((bf16[2,256,256]{2,1,0:T(8,128)(2,1)}, bf16[2,256,256]{2,1,0:T(8,128)(2,1)S(1)}, u32[]{:S(2)}, u32[]{:S(2)}) %collective-permute-start.45) | collective-permute-done | bytes 262176 | tf_op jit(solution)/shard_map/ppermute | solution.py:77
  828.4 10.6 %collective-permute-start.46 = (bf16[256,256]{1,0:T(8,128)(2,1)S(1)}, bf16[256,256]{1,0:T(8,128)(2,1)S(1)}, u32[]{:S(2)}, u32[]{:S(2)}) collective-permute-start(bf16[256,256]{1,0:T(8,128)(2,1)S(1)} %dynamic-slice_bitcast_fusion.18), channel_id=1, source_target_pairs={{0,16},{4,20},{8,24},{12,28},{16,0},{20,4},{24,8},{28,12},{1,17},{... | collective-permute-start | bytes 393224 | tf_op jit(solution)/shard_map/ppermute | solution.py:77
  857.5 9.7 all-to-all-start.5
  877.9 9.8 all-to-all-done.5
  887.7 14.5 %all-to-all-start.4 = ((bf16[8,2,4,32,256]{4,3,1,2,0:T(8,128)(2,1)}), bf16[8,2,4,32,256]{4,3,1,2,0:T(8,128)(2,1)}, u32[]{:S(2)}, u32[]{:S(2)}) async-start(bf16[8,2,4,32,256]{4,3,1,2,0:T(8,128)(2,1)} %maximum_bitcast_fusion), calls=%async_computation.7 | async-start | bytes 2097152 | tf_op jit(solution)/shard_map/all_to_all | solution.py:890
  918.0 5.1 all-to-all-done.4
  950.6 10.0 collective-permute-start.66
  961.2 4.7 collective-permute-start.67
  970.2 4.5 fusion.12
  975.3 4.3 fusion.13
  980.8 5.7 multiply_subtract_fusion
  (799 shorter events, 345.2 us)
Async XLA Ops:
  7.2 207.5 %all-gather.3.cloned.1.call-start = ((), (), s32[]{:S(2)}) async-start(), calls=%async_computation.10 | async-start | bytes 13369344 | tf_op jit(solution)/shard_map/all_gather | solution.py:187
  10.2 357.4 %all-gather.5.cloned.1.call-start = ((), (), s32[]{:S(2)}) async-start(), calls=%async_computation.11 | async-start | bytes 13369344 | tf_op jit(solution)/shard_map/all_gather | solution.py:187
  20.5 24.8 %collective-permute-start.3 = (bf16[256,1024]{1,0:T(8,128)(2,1)S(1)}, bf16[256,1024]{1,0:T(8,128)(2,1)S(1)}, u32[]{:S(2)}, u32[]{:S(2)}) collective-permute-start(bf16[256,1024]{1,0:T(8,128)(2,1)S(1)} %slice.615), channel_id=1, source_target_pairs={{0,1},{1,0},{2,3},{3,2},{4,5},{5,4},{6,7},{7,6},{8,9},{9,8},{10,11... | collective-permute-start | bytes 1572872 | tf_op jit(solution)/shard_map/ppermute | solution.py:77
  38.5 75.9 %all-to-all-start.2 = ((bf16[32,24,1024]{2,1,0:T(8,128)(2,1)}), bf16[32,24,1024]{2,1,0:T(8,128)(2,1)}, u32[]{:S(2)}, u32[]{:S(2)}) async-start(bf16[32,24,1024]{2,1,0:T(8,128)(2,1)} %select_convert_fusion.1), calls=%async_computation.2 | async-start | bytes 3145728 | tf_op jit(solution)/shard_map/all_to_all | solution.py:644
  45.2 828.8 %reduce-scatter.8.cloned.1.call-start = ((), (), s32[]{:S(2)}) async-start(), calls=%async_computation.14 | async-start | bytes 4456448 | tf_op jit(solution)/shard_map/reduce_scatter | solution.py:769
  52.0 128.5 %collective-permute-start.7 = (bf16[256,1024]{1,0:T(8,128)(2,1)}, bf16[256,1024]{1,0:T(8,128)(2,1)}, u32[]{:S(2)}, u32[]{:S(2)}) collective-permute-start(bf16[256,1024]{1,0:T(8,128)(2,1)} %broadcast_select_fusion.2), channel_id=1, source_target_pairs={{30,14},{28,12},{26,10},{24,8},{22,6},{20,4},{18,2},{16,0},{31,15}... | collective-permute-start | bytes 1572872 | tf_op jit(solution)/shard_map/ppermute | solution.py:158
  451.9 465.1 %reduce-scatter.4.cloned.1.call-start = ((), (), s32[]{:S(2)}) async-start(), calls=%async_computation.12 | async-start | bytes 4456448 | tf_op jit(solution)/shard_map/reduce_scatter | solution.py:769
  472.5 457.1 %reduce-scatter.6.cloned.1.call-start = ((), (), s32[]{:S(2)}) async-start(), calls=%async_computation.13 | async-start | bytes 4456448 | tf_op jit(solution)/shard_map/reduce_scatter | solution.py:769
  480.4 7.1 collective-permute-start.22
  520.6 44.6 %collective-permute-start.24 = (bf16[2,2,2,256,256]{4,3,2,1,0:T(8,128)(2,1)S(1)}, bf16[2,2,2,256,256]{4,3,2,1,0:T(8,128)(2,1)}, u32[]{:S(2)}, u32[]{:S(2)}) collective-permute-start(bf16[2,2,2,256,256]{4,3,2,1,0:T(8,128)(2,1)S(1)} %dynamic-slice_bitcast_fusion.1), channel_id=1, source_target_pairs={{0,2},{2,0},{1,3},{3,1},{4,6},{6,4},{5,7},{7,5},{8,10},{10,8},{9,1... | collective-permute-start | bytes 3145736 | tf_op jit(solution)/shard_map/ppermute | solution.py:77
  544.1 82.9 %collective-permute-start.59 = (bf16[2,2,2,256,256]{4,3,1,0,2:T(8,128)(2,1)}, bf16[2,2,2,256,256]{4,3,1,0,2:T(8,128)(2,1)}, u32[]{:S(2)}, u32[]{:S(2)}) collective-permute-start(bf16[2,2,2,256,256]{4,3,1,0,2:T(8,128)(2,1)} %bitcast.362), channel_id=1, source_target_pairs={{0,4},{4,0},{8,12},{12,8},{16,20},{20,16},{24,28},{28,24},{1,5},{5... | collective-permute-start | bytes 3145736 | tf_op jit(solution)/shard_map/ppermute | solution.py:77
  547.5 87.9 %collective-permute-start.55 = (bf16[2,2,2,256,256]{4,3,1,0,2:T(8,128)(2,1)}, bf16[2,2,2,256,256]{4,3,1,0,2:T(8,128)(2,1)}, u32[]{:S(2)}, u32[]{:S(2)}) collective-permute-start(bf16[2,2,2,256,256]{4,3,1,0,2:T(8,128)(2,1)} %bitcast.363), channel_id=1, source_target_pairs={{0,2},{2,0},{1,3},{3,1},{4,6},{6,4},{5,7},{7,5},{8,10},{10,8},{9,1... | collective-permute-start | bytes 3145736 | tf_op jit(solution)/shard_map/ppermute | solution.py:77
  554.2 17.7 %collective-permute-start.30 = (bf16[256,1024]{1,0:T(8,128)(2,1)}, bf16[256,1024]{1,0:T(8,128)(2,1)}, u32[]{:S(2)}, u32[]{:S(2)}) collective-permute-start(bf16[256,1024]{1,0:T(8,128)(2,1)} %slice.752), channel_id=1, source_target_pairs={{0,1},{1,0},{2,3},{3,2},{4,5},{5,4},{6,7},{7,6},{8,9},{9,8},{10,11... | collective-permute-start | bytes 1572872 | tf_op jit(solution)/shard_map/ppermute | solution.py:77
  567.5 17.4 %collective-permute-start.25 = (bf16[2,2,256,256]{3,2,1,0:T(8,128)(2,1)}, bf16[2,2,256,256]{3,2,1,0:T(8,128)(2,1)}, u32[]{:S(2)}, u32[]{:S(2)}) collective-permute-start(bf16[2,2,256,256]{3,2,1,0:T(8,128)(2,1)} %dynamic-slice_bitcast_fusion.7), channel_id=1, source_target_pairs={{0,8},{4,12},{8,0},{12,4},{16,24},{20,28},{24,16},{28,20},{1,9},{5... | collective-permute-start | bytes 1572872 | tf_op jit(solution)/shard_map/ppermute | solution.py:77
  586.1 16.6 %collective-permute-start.26 = (bf16[2,256,256]{2,1,0:T(8,128)(2,1)S(1)}, bf16[2,256,256]{2,1,0:T(8,128)(2,1)S(1)}, u32[]{:S(2)}, u32[]{:S(2)}) collective-permute-start(bf16[2,256,256]{2,1,0:T(8,128)(2,1)S(1)} %dynamic-slice_bitcast_fusion.13), channel_id=1, source_target_pairs={{0,16},{4,20},{8,24},{12,28},{16,0},{20,4},{24,8},{28,12},{1,17},{... | collective-permute-start | bytes 786440 | tf_op jit(solution)/shard_map/ppermute | solution.py:77
  589.2 20.4 %collective-permute-start.31 = (bf16[256,1024]{1,0:T(8,128)(2,1)S(1)}, bf16[256,1024]{1,0:T(8,128)(2,1)S(1)}, u32[]{:S(2)}, u32[]{:S(2)}) collective-permute-start(bf16[256,1024]{1,0:T(8,128)(2,1)S(1)} %get-tuple-element.421), channel_id=1, source_target_pairs={{0,1},{1,0},{2,3},{3,2},{4,5},{5,4},{6,7},{7,6},{8,9},{9,8},{10,11... | collective-permute-start | bytes 1572872 | tf_op jit(solution)/shard_map/ppermute | solution.py:77
  602.7 6.8 collective-permute-start.27
  628.8 31.9 %collective-permute-start.60 = (bf16[2,2,256,256]{3,2,1,0:T(8,128)(2,1)S(1)}, bf16[2,2,256,256]{3,2,1,0:T(8,128)(2,1)S(1)}, u32[]{:S(2)}, u32[]{:S(2)}) collective-permute-start(bf16[2,2,256,256]{3,2,1,0:T(8,128)(2,1)S(1)} %dynamic-slice_bitcast_fusion.2), channel_id=1, source_target_pairs={{0,2},{2,0},{1,3},{3,1},{4,6},{6,4},{5,7},{7,5},{8,10},{10,8},{9,1... | collective-permute-start | bytes 1572872 | tf_op jit(solution)/shard_map/ppermute | solution.py:77
  636.9 25.1 %collective-permute-start.56 = (bf16[2,2,256,256]{3,2,1,0:T(8,128)(2,1)S(1)}, bf16[2,2,256,256]{3,2,1,0:T(8,128)(2,1)S(1)}, u32[]{:S(2)}, u32[]{:S(2)}) collective-permute-start(bf16[2,2,256,256]{3,2,1,0:T(8,128)(2,1)S(1)} %dynamic-slice_bitcast_fusion.3), channel_id=1, source_target_pairs={{0,4},{4,0},{8,12},{12,8},{16,20},{20,16},{24,28},{28,24},{1,5},{5... | collective-permute-start | bytes 1572872 | tf_op jit(solution)/shard_map/ppermute | solution.py:77
  639.9 91.4 %collective-permute-start.51 = (bf16[2,2,2,256,256]{4,3,2,1,0:T(8,128)(2,1)}, bf16[2,2,2,256,256]{4,3,2,1,0:T(8,128)(2,1)}, u32[]{:S(2)}, u32[]{:S(2)}) collective-permute-start(bf16[2,2,2,256,256]{4,3,2,1,0:T(8,128)(2,1)} %dynamic-slice_bitcast_fusion), channel_id=1, source_target_pairs={{0,4},{4,0},{8,12},{12,8},{16,20},{20,16},{24,28},{28,24},{1,5},{5... | collective-permute-start | bytes 3145736 | tf_op jit(solution)/shard_map/ppermute | solution.py:77
  643.9 88.8 %collective-permute-start.47 = (bf16[2,2,2,256,256]{4,3,1,0,2:T(8,128)(2,1)}, bf16[2,2,2,256,256]{4,3,1,0,2:T(8,128)(2,1)}, u32[]{:S(2)}, u32[]{:S(2)}) collective-permute-start(bf16[2,2,2,256,256]{4,3,1,0,2:T(8,128)(2,1)} %bitcast.364), channel_id=1, source_target_pairs={{0,4},{4,0},{8,12},{12,8},{16,20},{20,16},{24,28},{28,24},{1,5},{5... | collective-permute-start | bytes 3145736 | tf_op jit(solution)/shard_map/ppermute | solution.py:77
  646.1 18.4 %collective-permute-start.32 = (bf16[256,1024]{1,0:T(8,128)(2,1)S(1)}, bf16[256,1024]{1,0:T(8,128)(2,1)S(1)}, u32[]{:S(2)}, u32[]{:S(2)}) collective-permute-start(bf16[256,1024]{1,0:T(8,128)(2,1)S(1)} %slice.751), channel_id=1, source_target_pairs={{0,1},{1,0},{2,3},{3,2},{4,5},{5,4},{6,7},{7,6},{8,9},{9,8},{10,11... | collective-permute-start | bytes 1572872 | tf_op jit(solution)/shard_map/ppermute | solution.py:77
  661.6 24.5 %collective-permute-start.61 = (bf16[2,256,256]{2,1,0:T(8,128)(2,1)}, bf16[2,256,256]{2,1,0:T(8,128)(2,1)}, u32[]{:S(2)}, u32[]{:S(2)}) collective-permute-start(bf16[2,256,256]{2,1,0:T(8,128)(2,1)} %dynamic-slice_bitcast_fusion.8), channel_id=1, source_target_pairs={{0,8},{4,12},{8,0},{12,4},{16,24},{20,28},{24,16},{28,20},{1,9},{5... | collective-permute-start | bytes 786440 | tf_op jit(solution)/shard_map/ppermute | solution.py:77
  662.9 28.4 %collective-permute-start.57 = (bf16[2,256,256]{2,1,0:T(8,128)(2,1)}, bf16[2,256,256]{2,1,0:T(8,128)(2,1)}, u32[]{:S(2)}, u32[]{:S(2)}) collective-permute-start(bf16[2,256,256]{2,1,0:T(8,128)(2,1)} %dynamic-slice_bitcast_fusion.9), channel_id=1, source_target_pairs={{0,8},{4,12},{8,0},{12,4},{16,24},{20,28},{24,16},{28,20},{1,9},{5... | collective-permute-start | bytes 786440 | tf_op jit(solution)/shard_map/ppermute | solution.py:77
  672.8 10.7 %collective-permute-start.34 = (f32[27652]{0:T(1024)S(1)}, f32[27652]{0:T(1024)S(1)}, u32[]{:S(2)}, u32[]{:S(2)}) collective-permute-start(f32[27652]{0:T(1024)S(1)} %add.1249), channel_id=1, source_target_pairs={{0,2},{2,0},{1,3},{3,1},{4,6},{6,4},{5,7},{7,5},{8,10},{10,8},{9,1... | collective-permute-start | bytes 331832 | tf_op jit(solution)/shard_map/ppermute | solution.py:77
  683.5 53.6 %collective-permute-start.43 = (bf16[2,2,2,256,256]{4,3,1,0,2:T(8,128)(2,1)S(1)}, bf16[2,2,2,256,256]{4,3,1,0,2:T(8,128)(2,1)S(1)}, u32[]{:S(2)}, u32[]{:S(2)}) collective-permute-start(bf16[2,2,2,256,256]{4,3,1,0,2:T(8,128)(2,1)S(1)} %bitcast.428), channel_id=1, source_target_pairs={{0,2},{2,0},{1,3},{3,1},{4,6},{6,4},{5,7},{7,5},{8,10},{10,8},{9,1... | collective-permute-start | bytes 3145736 | tf_op jit(solution)/shard_map/ppermute | solution.py:77
  686.1 53.6 %collective-permute-start.38 = (bf16[256,1024]{1,0:T(8,128)(2,1)}, bf16[256,1024]{1,0:T(8,128)(2,1)S(1)}, u32[]{:S(2)}, u32[]{:S(2)}) collective-permute-start(bf16[256,1024]{1,0:T(8,128)(2,1)} %add_convert_fusion), channel_id=1, source_target_pairs={{14,30},{12,28},{10,26},{8,24},{6,22},{4,20},{2,18},{0,16},{15,31}... | collective-permute-start | bytes 1572872 | tf_op jit(solution)/shard_map/ppermute | solution.py:168
  691.4 29.8 %collective-permute-start.35 = (f32[27652]{0:T(1024)S(1)}, f32[27652]{0:T(1024)S(1)}, u32[]{:S(2)}, u32[]{:S(2)}) collective-permute-start(f32[27652]{0:T(1024)S(1)} %add.1250), channel_id=1, source_target_pairs={{0,4},{4,0},{8,12},{12,8},{16,20},{20,16},{24,28},{28,24},{1,5},{5... | collective-permute-start | bytes 331832 | tf_op jit(solution)/shard_map/ppermute | solution.py:77
  727.0 122.7 %collective-permute-start.62 = (bf16[256,256]{1,0:T(8,128)(2,1)}, bf16[256,256]{1,0:T(8,128)(2,1)}, u32[]{:S(2)}, u32[]{:S(2)}) collective-permute-start(bf16[256,256]{1,0:T(8,128)(2,1)} %dynamic-slice_bitcast_fusion.14), channel_id=1, source_target_pairs={{0,16},{4,20},{8,24},{12,28},{16,0},{20,4},{24,8},{28,12},{1,17},{... | collective-permute-start | bytes 393224 | tf_op jit(solution)/shard_map/ppermute | solution.py:77
  731.2 117.5 %collective-permute-start.58 = (bf16[256,256]{1,0:T(8,128)(2,1)}, bf16[256,256]{1,0:T(8,128)(2,1)}, u32[]{:S(2)}, u32[]{:S(2)}) collective-permute-start(bf16[256,256]{1,0:T(8,128)(2,1)} %dynamic-slice_bitcast_fusion.15), channel_id=1, source_target_pairs={{0,16},{4,20},{8,24},{12,28},{16,0},{20,4},{24,8},{28,12},{1,17},{... | collective-permute-start | bytes 393224 | tf_op jit(solution)/shard_map/ppermute | solution.py:77
  732.7 22.6 %collective-permute-start.37 = (f32[27652]{0:T(1024)S(1)}, f32[27652]{0:T(1024)S(1)}, u32[]{:S(2)}, u32[]{:S(2)}) collective-permute-start(f32[27652]{0:T(1024)S(1)} %add.1252), channel_id=1, source_target_pairs={{0,16},{4,20},{8,24},{12,28},{16,0},{20,4},{24,8},{28,12},{1,17},{... | collective-permute-start | bytes 331832 | tf_op jit(solution)/shard_map/ppermute | solution.py:77
  737.1 24.5 %collective-permute-start.52 = (bf16[2,2,256,256]{3,2,1,0:T(8,128)(2,1)S(1)}, bf16[2,2,256,256]{3,2,1,0:T(8,128)(2,1)S(1)}, u32[]{:S(2)}, u32[]{:S(2)}) collective-permute-start(bf16[2,2,256,256]{3,2,1,0:T(8,128)(2,1)S(1)} %dynamic-slice_bitcast_fusion.4), channel_id=1, source_target_pairs={{0,8},{4,12},{8,0},{12,4},{16,24},{20,28},{24,16},{28,20},{1,9},{5... | collective-permute-start | bytes 1572872 | tf_op jit(solution)/shard_map/ppermute | solution.py:77
  739.8 33.3 %collective-permute-start.48 = (bf16[2,2,256,256]{3,2,1,0:T(8,128)(2,1)S(1)}, bf16[2,2,256,256]{3,2,1,0:T(8,128)(2,1)S(1)}, u32[]{:S(2)}, u32[]{:S(2)}) collective-permute-start(bf16[2,2,256,256]{3,2,1,0:T(8,128)(2,1)S(1)} %dynamic-slice_bitcast_fusion.5), channel_id=1, source_target_pairs={{0,2},{2,0},{1,3},{3,1},{4,6},{6,4},{5,7},{7,5},{8,10},{10,8},{9,1... | collective-permute-start | bytes 1572872 | tf_op jit(solution)/shard_map/ppermute | solution.py:77
  755.3 19.1 %collective-permute-start.44 = (bf16[2,2,256,256]{3,2,1,0:T(8,128)(2,1)S(1)}, bf16[2,2,256,256]{3,2,1,0:T(8,128)(2,1)S(1)}, u32[]{:S(2)}, u32[]{:S(2)}) collective-permute-start(bf16[2,2,256,256]{3,2,1,0:T(8,128)(2,1)S(1)} %dynamic-slice_bitcast_fusion.6), channel_id=1, source_target_pairs={{0,4},{4,0},{8,12},{12,8},{16,20},{20,16},{24,28},{28,24},{1,5},{5... | collective-permute-start | bytes 1572872 | tf_op jit(solution)/shard_map/ppermute | solution.py:77
  761.6 105.6 %collective-permute-start.39 = (bf16[256,1024]{1,0:T(8,128)(2,1)}, bf16[256,1024]{1,0:T(8,128)(2,1)}, u32[]{:S(2)}, u32[]{:S(2)}) collective-permute-start(bf16[256,1024]{1,0:T(8,128)(2,1)} %fusion.77), channel_id=1, source_target_pairs={{22,30},{20,28},{18,26},{16,24},{23,31},{21,29},{19,27},{17,25}} | collective-permute-start | bytes 1572872 | tf_op jit(solution)/shard_map/ppermute | solution.py:168
  773.1 16.2 %collective-permute-start.53 = (bf16[2,256,256]{2,1,0:T(8,128)(2,1)}, bf16[2,256,256]{2,1,0:T(8,128)(2,1)}, u32[]{:S(2)}, u32[]{:S(2)}) collective-permute-start(bf16[2,256,256]{2,1,0:T(8,128)(2,1)} %dynamic-slice_bitcast_fusion.10), channel_id=1, source_target_pairs={{0,16},{4,20},{8,24},{12,28},{16,0},{20,4},{24,8},{28,12},{1,17},{... | collective-permute-start | bytes 786440 | tf_op jit(solution)/shard_map/ppermute | solution.py:77
  774.4 54.0 %collective-permute-start.49 = (bf16[2,256,256]{2,1,0:T(8,128)(2,1)}, bf16[2,256,256]{2,1,0:T(8,128)(2,1)}, u32[]{:S(2)}, u32[]{:S(2)}) collective-permute-start(bf16[2,256,256]{2,1,0:T(8,128)(2,1)} %dynamic-slice_bitcast_fusion.11), channel_id=1, source_target_pairs={{0,8},{4,12},{8,0},{12,4},{16,24},{20,28},{24,16},{28,20},{1,9},{5... | collective-permute-start | bytes 786440 | tf_op jit(solution)/shard_map/ppermute | solution.py:77
  776.3 77.4 %all-to-all-start.3 = ((bf16[32,24,1024]{2,1,0:T(8,128)(2,1)}), bf16[32,24,1024]{2,1,0:T(8,128)(2,1)S(1)}, u32[]{:S(2)}, u32[]{:S(2)}) async-start(bf16[32,24,1024]{2,1,0:T(8,128)(2,1)} %bitcast.48), calls=%async_computation.3 | async-start | bytes 3145728 | tf_op jit(solution)/shard_map/all_to_all | solution.py:644
  789.4 39.0 %collective-permute-start.45 = (bf16[2,256,256]{2,1,0:T(8,128)(2,1)}, bf16[2,256,256]{2,1,0:T(8,128)(2,1)S(1)}, u32[]{:S(2)}, u32[]{:S(2)}) collective-permute-start(bf16[2,256,256]{2,1,0:T(8,128)(2,1)} %dynamic-slice_bitcast_fusion.12), channel_id=1, source_target_pairs={{0,8},{4,12},{8,0},{12,4},{16,24},{20,28},{24,16},{28,20},{1,9},{5... | collective-permute-start | bytes 786440 | tf_op jit(solution)/shard_map/ppermute | solution.py:77
  828.3 20.4 %collective-permute-start.54 = (bf16[256,256]{1,0:T(8,128)(2,1)S(1)}, bf16[256,256]{1,0:T(8,128)(2,1)S(1)}, u32[]{:S(2)}, u32[]{:S(2)}) collective-permute-start(bf16[256,256]{1,0:T(8,128)(2,1)S(1)} %dynamic-slice_bitcast_fusion.16), channel_id=1, source_target_pairs={{0,2},{2,0},{1,3},{3,1},{4,6},{6,4},{5,7},{7,5},{8,10},{10,8},{9,1... | collective-permute-start | bytes 393224 | tf_op jit(solution)/shard_map/ppermute | solution.py:77
  828.4 13.6 %collective-permute-start.46 = (bf16[256,256]{1,0:T(8,128)(2,1)S(1)}, bf16[256,256]{1,0:T(8,128)(2,1)S(1)}, u32[]{:S(2)}, u32[]{:S(2)}) collective-permute-start(bf16[256,256]{1,0:T(8,128)(2,1)S(1)} %dynamic-slice_bitcast_fusion.18), channel_id=1, source_target_pairs={{0,16},{4,20},{8,24},{12,28},{16,0},{20,4},{24,8},{28,12},{1,17},{... | collective-permute-start | bytes 393224 | tf_op jit(solution)/shard_map/ppermute | solution.py:77
  857.5 30.2 %all-to-all-start.5 = ((bf16[8,2,4,32,256]{4,3,1,2,0:T(8,128)(2,1)}), bf16[8,2,4,32,256]{4,3,1,2,0:T(8,128)(2,1)}, u32[]{:S(2)}, u32[]{:S(2)}) async-start(bf16[8,2,4,32,256]{4,3,1,2,0:T(8,128)(2,1)} %maximum_bitcast_fusion.1), calls=%async_computation.8 | async-start | bytes 2097152 | tf_op jit(solution)/shard_map/all_to_all | solution.py:890
  872.5 29.7 %collective-permute-start.41 = (bf16[256,1024]{1,0:T(8,128)(2,1)}, bf16[256,1024]{1,0:T(8,128)(2,1)}, u32[]{:S(2)}, u32[]{:S(2)}) collective-permute-start(bf16[256,1024]{1,0:T(8,128)(2,1)} %fusion.84), channel_id=1, source_target_pairs={{28,30},{29,31}} | collective-permute-start | bytes 1572872 | tf_op jit(solution)/shard_map/ppermute | solution.py:168
  887.7 35.5 %all-to-all-start.4 = ((bf16[8,2,4,32,256]{4,3,1,2,0:T(8,128)(2,1)}), bf16[8,2,4,32,256]{4,3,1,2,0:T(8,128)(2,1)}, u32[]{:S(2)}, u32[]{:S(2)}) async-start(bf16[8,2,4,32,256]{4,3,1,2,0:T(8,128)(2,1)} %maximum_bitcast_fusion), calls=%async_computation.7 | async-start | bytes 2097152 | tf_op jit(solution)/shard_map/all_to_all | solution.py:890
  934.4 6.9 collective-permute-start.63
  937.7 48.8 %all-to-all-start.6 = ((bf16[8,2,4,32,256]{4,3,1,2,0:T(8,128)(2,1)}), bf16[8,2,4,32,256]{4,3,1,2,0:T(8,128)(2,1)S(1)}, u32[]{:S(2)}, u32[]{:S(2)}) async-start(bf16[8,2,4,32,256]{4,3,1,2,0:T(8,128)(2,1)} %copy_bitcast_fusion), calls=%async_computation.9 | async-start | bytes 2097152 | tf_op jit(solution)/shard_map/all_to_all | solution.py:890
  950.6 10.0 collective-permute-start.66
  961.2 6.9 collective-permute-start.67
  (206 other events, 3294.8 us)
Sparse Core Ops, SparseCore 0:
  11.4 203.2 all-gather.2
  218.1 149.4 all-gather.4
  452.1 110.5 reduce-scatter.7
  564.8 121.5 reduce-scatter.3
  688.5 135.5 reduce-scatter.5

commit v2 on v1

--- a/solution.py
+++ b/solution.py
@@ -87,33 +87,18 @@
     return found
 
 
-def routes():
+def scatter_sum(slots):
     masks = [1]
     while masks[-1] * 2 < lax.axis_size("dp"):
         masks.append(masks[-1] * 2)
-    across = [("x", 1)]
-    near = [("dp", masks[0])]
-    far = [("dp", mask) for mask in masks[1:]]
-    return (
-        across + near + far,
-        near + across + far,
-        across + far + near,
-        near + far + across,
-    )
-
-
-def scatter_sum(parts, route):
-    masks = sorted((mask for axis, mask in route if axis == "dp"), reverse=True)
-    left = [("dp", mask) for mask in masks] + [("x", 1)]
-    parts = parts.reshape((2,) * len(left) + parts.shape[-2:])
-    for axis, mask in route:
-        dim = left.index((axis, mask))
-        left.pop(dim)
-        bit = lax.axis_index(axis) // mask % 2
-        keep = lax.dynamic_index_in_dim(parts, bit, dim, keepdims=False)
-        away = lax.dynamic_index_in_dim(parts, 1 - bit, dim, keepdims=False)
-        parts = keep + from_peer(away, axis, mask)
-    return parts
+    slots = slots.reshape((2,) * len(masks) + slots.shape[1:])
+    for at, mask in enumerate(masks):
+        bit = lax.axis_index("dp") // mask % 2
+        dim = len(masks) - 1 - at
+        away = lax.dynamic_index_in_dim(slots, 1 - bit, dim, keepdims=False)
+        keep = lax.dynamic_index_in_dim(slots, bit, dim, keepdims=False)
+        slots = keep + from_peer(away, "dp", mask)
+    return slots
 
 
 def sum_over_all(values):
@@ -142,23 +127,24 @@
     count = lax.axis_size("dp") * lax.axis_size("x")
     holders = [count - 1]
     steps = []
-    mask = 1
-    while mask < count:
+    mask = count // 2
+    while mask > 0:
         steps.append([(at, at ^ mask) for at in holders])
         holders = holders + [at ^ mask for at in holders]
-        mask = mask * 2
+        mask = mask // 2
     return steps
 
 
 def from_last(parts):
+    last = lax.axis_size("core") - 1
+    return jnp.where(lax.axis_index("core") == last, parts[last], from_peer(parts[0], "core"))
+
+
+def spread_from(value, step):
     at = lax.axis_index("dp") * lax.axis_size("x") + lax.axis_index("x")
-    last = lax.axis_size("core") - 1
-    value = jnp.where(lax.axis_index("core") == last, parts[last], from_peer(parts[0], "core"))
-    for step in tree():
-        found = lax.ppermute(value, GROUP, step)
-        reached = jnp.any(at == jnp.array([there for here, there in step]))
-        value = jnp.where(reached, found, value)
-    return value
+    found = lax.ppermute(value, GROUP, step)
+    reached = jnp.any(at == jnp.array([there for here, there in step]))
+    return jnp.where(reached, found, value)
 
 
 def to_last(value):
@@ -169,43 +155,62 @@
     return jnp.concatenate([from_peer(total.astype(BF), "core").astype(F32), total], axis=0)
 
 
+def after(values, *first):
+    return lax.optimization_barrier((values,) + first)[0]
+
+
 def collect(values):
-    return jnp.concatenate([values, from_peer(values, "core")], axis=0)
-
-
-def spread(values):
-    half = values.shape[0] // 2
-    return values[:half] + from_peer(values[half:].astype(BF), "core").astype(F32)
-
-
-def column_sum(values):
-    return jnp.sum(values.astype(F32), axis=0)
+    across = from_peer(values, "x")
+    return jnp.concatenate([values, from_peer(values, "core")], axis=0), across
+
+
+def complete(across):
+    return jnp.concatenate([across, from_peer(across, "core")], axis=0)
+
+
+def spread_first(other):
+    rows = other.shape[0] // 2
+    away = other[:rows] + from_peer(other[rows:].astype(BF), "core").astype(F32)
+    return away.astype(BF)
+
+
+def spread_last(own, away):
+    rows = own.shape[0] // 2
+    near = own[:rows] + from_peer(own[rows:].astype(BF), "core").astype(F32)
+    return near + from_peer(away, "x").astype(F32)
+
+
+def column_sum(*members):
+    return sum(jnp.sum(values.astype(F32), axis=0) for values in members)
 
 
 def fetch(pieces):
-    low = pieces.astype(BF)
-    whole = lax.all_gather(low, GROUP, axis=0, tiled=False)
-    return whole.reshape((lax.axis_size("dp"), lax.axis_size("x")) + low.shape)
-
-
-def fetch_layer(in_proj, out_proj, up_proj, down_proj, layer_no):
+    return lax.all_gather(pieces, "dp", axis=0, tiled=False)[:, None]
+
+
+def layer_rows(in_proj, out_proj, up_proj, down_proj, layer_no):
     rows, width = in_proj.shape[-2:]
     row_blocks = in_proj.shape[1]
     feed = up_proj.shape[2]
-    pieces = [
+    attend_rows = [
         in_proj[layer_no].reshape(row_blocks, 3, rows, width).transpose(1, 0, 2, 3),
         out_proj[layer_no].reshape(1, row_blocks, rows, width),
+    ]
+    feed_rows = [
         up_proj[layer_no].reshape(row_blocks, feed, rows, width),
         down_proj[layer_no].reshape(feed, row_blocks, rows, width),
     ]
-    all_of = fetch(jnp.concatenate(pieces, axis=0))
-    of_x = (1, all_of.shape[1], 0)
+    return [jnp.concatenate(rows, axis=0).astype(BF) for rows in (attend_rows, feed_rows)]
+
+
+def named_layer(attend_all, feed_all, row_blocks, feed):
+    of_x = (1, attend_all.shape[1], 0)
     second = (3, row_blocks, 0)
     return (
-        (all_of, {"x": of_x, "low": (2, 3, 0), "high": second}),
-        (all_of, {"x": of_x, "low": second, "high": (2, 1, 3)}),
-        (all_of, {"x": of_x, "low": second, "high": (2, row_blocks, 4)}),
-        (all_of, {"x": of_x, "low": second, "high": (2, feed, 4 + row_blocks)}),
+        (attend_all, {"x": of_x, "low": (2, 3, 0), "high": second}),
+        (attend_all, {"x": of_x, "low": second, "high": (2, 1, 3)}),
+        (feed_all, {"x": of_x, "low": second, "high": (2, row_blocks, 0)}),
+        (feed_all, {"x": of_x, "low": second, "high": (2, feed, row_blocks)}),
     )
 
 
@@ -307,38 +312,58 @@
     )(left, weights, *by_column)
 
 
-def block_grads(left, right, ranks, high, low, side, x_on_left):
-    def kernel(left_ref, right_ref, out_ref):
+def block_grads(lefts, rights, ranks, high, low, side, x_on_left, owners=None):
+    count = len(lefts)
+
+    def kernel(*refs):
         step = pl.program_id(0)
+        out_ref = refs[2 * count]
         for at in range(ranks if x_on_left else 1):
             begin = pl.multiple_of((at * high + step) * side, side)
-            part = left_ref[:, pl.ds(begin, side)]
+            parts = [ref[:, pl.ds(begin, side)] for ref in refs[:count]]
             for low_at in range(low):
                 for rank in range(1 if x_on_left else ranks):
                     if x_on_left:
                         number, target = low_at, at
-                    elif len(right_ref.shape) == 3:
+                    elif len(refs[count].shape) == 3:
                         number, target = low_at * ranks + rank, rank
                     else:
                         number, target = rank * low + low_at, rank
-                    block = columns_of(right_ref, number, side)
-                    out_ref[low_at, target] = lax.dot_general(
-                        part, block, (((0,), (0,)), ((), ())), preferred_element_type=F32
-                    ).astype(BF)
-
+                    total = None
+                    for part, right_ref in zip(parts, refs[count : 2 * count]):
+                        block = columns_of(right_ref, number, side)
+                        term = lax.dot_general(
+                            part, block, (((0,), (0,)), ((), ())), preferred_element_type=F32
+                        )
+                        total = term if total is None else total + term
+                    if owners is None:
+                        out_ref[low_at, target] = total.astype(BF)
+                    else:
+                        out_ref[low_at, target, 0] = total.astype(BF)
+
+    if owners is None:
+        out_spec = pl.BlockSpec((low, ranks, side, side), lambda step: (step, 0, 0, 0))
+        out_shape = (high * low, ranks, side, side)
+    else:
+        per = owners // low
+        out_spec = pl.BlockSpec(
+            (low, ranks, 1, side, side),
+            lambda step: (lax.rem(step, per), 0, lax.div(step, per), 0, 0),
+        )
+        out_shape = (owners, ranks, high * low // owners, side, side)
     return pl.pallas_call(
         kernel,
         grid=(high,),
-        in_specs=[whole(left.shape), whole(right.shape)],
-        out_specs=pl.BlockSpec((low, ranks, side, side), lambda step: (step, 0, 0, 0)),
-        out_shape=jax.ShapeDtypeStruct((high * low, ranks, side, side), BF),
+        in_specs=[whole(member.shape) for member in tuple(lefts) + tuple(rights)],
+        out_specs=out_spec,
+        out_shape=jax.ShapeDtypeStruct(out_shape, BF),
         compiler_params=wide(),
         cost_estimate=pl.CostEstimate(
-            flops=2 * left.shape[-2] * high * low * ranks * side * side,
+            flops=2 * count * lefts[0].shape[-2] * high * low * ranks * side * side,
             bytes_accessed=2 * high * low * ranks * side * side,
             transcendentals=0,
         ),
-    )(left, right)
+    )(*lefts, *rights)
 
 
 PAIR = 2 * HD
@@ -469,41 +494,60 @@
 def layer_forward(residual, weights, pieces, keys_live):
     w_in, w_out, w_up, w_down = weights
     bias_q, bias_v, bias_up, bias_out, bias_down, gain_one, shift_one, gain_two, shift_two = pieces
-    gathered = collect(residual.astype(BF))
     bias_in = jnp.concatenate([bias_q, jnp.zeros_like(bias_q), bias_v]).reshape(1, -1)
-    (qkv,) = rows_product(
-        gathered, *w_in, ("high",), ("low", "x"), [(3, BF)], plus, [bias_in]
-    )
-    mixed = attend(qkv, keys_live)
-    (mixed_out,) = rows_product(mixed, *w_out, ("x", "high"), ("low",), [(1, F32)], same)
-    first_in = residual + (spread(mixed_out) + bias_out)
+
+    def mix(rows, live):
+        (projected,) = rows_product(
+            rows, *w_in, ("high",), ("low", "x"), [(3, BF)], plus, [bias_in]
+        )
+        return projected, attend(projected, live)
+
+    def mix_out(mixed):
+        return rows_product(mixed, *w_out, ("x", "high"), ("low",), [(1, F32)], same)[0]
+
+    def feed(rows):
+        return rows_product(
+            rows,
+            *w_up,
+            ("high",),
+            ("x", "low"),
+            [(1, F32), (1, BF)],
+            plus_gelu,
+            [bias_up.reshape(1, -1)],
+        )
+
+    def feed_out(active):
+        return rows_product(active, *w_down, ("x", "high"), ("low",), [(1, F32)], same)[0]
+
+    own, across = collect(residual.astype(BF))
+    own_qkv, own_mixed = mix(own, keys_live[0])
+    other = complete(after(across, own_mixed))
+    other_qkv, other_mixed = mix(other, keys_live[1])
+    away = spread_first(mix_out(other_mixed))
+    own_out = mix_out(after(own_mixed, away))
+    first_in = residual + (spread_last(own_out, away) + bias_out)
     middle = layer_norm(first_in, gain_one, shift_one)
-    spread_mid = collect(middle.astype(BF))
-    hidden_pre, hidden_act = rows_product(
-        spread_mid,
-        *w_up,
-        ("high",),
-        ("x", "low"),
-        [(1, F32), (1, BF)],
-        plus_gelu,
-        [bias_up.reshape(1, -1)],
-    )
-    (fed_out,) = rows_product(hidden_act, *w_down, ("x", "high"), ("low",), [(1, F32)], same)
-    second_in = middle + (spread(fed_out) + bias_down)
+    own_mid, across = collect(middle.astype(BF))
+    own_pre, own_act = feed(own_mid)
+    other_mid = complete(after(across, own_act))
+    other_pre, other_act = feed(other_mid)
+    away = spread_first(feed_out(other_act))
+    own_out = feed_out(after(own_act, away))
+    second_in = middle + (spread_last(own_out, away) + bias_down)
     kept_values = (
         first_in,
         second_in,
-        gathered,
-        qkv,
-        mixed,
-        spread_mid,
-        hidden_pre,
-        hidden_act,
+        (own, other),
+        (own_qkv, other_qkv),
+        (own_mixed, other_mixed),
+        (own_mid, other_mid),
+        (own_pre, other_pre),
+        (own_act, other_act),
     )
     return (layer_norm(second_in, gain_two, shift_two), kept_values)
 
 
-def layer_backward(upstream, kept_values, weights, pieces, keys_live):
+def layer_backward(upstream, kept_values, weights, pieces, keys_live, dealt, emit):
     (
         first_in,
         second_in,
@@ -520,35 +564,53 @@
     row_blocks, feed = w_in[1]["high"][1], w_up[1]["low"][1]
     d_second, d_gain_two, d_shift_two = norm_back(second_in, gain_two, shift_two, upstream)
     d_fed = d_second.astype(BF)
-    d_fed_all = collect(d_fed)
-    parts = block_grads(hidden_act, d_fed_all, ranks, feed, row_blocks, side, True)
-    d_fed_all, parts = lax.optimization_barrier((d_fed_all, parts))
-    yield "down", parts
-    (d_pre,) = rows_product(
-        d_fed_all, *w_down, ("low",), ("x", "high"), [(1, BF)], times_gelu_slope, [hidden_pre]
-    )
-    parts = block_grads(spread_mid, d_pre, ranks, row_blocks, feed, side, False)
-    d_pre, parts = lax.optimization_barrier((d_pre, parts))
-    yield "up", parts
-    (d_up_in,) = rows_product(d_pre, *w_up, ("x", "low"), ("high",), [(1, F32)], same)
-    d_middle = d_second + spread(d_up_in)
+
+    def feed_back(rows, before):
+        return rows_product(
+            rows, *w_down, ("low",), ("x", "high"), [(1, BF)], times_gelu_slope, [before]
+        )[0]
+
+    def up_back(rows):
+        return rows_product(rows, *w_up, ("x", "low"), ("high",), [(1, F32)], same)[0]
+
+    own, across = collect(d_fed)
+    own_pre = feed_back(own, hidden_pre[0])
+    other = complete(after(across, own_pre))
+    other_pre = feed_back(other, hidden_pre[1])
+    away = spread_first(up_back(other_pre))
+    own = after(own, away)
+    parts = block_grads(hidden_act, (own, other), ranks, feed, row_blocks, side, True, dealt["down"])
+    own_pre = emit("down", parts, own_pre)
+    d_pre = (own_pre, other_pre)
+    parts = block_grads(spread_mid, d_pre, ranks, row_blocks, feed, side, False, dealt["up"])
+    own_pre = emit("up", parts, own_pre)
+    d_middle = d_second + spread_last(up_back(own_pre), away)
     d_first, d_gain_one, d_shift_one = norm_back(first_in, gain_one, shift_one, d_middle)
     d_branch = d_first.astype(BF)
-    d_branch_all = collect(d_branch)
-    parts = block_grads(mixed, d_branch_all, ranks, 1, row_blocks, side, True)
-    d_branch_all, parts = lax.optimization_barrier((d_branch_all, parts))
-    yield "out", parts
-    (d_mixed,) = rows_product(d_branch_all, *w_out, ("low",), ("x", "high"), [(1, BF)], same)
-    d_qkv = attend(qkv, keys_live, d_mixed)
+
+    def mix_back(rows, projected, live):
+        (d_mixed,) = rows_product(rows, *w_out, ("low",), ("x", "high"), [(1, BF)], same)
+        return attend(projected, live, d_mixed)
+
+    def in_back(rows):
+        return rows_product(rows, *w_in, ("low", "x"), ("high",), [(1, F32)], same)[0]
+
+    own, across = collect(d_branch)
+    own_qkv = mix_back(own, qkv[0], keys_live[0])
+    other = complete(after(across, own_qkv))
+    other_qkv = mix_back(other, qkv[1], keys_live[1])
+    away = spread_first(in_back(other_qkv))
+    own = after(own, away)
+    parts = block_grads(mixed, (own, other), ranks, 1, row_blocks, side, True)
+    own_qkv = emit("out", parts, own_qkv)
+    d_qkv = (own_qkv, other_qkv)
     parts = block_grads(gathered, d_qkv, ranks, row_blocks, 3, side, False)
-    d_qkv, parts = lax.optimization_barrier((d_qkv, parts))
-    yield "in", parts
-    (d_in,) = rows_product(d_qkv, *w_in, ("low", "x"), ("high",), [(1, F32)], same)
-    d_residual = d_first + spread(d_in)
+    own_qkv = emit("in", parts, own_qkv)
+    d_residual = d_first + spread_last(in_back(own_qkv), away)
     bias_grads = (
-        column_sum(d_qkv[0]),
-        column_sum(d_qkv[2]),
-        column_sum(d_pre),
+        column_sum(*[member[0] for member in d_qkv]),
+        column_sum(*[member[2] for member in d_qkv]),
+        column_sum(*d_pre),
         column_sum(d_branch),
         column_sum(d_fed),
         d_gain_one,
@@ -556,7 +618,7 @@
         d_gain_two,
         d_shift_two,
     )
-    yield "rest", (d_residual, bias_grads)
+    return d_residual, bias_grads
 
 
 def shards(
@@ -610,14 +672,31 @@
     my_length = jnp.take(lengths, my_sequence)
     counted = (my_rows % seq_slots < my_length).astype(F32)
     my_labels = mine(labels).astype(F32)
-    turned = (jnp.arange(group_rows) + core * local_rows) % group_rows
-    keys_live = (turned % seq_slots < jnp.take(lengths, rank * seqs + turned // seq_slots)).reshape(
-        seqs, seq_slots
-    )
+    turned = (jnp.arange(seq_slots) + core * local_rows) % seq_slots
+    keys_live = [
+        (turned < lax.dynamic_index_in_dim(lengths, which, 0, keepdims=False))[None]
+        for which in (rank, rank ^ 1)
+    ]
+
+    rows_here = [
+        layer_rows(in_proj, out_proj, up_proj, down_proj, layer_no) for layer_no in range(layers)
+    ]
+    rows_here[0][0], token_ids = lax.optimization_barrier((rows_here[0][0], token_ids))
 
     shard_rows = embed_table.shape[0]
+    last_base = VOCAB - (devices - 1) * shard_rows
+    places_last = last_base >= 0 and local_rows * cores == seq_slots
     all_ids = gather_small(token_ids).reshape(-1)
-    last_base = VOCAB - (devices - 1) * shard_rows
+    if places_last:
+        place_rows = from_last(
+            [
+                embed_table[last_base + at * local_rows : last_base + (at + 1) * local_rows].astype(BF)
+                for at in range(cores)
+            ]
+        )
+        hops = tree()
+        place_rows = spread_from(place_rows, hops[0])
+        all_ids, place_rows = lax.optimization_barrier((all_ids, place_rows))
     by_device = all_ids.reshape(devices, local_rows)
     holder = by_device // shard_rows
     earlier = jnp.arange(local_rows)[None, :] < jnp.arange(local_rows)[:, None]
@@ -643,10 +722,12 @@
     def exchange(filled):
         return lax.all_to_all(filled, EVERY, split_axis=0, concat_axis=0, tiled=True)
 
-    def fetch_rows(round_no):
-        row_of_slot, slot_of_token = plan(round_no)
-        filled = jnp.take(embed_table, jnp.maximum(row_of_slot - 1, 0), axis=0).astype(BF)
-        return product_tn(slot_of_token, exchange(filled))
+    def rows_to_send(round_no):
+        rows = jnp.maximum(plan(round_no)[0] - 1, 0)
+        return jnp.take(embed_table, rows, axis=0).astype(BF)
+
+    def rows_reached(round_no, reached):
+        return product_tn(plan(round_no)[1], reached)
 
     def return_rows(round_no, grads):
         row_of_slot, slot_of_token = plan(round_no)
@@ -669,28 +750,25 @@
         rows = rows + lookup(VOCAB + jnp.arange(rows.shape[0]) % seq_slots)
         return lax.psum_scatter(rows, ("x", "core"), scatter_dimension=0, tiled=True).astype(F32)
 
-    places_last = last_base >= 0 and local_rows * cores == seq_slots
+    fetched = [[fetch(rows) for rows in of_layer] for of_layer in rows_here]
     if places_last:
+        place_rows = spread_from(place_rows, hops[1])
+        filled, place_rows = lax.optimization_barrier((rows_to_send(0), place_rows))
+        for step in hops[2:]:
+            place_rows = spread_from(place_rows, step)
+        reached, fetched[0][0] = lax.optimization_barrier((exchange(filled), fetched[0][0]))
         token_rows = lax.fori_loop(
-            1, rounds, lambda at, rows: rows + fetch_rows(at), fetch_rows(0)
-        )
-        place_rows = from_last(
-            [
-                embed_table[last_base + at * local_rows : last_base + (at + 1) * local_rows].astype(BF)
-                for at in range(cores)
-            ]
+            1,
+            rounds,
+            lambda at, rows: rows + rows_reached(at, exchange(rows_to_send(at))),
+            rows_reached(0, reached),
         )
         embedded = token_rows + place_rows.astype(F32)
     else:
         embedded = full_rows()
 
     def by_rank(base_at, width):
-        return jnp.concatenate(
-            [
-                lax.dynamic_slice_in_dim(vectors, base_at + (at * cores + core) * width, width)
-                for at in range(ranks)
-            ]
-        )
+        return lax.dynamic_slice_in_dim(vectors, base_at + (rank * cores + core) * width, width)
 
     head_width = D // (ranks * cores)
     feed_width = FF // (ranks * cores)
@@ -711,7 +789,7 @@
     kept_all = []
     weights_all = []
     for layer_no in range(layers):
-        weights = fetch_layer(in_proj, out_proj, up_proj, down_proj, layer_no)
+        weights = named_layer(*fetched[layer_no], row_blocks, feed_blocks)
         residual, kept_values = layer_forward(
             residual, weights, pieces_of(layer_no), keys_live
         )
@@ -753,59 +831,150 @@
         starts[name] = begin_at
         begin_at = begin_at + layers * counts[name]
     block_count = begin_at
+    dealt = {
+        name: owners if counts[name] % owners == 0 and starts[name] % owners == 0 else None
+        for name in counts
+    }
     ready = {}
+    ready_slots = {}
     summed = {}
-
-    def send_ready(offload):
+    sends = []
+
+    def slot_parts(slot):
+        if slot in ready_slots:
+            array, at = ready_slots[slot]
+            return array[:, :, at]
+        numbers = range(slot * owners, (slot + 1) * owners)
+        members = []
+        at = 0
+        while at < owners:
+            number = numbers[at]
+            if number >= block_count:
+                members.append(jnp.zeros((owners - at, 1, block_size, block_size), BF))
+                break
+            array, offset = ready[number]
+            span = 1
+            while at + span < owners and ready.get(number + span, (None, 0))[0] is array:
+                span = span + 1
+            members.append(array[offset : offset + span])
+            at = at + span
+        return jnp.concatenate(members, axis=0)
+
+    def once_there(slots, values):
+        sums = jnp.stack([summed[slot] for slot in slots])
+        values, sums = lax.optimization_barrier((values, sums))
+        for at, slot in enumerate(slots):
+            summed[slot] = sums[at]
+        return values
+
+    def sum_ready(next_in):
         taken = []
         for slot in range(slot_count):
             numbers = range(slot * owners, min((slot + 1) * owners, block_count))
-            if slot not in summed and all(number in ready for number in numbers):
+            if slot not in summed and (
+                slot in ready_slots or all(number in ready for number in numbers)
+            ):
                 taken.append(slot)
-        if offload and len(taken) > 0:
-            array = ready[taken[0] * owners][0]
-            array = array.reshape((len(taken), owners * ranks) + array.shape[2:])
-            array = array.transpose(1, 0, 2, 3).reshape((-1,) + array.shape[2:])
-            arrived = lax.psum_scatter(array, GROUP, scatter_dimension=0, tiled=True)
-            for at, slot in enumerate(taken):
-                summed[slot] = arrived[at]
-            return
-        for slot in taken:
-            numbers = range(slot * owners, (slot + 1) * owners)
-            members = []
-            at = 0
-            while at < owners:
-                number = numbers[at]
-                if number >= block_count:
-                    members.append(jnp.zeros((owners - at, ranks, block_size, block_size), BF))
-                    break
-                array, offset = ready[number]
-                span = 1
-                while at + span < owners and ready.get(number + span, (None, 0))[0] is array:
-                    span = span + 1
-                members.append(array[offset : offset + span])
-                at = at + span
-            joined = jnp.concatenate(members, axis=0) if len(members) > 1 else members[0]
-            summed[slot] = scatter_sum(joined, routes()[slot % 4])
-
-    early = {("down", layers - 1), ("up", layers - 1), ("down", layers - 2)}
+        if not taken:
+            return next_in
+        outgoing = jnp.concatenate([slot_parts(slot) for slot in taken], axis=1)
+        next_in, outgoing = lax.optimization_barrier((next_in, outgoing))
+        if len(sends) < 2:
+            arrived = lax.psum_scatter(
+                outgoing.reshape((-1,) + outgoing.shape[2:]), "dp", scatter_dimension=0, tiled=True
+            )
+        else:
+            arrived = once_there(sends[-1], scatter_sum(outgoing))
+        for at, slot in enumerate(taken):
+            summed[slot] = arrived[at]
+        sends.append(taken)
+        return next_in
+
+    flat_stats = (slot_count, block_size, block_size)
+    left_root = root_left.reshape(flat_stats)
+    right_root = root_right.reshape(flat_stats)
+    returned = [None] * slot_count
+
+    def send_back(taken, next_in=None):
+        some = jnp.stack([summed[slot] for slot in taken])
+
+        def roots(array):
+            return jnp.stack([array[slot] for slot in taken])
+
+        direction = jnp.einsum(
+            "sij,sjk->sik",
+            jnp.einsum(
+                "sij,sjk->sik", roots(left_root), some.astype(F32), precision=lax.Precision.HIGH
+            ),
+            roots(right_root),
+            precision=lax.Precision.HIGH,
+        )
+        both = jnp.stack([some, direction.astype(BF)])
+        outgoing = both.reshape(2, len(taken), owners, rows_per, block_size)
+        back = lax.all_to_all(
+            outgoing.transpose(2, 0, 1, 3, 4), "dp", split_axis=0, concat_axis=0, tiled=True
+        )
+        if next_in is not None:
+            next_in, back = lax.optimization_barrier((next_in, back))
+        for at, slot in enumerate(taken):
+            returned[slot] = back[:, :, at]
+        return next_in
+
+    def emit_of(layer_no):
+        def emit(name, value, next_in):
+            next_in, value = lax.optimization_barrier((next_in, value))
+            first = starts[name] + layer_no * counts[name]
+            if dealt[name]:
+                for at in range(counts[name] // owners):
+                    ready_slots[first // owners + at] = (value, at)
+            else:
+                for at in range(counts[name]):
+                    ready[first + at] = (value, at)
+            if name == "down" and layer_no == 0 and sends:
+                next_in = once_there(sends[0], next_in)
+            if name == "up" or (name == "in" and layer_no == 0):
+                next_in = sum_ready(next_in)
+            if name == "out" and layer_no == 0 and len(sends) > 1:
+                next_in = send_back(sends[0], next_in)
+                if layers in early_vectors:
+                    next_in, early_vectors[layers] = lax.optimization_barrier(
+                        (next_in, early_vectors[layers])
+                    )
+            return next_in
+
+        return emit
+
+    def placed(piece, width):
+        row = jnp.zeros((ranks * cores * width,), F32)
+        return lax.dynamic_update_slice(row, piece, ((rank * cores + core) * width,))
+
     bias_parts = [None] * layers
+    early_vectors = {}
+
+    def vector_rows_of(layer_no):
+        grad_items = bias_parts[layer_no]
+        return [
+            placed(grad_items[0], head_width),
+            placed(grad_items[1], head_width),
+            placed(grad_items[2], feed_width),
+        ] + list(grad_items[3:])
+
     for layer_no in reversed(range(layers)):
-        for name, value in layer_backward(
+        if layer_no == 0:
+            rows = []
+            for done_no in range(1, layers):
+                rows = rows + vector_rows_of(done_no)
+            others = jnp.stack([d_head_bias, leader * d_scale, bce_part, count_part])
+            early_vectors[layers] = sum_over_all(jnp.concatenate(rows + [d_head_weight, others]))
+        upstream, bias_parts[layer_no] = layer_backward(
             upstream,
             kept_all[layer_no],
             weights_all[layer_no],
             pieces_of(layer_no),
             keys_live,
-        ):
-            if name == "rest":
-                upstream, bias_parts[layer_no] = value
-                continue
-            first = starts[name] + layer_no * counts[name]
-            for at in range(counts[name]):
-                ready[first + at] = (value, at)
-            whole_slots = first % owners == 0 and counts[name] % owners == 0
-            send_ready(whole_slots and (name, layer_no) in early)
+            dealt,
+            emit_of(layer_no),
+        )
 
     d_embed, d_gain_embed, d_shift_embed = norm_back(embedded, gain_embed, shift_embed, upstream)
     d_embed = d_embed.astype(BF)
@@ -827,69 +996,27 @@
         ).astype(BF)
         table_shard = product(picker, d_rows)
 
-    def placed(piece, base_at, width):
-        row = jnp.zeros((ranks * cores * width,), F32)
-        for at in range(ranks):
-            row = lax.dynamic_update_slice(
-                row, piece[at * width : (at + 1) * width], ((at * cores + core) * width,)
-            )
-        return row
-
-    vector_rows = []
-    for layer_no in range(layers):
-        grad_items = bias_parts[layer_no]
-        vector_rows.append(placed(grad_items[0], 0, head_width))
-        vector_rows.append(placed(grad_items[1], 0, head_width))
-        vector_rows.append(placed(grad_items[2], 0, feed_width))
-        vector_rows.extend(grad_items[3:])
-    vector_grad = jnp.concatenate(
-        vector_rows
-        + [d_gain_embed, d_shift_embed, d_head_weight, jnp.stack([d_head_bias, leader * d_scale])]
-    )
-    vector_total = sum_over_all(jnp.concatenate([vector_grad, jnp.stack([bce_part, count_part])]))
-    offloaded = {
-        starts[name] // owners + (layer_no * counts[name]) // owners + at
-        for name, layer_no in early
-        for at in range(counts[name] // owners)
-    }
-    order = [slot for slot in summed if slot not in offloaded] + [
-        slot for slot in summed if slot in offloaded
-    ]
-    summed[order[0]], vector_total = lax.optimization_barrier((summed[order[0]], vector_total))
-    bce_total, count_total = vector_total[-2], vector_total[-1]
-    vector_total = vector_total[:-2]
+    for at, taken in enumerate(sends):
+        if returned[taken[0]] is None:
+            last = summed[sends[-1][0]] if at < len(sends) - 1 else None
+            last = send_back(taken, last)
+            if last is not None:
+                summed[sends[-1][0]] = last
 
     blocks_low = jnp.stack([summed[slot] for slot in range(slot_count)])
     blocks = blocks_low.astype(F32)
     squares = jnp.sum(table_shard * table_shard) + jnp.sum(blocks * blocks)
-    square_total = sum_over_all(squares.reshape(1, 1))[0, 0]
+    late = sum_over_all(
+        jnp.concatenate(vector_rows_of(0) + [d_gain_embed, d_shift_embed, squares.reshape(1)])
+    )
+    early = early_vectors[layers]
+    vector_total = jnp.concatenate(
+        [late[:per_layer], early[: tail_at - per_layer], late[per_layer:-1], early[tail_at - per_layer : -2]]
+    )
+    bce_total, count_total, square_total = early[-2], early[-1], late[-1]
     grad_norm = jnp.sqrt(square_total + jnp.sum(vector_total * vector_total))
     factor = CLIP_NORM / jnp.maximum(grad_norm, CLIP_NORM)
 
-    left_root = root_left.reshape(blocks.shape)
-    right_root = root_right.reshape(blocks.shape)
-    returned = [None] * slot_count
-    per_send = max(1, slot_count // 3)
-    for begin_at in range(0, slot_count, per_send):
-        taken = sorted(order[begin_at : begin_at + per_send])
-        some = jnp.stack([summed[slot] for slot in taken])
-
-        def roots(array):
-            return jnp.stack([array[slot] for slot in taken])
-
-        direction = jnp.einsum(
-            "sij,sjk->sik",
-            jnp.einsum(
-                "sij,sjk->sik", roots(left_root), some.astype(F32), precision=lax.Precision.HIGH
-            ),
-            roots(right_root),
-            precision=lax.Precision.HIGH,
-        )
-        both = jnp.stack([some, direction.astype(BF)])
-        outgoing = both.reshape(2, len(taken), owners, rows_per, block_size).transpose(2, 0, 1, 3, 4)
-        back = lax.all_to_all(outgoing, "dp", split_axis=0, concat_axis=0, tiled=True)
-        for at, slot in enumerate(taken):
-            returned[slot] = back[:, :, at]
     mine_back = (
         jnp.stack(returned)
         .transpose(2, 0, 1, 3, 4)

time: 1020 us -> 886 us (0.87)
  waiting for transfers between devices: 471 us -> 305 us
  local copies, waits for them, and re-layouts: 91.3 us -> 130 us
    all_gather x2 -> x4, waiting for transfers between devices: 141 us -> 12.4 us  [fetch(): return lax.all_gather(pieces, 'dp', axis=0, tiled=False)[:, None]]
    ppermute x4, waiting for transfers between devices: 64.1 us -> 0.01 us  [spread_from(): found = lax.ppermute(value, GROUP, step)]
    unnamed x364 -> x565, local copies, waits for them, and re-layouts: 21.4 us -> 74.8 us
    ppermute x60 -> x71, waiting for transfers between devices: 193 us -> 229 us  [from_peer(): return lax.ppermute(values, axis, [(at, at ^ mask) for at in range(size)])]
    all_to_all x2, starting transfers between devices: 15.9 us -> 35.5 us  [exchange(): lax.all_to_all(filled, EVERY, split_axis=0, concat_axis=0, tiled=True)]
    all_to_all x2, waiting for transfers between devices: 57.7 us -> 42.2 us  [exchange(): lax.all_to_all(filled, EVERY, split_axis=0, concat_axis=0, tiled=True)]
    ppermute x60 -> x71, starting transfers between devices: 86.2 us -> 72.1 us  [from_peer(): return lax.ppermute(values, axis, [(at, at ^ mask) for at in range(size)])]
    all_to_all x3, starting transfers between devices: 27.8 us -> 14.5 us  [send_back(): lax.all_to_all(outgoing.transpose(2, 0, 1, 3, 4), 'dp', split_axis=0, con...]
  transfers between devices with their start and end apart: 78 -> 90, of which waited for: 40 -> 55; matrix products, arithmetic and copies ran while one was open for 17% -> 19% of each run, Pallas kernels for 11% -> 13%
where the time goes in v2:
time: 886 us; the launch traced here: 875 us
  waiting for transfers between devices  305 us (34%)
  Pallas kernels  140 us (16%)
  starting transfers between devices  134 us (15%)
  local copies, waits for them, and re-layouts  130 us (15%)
  other arithmetic  105 us (12%)
  matrix products  32.4 us (4%)
  between operations  27.4 us (3%)
    ppermute x71, waiting for transfers between devices, from_peer(): return lax.ppermute(values, axis, [(at, at ^ mask) for at in range(size)])  229 us
    pallas_call x32, Pallas kernels, rows_product(): pl.pallas_call(kernel, grid=(steps,), in_specs=[whole(left.shape), pl.Blo...  83.9 us
    unnamed x565, local copies, waits for them, and re-layouts  74.8 us
    ppermute x71, starting transfers between devices, from_peer(): return lax.ppermute(values, axis, [(at, at ^ mask) for at in range(size)])  72.1 us
    all_to_all x2, waiting for transfers between devices, exchange(): lax.all_to_all(filled, EVERY, split_axis=0, concat_axis=0, tiled=True)  42.2 us
    all_to_all x2, starting transfers between devices, exchange(): lax.all_to_all(filled, EVERY, split_axis=0, concat_axis=0, tiled=True)  35.5 us
    pallas_call x8, Pallas kernels, attend(): pl.pallas_call(body, grid=(seqs, pairs), in_specs=specs, out_specs=out_sp...  34 us
    pallas_call x8, Pallas kernels, block_grads(): pl.pallas_call(kernel, grid=(high,), in_specs=[whole(member.shape) for me...  22.4 us
  transfers between devices with their start and end apart: 90, of which 55 were waited for; matrix products, arithmetic and copies ran while one was open for 19% of the time, Pallas kernels for 13%

profile of v2, /device:TPU:0, one launch (start us, length us, event | category | flops | bytes accessed | tf_op | source)
XLA Modules:
  0.0 875.2 jit_solution(1614044282531379163)
XLA Ops:
  31.2 6.7 gather_fusion.1
  42.3 31.8 %all-to-all-start.2 = ((bf16[32,24,1024]{2,1,0:T(8,128)(2,1)}), bf16[32,24,1024]{2,1,0:T(8,128)(2,1)}, u32[]{:S(2)}, u32[]{:S(2)}) async-start(bf16[32,24,1024]{2,1,0:T(8,128)(2,1)} %bitcast.325), calls=%async_computation.2 | async-start | bytes 3145728 | tf_op jit(solution)/shard_map/all_to_all | solution.py:723
  86.3 42.2 %all-to-all-done.2 = bf16[32,24,1024]{2,1,0:T(8,128)(2,1)} async-done(((bf16[32,24,1024]{2,1,0:T(8,128)(2,1)}), bf16[32,24,1024]{2,1,0:T(8,128)(2,1)}, u32[]{:S(2)}, u32[]{:S(2)}) %all-to-all-start.2) | async-done | bytes 1572896 | tf_op jit(solution)/shard_map/all_to_all | solution.py:723
  143.4 5.1 collective-permute-done.9
  165.7 12.4 %collective-permute-done.13 = bf16[256,1024]{1,0:T(8,128)(2,1)S(1)} collective-permute-done((bf16[256,1024]{1,0:T(8,128)(2,1)S(1)}, bf16[256,1024]{1,0:T(8,128)(2,1)S(1)}, u32[]{:S(2)}, u32[]{:S(2)}) %collective-permute-start.13) | collective-permute-done | bytes 524320 | tf_op jit(solution)/shard_map/ppermute | solution.py:77
  183.9 4.1 shard_map.363
  189.4 5.9 collective-permute-done.15
  197.5 4.1 shard_map.364
  203.0 4.0 shard_map.365
  218.8 12.4 %collective-permute-done.19 = bf16[256,1024]{1,0:T(8,128)(2,1)S(1)} collective-permute-done((bf16[256,1024]{1,0:T(8,128)(2,1)S(1)}, bf16[256,1024]{1,0:T(8,128)(2,1)S(1)}, u32[]{:S(2)}, u32[]{:S(2)}) %collective-permute-start.19) | collective-permute-done | bytes 524320 | tf_op jit(solution)/shard_map/ppermute | solution.py:77
  243.5 4.9 collective-permute-done.21
  262.9 12.4 %collective-permute-done.25 = bf16[256,1024]{1,0:T(8,128)(2,1)S(1)} collective-permute-done((bf16[256,1024]{1,0:T(8,128)(2,1)S(1)}, bf16[256,1024]{1,0:T(8,128)(2,1)S(1)}, u32[]{:S(2)}, u32[]{:S(2)}) %collective-permute-start.25) | collective-permute-done | bytes 524320 | tf_op jit(solution)/shard_map/ppermute | solution.py:77
  282.3 12.3 %all-gather.10.cloned.1.call-done = bf16[8,8,4,32,256]{4,3,2,1,0:T(8,128)(2,1)} async-done(((bf16[1,8,4,32,256]{4,3,2,1,0:T(8,128)(2,1)}), bf16[8,8,4,32,256]{4,3,2,1,0:T(8,128)(2,1)}) %all-gather.10.cloned.1.call-update) | async-done | bytes 4194320 | tf_op jit(solution)/shard_map/all_gather | solution.py:188
  303.1 4.1 shard_map.374
  308.6 4.0 shard_map.375
  325.9 6.7 collective-permute-done.31
  379.6 8.5 collective-permute-done.38
  393.9 4.0 shard_map.379
  400.9 3.9 shard_map.380
  404.9 3.9 shard_map.381
  421.2 10.5 %collective-permute-done.42 = bf16[256,1024]{1,0:T(8,128)(2,1)} collective-permute-done((bf16[256,1024]{1,0:T(8,128)(2,1)}, bf16[256,1024]{1,0:T(8,128)(2,1)}, u32[]{:S(2)}, u32[]{:S(2)}) %collective-permute-start.42) | collective-permute-done | bytes 524320 | tf_op jit(solution)/shard_map/ppermute | solution.py:77
  438.3 5.3 shard_map.384.refs_2_.refs_0_
  443.7 5.9 collective-permute-done.44
  452.0 5.1 shard_map.386.refs_0_.refs_3_
  484.4 4.2 shard_map.391.refs_2_.refs_0_
  488.6 5.2 collective-permute-done.50
  504.0 4.5 shard_map.393
  513.5 3.9 shard_map.394
  521.1 3.9 shard_map.395
  527.9 4.5 shard_map.396
  537.4 5.3 copy.150
  552.5 5.1 shard_map.398.refs_2_.refs_0_
  558.6 5.2 collective-permute-done.56
  563.8 4.4 all-to-all-start.3
  579.9 5.1 shard_map.400.refs_0_.refs_3_
  594.1 11.4 %collective-permute-done.62 = f32[13316]{0:T(1024)S(1)} collective-permute-done((f32[13316]{0:T(1024)S(1)}, f32[13316]{0:T(1024)S(1)}, u32[]{:S(2)}, u32[]{:S(2)}) %collective-permute-start.62) | collective-permute-done | bytes 53296 | tf_op jit(solution)/shard_map/ppermute | solution.py:77
  605.5 4.8 collective-permute-start.63
  657.6 40.3 %collective-permute-done.71 = bf16[2,2,3,256,256]{4,3,2,1,0:T(8,128)(2,1)} collective-permute-done((bf16[2,2,3,256,256]{4,3,2,1,0:T(8,128)(2,1)}, bf16[2,2,3,256,256]{4,3,2,1,0:T(8,128)(2,1)}, u32[]{:S(2)}, u32[]{:S(2)}) %collective-permute-start.71) | collective-permute-done | bytes 1572896 | tf_op jit(solution)/shard_map/ppermute | solution.py:77
  702.2 16.1 %collective-permute-done.72 = bf16[2,3,256,256]{3,2,1,0:T(8,128)(2,1)S(1)} collective-permute-done((bf16[2,3,256,256]{3,2,1,0:T(8,128)(2,1)S(1)}, bf16[2,3,256,256]{3,2,1,0:T(8,128)(2,1)S(1)}, u32[]{:S(2)}, u32[]{:S(2)}) %collective-permute-start.72) | collective-permute-done | bytes 786464 | tf_op jit(solution)/shard_map/ppermute | solution.py:77
  721.3 14.4 %collective-permute-done.73 = bf16[3,256,256]{2,1,0:T(8,128)(2,1)S(1)} collective-permute-done((bf16[3,256,256]{2,1,0:T(8,128)(2,1)S(1)}, bf16[3,256,256]{2,1,0:T(8,128)(2,1)S(1)}, u32[]{:S(2)}, u32[]{:S(2)}) %collective-permute-start.73) | collective-permute-done | bytes 393248 | tf_op jit(solution)/shard_map/ppermute | solution.py:77
  736.5 5.1 fusion.14
  747.1 5.0 all-to-all-start.5
  762.5 21.3 %all-to-all-done.5 = bf16[8,2,5,32,256]{4,3,1,2,0:T(8,128)(2,1)} async-done(((bf16[8,2,5,32,256]{4,3,1,2,0:T(8,128)(2,1)}), bf16[8,2,5,32,256]{4,3,1,2,0:T(8,128)(2,1)}, u32[]{:S(2)}, u32[]{:S(2)}) %all-to-all-start.5) | async-done | bytes 1310752 | tf_op jit(solution)/shard_map/all_to_all | solution.py:914
  801.1 17.2 %collective-permute-start.77 = (f32[14337]{0:T(1024)S(1)}, f32[14337]{0:T(1024)S(1)}, u32[]{:S(2)}, u32[]{:S(2)}) collective-permute-start(f32[14337]{0:T(1024)S(1)} %add.1032), channel_id=1, source_target_pairs={{0,8},{4,12},{8,0},{12,4},{16,24},{20,28},{24,16},{28,20},{1,9},{5... | collective-permute-start | bytes 172052 | tf_op jit(solution)/shard_map/ppermute | solution.py:77
  824.9 5.0 all-to-all-start.6
  833.3 4.3 fusion.13
  837.7 4.5 fusion.12
  843.3 5.7 multiply_subtract_fusion
  (1031 shorter events, 420.7 us)
Async XLA Ops:
  7.2 79.1 %all-gather.12.cloned.1.call-start = ((), (), s32[]{:S(2)}) async-start(), calls=%async_computation.14 | async-start | bytes 2359296 | tf_op jit(solution)/shard_map/all_gather | solution.py:188
  16.9 10.0 %collective-permute-start.4 = (bf16[256,1024]{1,0:T(8,128)(2,1)S(1)}, bf16[256,1024]{1,0:T(8,128)(2,1)}, u32[]{:S(2)}, u32[]{:S(2)}) collective-permute-start(bf16[256,1024]{1,0:T(8,128)(2,1)S(1)} %slice_select_fusion), channel_id=1, source_target_pairs={{30,14},{31,15}} | collective-permute-start | bytes 1572872 | tf_op jit(solution)/shard_map/ppermute | solution.py:145
  26.9 13.9 %collective-permute-start.5 = (bf16[256,1024]{1,0:T(8,128)(2,1)S(1)}, bf16[256,1024]{1,0:T(8,128)(2,1)S(1)}, u32[]{:S(2)}, u32[]{:S(2)}) collective-permute-start(bf16[256,1024]{1,0:T(8,128)(2,1)S(1)} %broadcast_select_fusion), channel_id=1, source_target_pairs={{30,22},{14,6},{31,23},{15,7}} | collective-permute-start | bytes 1572872 | tf_op jit(solution)/shard_map/ppermute | solution.py:145
  42.3 86.1 %all-to-all-start.2 = ((bf16[32,24,1024]{2,1,0:T(8,128)(2,1)}), bf16[32,24,1024]{2,1,0:T(8,128)(2,1)}, u32[]{:S(2)}, u32[]{:S(2)}) async-start(bf16[32,24,1024]{2,1,0:T(8,128)(2,1)} %bitcast.325), calls=%async_computation.2 | async-start | bytes 3145728 | tf_op jit(solution)/shard_map/all_to_all | solution.py:723
  74.1 109.9 %all-gather.6.cloned.1.call-start = ((), (), s32[]{:S(2)}) async-start(), calls=%async_computation.9 | async-start | bytes 4718592 | tf_op jit(solution)/shard_map/all_gather | solution.py:188
  74.1 5.4 collective-permute-start.6
  78.8 158.2 %all-gather.8.cloned.1.call-start = ((), (), s32[]{:S(2)}) async-start(), calls=%async_computation.10 | async-start | bytes 2359296 | tf_op jit(solution)/shard_map/all_gather | solution.py:188
  81.0 49.5 %collective-permute-start.7 = (bf16[256,1024]{1,0:T(8,128)(2,1)}, bf16[256,1024]{1,0:T(8,128)(2,1)}, u32[]{:S(2)}, u32[]{:S(2)}) collective-permute-start(bf16[256,1024]{1,0:T(8,128)(2,1)} %broadcast_select_fusion.1), channel_id=1, source_target_pairs={{30,28},{14,12},{22,20},{6,4},{26,24},{10,8},{18,16},{2,0},{31,29}... | collective-permute-start | bytes 1572872 | tf_op jit(solution)/shard_map/ppermute | solution.py:145
  134.2 14.4 %collective-permute-start.9 = (bf16[256,1024]{1,0:T(8,128)(2,1)S(1)}, bf16[256,1024]{1,0:T(8,128)(2,1)}, u32[]{:S(2)}, u32[]{:S(2)}) collective-permute-start(bf16[256,1024]{1,0:T(8,128)(2,1)S(1)} %fusion.67), channel_id=1, source_target_pairs={{0,2},{2,0},{1,3},{3,1},{4,6},{6,4},{5,7},{7,5},{8,10},{10,8},{9,1... | collective-permute-start | bytes 1572872 | tf_op jit(solution)/shard_map/ppermute | solution.py:77
  160.1 134.6 %all-gather.10.cloned.1.call-start = ((), (), s32[]{:S(2)}) async-start(), calls=%async_computation.11 | async-start | bytes 4718592 | tf_op jit(solution)/shard_map/all_gather | solution.py:188
  163.9 14.2 %collective-permute-start.13 = (bf16[256,1024]{1,0:T(8,128)(2,1)S(1)}, bf16[256,1024]{1,0:T(8,128)(2,1)S(1)}, u32[]{:S(2)}, u32[]{:S(2)}) collective-permute-start(bf16[256,1024]{1,0:T(8,128)(2,1)S(1)} %fusion.50), channel_id=1, source_target_pairs={{0,2},{2,0},{1,3},{3,1},{4,6},{6,4},{5,7},{7,5},{8,10},{10,8},{9,1... | collective-permute-start | bytes 1572872 | tf_op jit(solution)/shard_map/ppermute | solution.py:77
  180.7 14.7 %collective-permute-start.15 = (bf16[256,1024]{1,0:T(8,128)(2,1)}, bf16[256,1024]{1,0:T(8,128)(2,1)}, u32[]{:S(2)}, u32[]{:S(2)}) collective-permute-start(bf16[256,1024]{1,0:T(8,128)(2,1)} %fusion.68), channel_id=1, source_target_pairs={{0,2},{2,0},{1,3},{3,1},{4,6},{6,4},{5,7},{7,5},{8,10},{10,8},{9,1... | collective-permute-start | bytes 1572872 | tf_op jit(solution)/shard_map/ppermute | solution.py:77
  210.2 307.2 %reduce-scatter.3.cloned.1.call-start = ((), (), s32[]{:S(2)}) async-start(), calls=%async_computation.12 | async-start | bytes 4718592 | tf_op jit(solution)/shard_map/reduce_scatter | solution.py:883
  217.0 14.2 %collective-permute-start.19 = (bf16[256,1024]{1,0:T(8,128)(2,1)S(1)}, bf16[256,1024]{1,0:T(8,128)(2,1)S(1)}, u32[]{:S(2)}, u32[]{:S(2)}) collective-permute-start(bf16[256,1024]{1,0:T(8,128)(2,1)S(1)} %fusion.46), channel_id=1, source_target_pairs={{0,2},{2,0},{1,3},{3,1},{4,6},{6,4},{5,7},{7,5},{8,10},{10,8},{9,1... | collective-permute-start | bytes 1572872 | tf_op jit(solution)/shard_map/ppermute | solution.py:77
  233.7 14.7 %collective-permute-start.21 = (bf16[256,1024]{1,0:T(8,128)(2,1)}, bf16[256,1024]{1,0:T(8,128)(2,1)}, u32[]{:S(2)}, u32[]{:S(2)}) collective-permute-start(bf16[256,1024]{1,0:T(8,128)(2,1)} %fusion.69), channel_id=1, source_target_pairs={{0,2},{2,0},{1,3},{3,1},{4,6},{6,4},{5,7},{7,5},{8,10},{10,8},{9,1... | collective-permute-start | bytes 1572872 | tf_op jit(solution)/shard_map/ppermute | solution.py:77
  261.2 14.2 %collective-permute-start.25 = (bf16[256,1024]{1,0:T(8,128)(2,1)S(1)}, bf16[256,1024]{1,0:T(8,128)(2,1)S(1)}, u32[]{:S(2)}, u32[]{:S(2)}) collective-permute-start(bf16[256,1024]{1,0:T(8,128)(2,1)S(1)} %fusion.42), channel_id=1, source_target_pairs={{0,2},{2,0},{1,3},{3,1},{4,6},{6,4},{5,7},{7,5},{8,10},{10,8},{9,1... | collective-permute-start | bytes 1572872 | tf_op jit(solution)/shard_map/ppermute | solution.py:77
  278.0 22.9 %collective-permute-start.27 = (bf16[256,1024]{1,0:T(8,128)(2,1)}, bf16[256,1024]{1,0:T(8,128)(2,1)}, u32[]{:S(2)}, u32[]{:S(2)}) collective-permute-start(bf16[256,1024]{1,0:T(8,128)(2,1)} %fusion.70), channel_id=1, source_target_pairs={{0,2},{2,0},{1,3},{3,1},{4,6},{6,4},{5,7},{7,5},{8,10},{10,8},{9,1... | collective-permute-start | bytes 1572872 | tf_op jit(solution)/shard_map/ppermute | solution.py:77
  318.6 14.0 %collective-permute-start.31 = (bf16[256,1024]{1,0:T(8,128)(2,1)S(1)}, bf16[256,1024]{1,0:T(8,128)(2,1)S(1)}, u32[]{:S(2)}, u32[]{:S(2)}) collective-permute-start(bf16[256,1024]{1,0:T(8,128)(2,1)S(1)} %fusion.38), channel_id=1, source_target_pairs={{0,2},{2,0},{1,3},{3,1},{4,6},{6,4},{5,7},{7,5},{8,10},{10,8},{9,1... | collective-permute-start | bytes 1572872 | tf_op jit(solution)/shard_map/ppermute | solution.py:77
  373.7 14.3 %collective-permute-start.38 = (bf16[256,1024]{1,0:T(8,128)(2,1)S(1)}, bf16[256,1024]{1,0:T(8,128)(2,1)S(1)}, u32[]{:S(2)}, u32[]{:S(2)}) collective-permute-start(bf16[256,1024]{1,0:T(8,128)(2,1)S(1)} %get-tuple-element.497), channel_id=1, source_target_pairs={{0,2},{2,0},{1,3},{3,1},{4,6},{6,4},{5,7},{7,5},{8,10},{10,8},{9,1... | collective-permute-start | bytes 1572872 | tf_op jit(solution)/shard_map/ppermute | solution.py:77
  417.2 14.5 %collective-permute-start.42 = (bf16[256,1024]{1,0:T(8,128)(2,1)}, bf16[256,1024]{1,0:T(8,128)(2,1)}, u32[]{:S(2)}, u32[]{:S(2)}) collective-permute-start(bf16[256,1024]{1,0:T(8,128)(2,1)} %fusion.34), channel_id=1, source_target_pairs={{0,2},{2,0},{1,3},{3,1},{4,6},{6,4},{5,7},{7,5},{8,10},{10,8},{9,1... | collective-permute-start | bytes 1572872 | tf_op jit(solution)/shard_map/ppermute | solution.py:77
  421.1 320.5 %reduce-scatter.5.cloned.1.call-start = ((), (), s32[]{:S(2)}) async-start(), calls=%async_computation.13 | async-start | bytes 5898240 | tf_op jit(solution)/shard_map/reduce_scatter | solution.py:883
  435.2 14.3 %collective-permute-start.44 = (bf16[256,1024]{1,0:T(8,128)(2,1)S(1)}, bf16[256,1024]{1,0:T(8,128)(2,1)S(1)}, u32[]{:S(2)}, u32[]{:S(2)}) collective-permute-start(bf16[256,1024]{1,0:T(8,128)(2,1)S(1)} %get-tuple-element.499), channel_id=1, source_target_pairs={{0,2},{2,0},{1,3},{3,1},{4,6},{6,4},{5,7},{7,5},{8,10},{10,8},{9,1... | collective-permute-start | bytes 1572872 | tf_op jit(solution)/shard_map/ppermute | solution.py:77
  461.3 14.0 %collective-permute-start.48 = (bf16[256,1024]{1,0:T(8,128)(2,1)S(1)}, bf16[256,1024]{1,0:T(8,128)(2,1)S(1)}, u32[]{:S(2)}, u32[]{:S(2)}) collective-permute-start(bf16[256,1024]{1,0:T(8,128)(2,1)S(1)} %fusion.31), channel_id=1, source_target_pairs={{0,2},{2,0},{1,3},{3,1},{4,6},{6,4},{5,7},{7,5},{8,10},{10,8},{9,1... | collective-permute-start | bytes 1572872 | tf_op jit(solution)/shard_map/ppermute | solution.py:77
  479.1 14.7 %collective-permute-start.50 = (bf16[256,1024]{1,0:T(8,128)(2,1)}, bf16[256,1024]{1,0:T(8,128)(2,1)}, u32[]{:S(2)}, u32[]{:S(2)}) collective-permute-start(bf16[256,1024]{1,0:T(8,128)(2,1)} %get-tuple-element.489), channel_id=1, source_target_pairs={{0,2},{2,0},{1,3},{3,1},{4,6},{6,4},{5,7},{7,5},{8,10},{10,8},{9,1... | collective-permute-start | bytes 1572872 | tf_op jit(solution)/shard_map/ppermute | solution.py:77
  493.8 5.3 collective-permute-start.51
  512.0 30.9 %collective-permute-start.54 = (bf16[256,1024]{1,0:T(8,128)(2,1)}, bf16[256,1024]{1,0:T(8,128)(2,1)}, u32[]{:S(2)}, u32[]{:S(2)}) collective-permute-start(bf16[256,1024]{1,0:T(8,128)(2,1)} %fusion.28), channel_id=1, source_target_pairs={{0,2},{2,0},{1,3},{3,1},{4,6},{6,4},{5,7},{7,5},{8,10},{10,8},{9,1... | collective-permute-start | bytes 1572872 | tf_op jit(solution)/shard_map/ppermute | solution.py:77
  534.6 8.2 collective-permute-start.53
  537.1 32.7 %collective-permute-start.59 = (f32[13316]{0:T(1024)S(1)}, f32[13316]{0:T(1024)S(1)}, u32[]{:S(2)}, u32[]{:S(2)}) collective-permute-start(f32[13316]{0:T(1024)S(1)} %concatenate.212), channel_id=1, source_target_pairs={{0,1},{1,0},{2,3},{3,2},{4,5},{5,4},{6,7},{7,6},{8,9},{9,8},{10,11... | collective-permute-start | bytes 159800 | tf_op jit(solution)/shard_map/ppermute | solution.py:77
  549.4 14.4 %collective-permute-start.56 = (bf16[256,1024]{1,0:T(8,128)(2,1)S(1)}, bf16[256,1024]{1,0:T(8,128)(2,1)}, u32[]{:S(2)}, u32[]{:S(2)}) collective-permute-start(bf16[256,1024]{1,0:T(8,128)(2,1)S(1)} %get-tuple-element.491), channel_id=1, source_target_pairs={{0,2},{2,0},{1,3},{3,1},{4,6},{6,4},{5,7},{7,5},{8,10},{10,8},{9,1... | collective-permute-start | bytes 1572872 | tf_op jit(solution)/shard_map/ppermute | solution.py:77
  563.8 13.5 %collective-permute-start.57 = (bf16[256,1024]{1,0:T(8,128)(2,1)}, bf16[256,1024]{1,0:T(8,128)(2,1)}, u32[]{:S(2)}, u32[]{:S(2)}) collective-permute-start(bf16[256,1024]{1,0:T(8,128)(2,1)} %collective-permute-done.56), channel_id=1, source_target_pairs={{0,1},{1,0},{2,3},{3,2},{4,5},{5,4},{6,7},{7,6},{8,9},{9,8},{10,11... | collective-permute-start | bytes 1572872 | tf_op jit(solution)/shard_map/ppermute | solution.py:77
  563.8 58.3 %all-to-all-start.3 = ((bf16[8,2,4,32,256]{4,3,1,2,0:T(8,128)(2,1)}), bf16[8,2,4,32,256]{4,3,1,2,0:T(8,128)(2,1)}, u32[]{:S(2)}, u32[]{:S(2)}) async-start(bf16[8,2,4,32,256]{4,3,1,2,0:T(8,128)(2,1)} %copy_bitcast_fusion.1), calls=%async_computation.4 | async-start | bytes 2097152 | tf_op jit(solution)/shard_map/all_to_all | solution.py:914
  574.3 16.5 %collective-permute-start.61 = (f32[13316]{0:T(1024)S(1)}, f32[13316]{0:T(1024)S(1)}, u32[]{:S(2)}, u32[]{:S(2)}) collective-permute-start(f32[13316]{0:T(1024)S(1)} %add.1002), channel_id=1, source_target_pairs={{0,4},{4,0},{8,12},{12,8},{16,20},{20,16},{24,28},{28,24},{1,5},{5... | collective-permute-start | bytes 159800 | tf_op jit(solution)/shard_map/ppermute | solution.py:77
  589.2 29.1 %collective-permute-start.58 = (bf16[256,1024]{1,0:T(8,128)(2,1)}, bf16[256,1024]{1,0:T(8,128)(2,1)}, u32[]{:S(2)}, u32[]{:S(2)}) collective-permute-start(bf16[256,1024]{1,0:T(8,128)(2,1)} %slice.989), channel_id=1, source_target_pairs={{0,1},{1,0},{2,3},{3,2},{4,5},{5,4},{6,7},{7,6},{8,9},{9,8},{10,11... | collective-permute-start | bytes 1572872 | tf_op jit(solution)/shard_map/ppermute | solution.py:77
  590.8 14.6 %collective-permute-start.62 = (f32[13316]{0:T(1024)S(1)}, f32[13316]{0:T(1024)S(1)}, u32[]{:S(2)}, u32[]{:S(2)}) collective-permute-start(f32[13316]{0:T(1024)S(1)} %add.1003), channel_id=1, source_target_pairs={{0,8},{4,12},{8,0},{12,4},{16,24},{20,28},{24,16},{28,20},{1,9},{5... | collective-permute-start | bytes 159800 | tf_op jit(solution)/shard_map/ppermute | solution.py:77
  605.5 12.1 %collective-permute-start.63 = (f32[13316]{0:T(1024)S(1)}, f32[13316]{0:T(1024)S(1)}, u32[]{:S(2)}, u32[]{:S(2)}) collective-permute-start(f32[13316]{0:T(1024)S(1)} %add.1004), channel_id=1, source_target_pairs={{0,16},{4,20},{8,24},{12,28},{16,0},{20,4},{24,8},{28,12},{1,17},{... | collective-permute-start | bytes 159800 | tf_op jit(solution)/shard_map/ppermute | solution.py:77
  630.5 13.9 %collective-permute-start.65 = (bf16[256,1024]{1,0:T(8,128)(2,1)S(1)}, bf16[256,1024]{1,0:T(8,128)(2,1)S(1)}, u32[]{:S(2)}, u32[]{:S(2)}) collective-permute-start(bf16[256,1024]{1,0:T(8,128)(2,1)S(1)} %copy-done.156), channel_id=1, source_target_pairs={{0,2},{2,0},{1,3},{3,1},{4,6},{6,4},{5,7},{7,5},{8,10},{10,8},{9,1... | collective-permute-start | bytes 1572872 | tf_op jit(solution)/shard_map/ppermute | solution.py:77
  634.5 6.3 collective-permute-start.64
  639.2 58.7 %collective-permute-start.71 = (bf16[2,2,3,256,256]{4,3,2,1,0:T(8,128)(2,1)}, bf16[2,2,3,256,256]{4,3,2,1,0:T(8,128)(2,1)}, u32[]{:S(2)}, u32[]{:S(2)}) collective-permute-start(bf16[2,2,3,256,256]{4,3,2,1,0:T(8,128)(2,1)} %dynamic-slice_bitcast_fusion), channel_id=1, source_target_pairs={{0,4},{4,0},{8,12},{12,8},{16,20},{20,16},{24,28},{28,24},{1,5},{5... | collective-permute-start | bytes 4718600 | tf_op jit(solution)/shard_map/ppermute | solution.py:77
  649.5 87.0 %all-to-all-start.4 = ((bf16[32,24,1024]{2,1,0:T(8,128)(2,1)}), bf16[32,24,1024]{2,1,0:T(8,128)(2,1)}, u32[]{:S(2)}, u32[]{:S(2)}) async-start(bf16[32,24,1024]{2,1,0:T(8,128)(2,1)} %bitcast.326), calls=%async_computation.5 | async-start | bytes 3145728 | tf_op jit(solution)/shard_map/all_to_all | solution.py:723
  653.8 46.6 %collective-permute-start.66 = (bf16[256,1024]{1,0:T(8,128)(2,1)}, bf16[256,1024]{1,0:T(8,128)(2,1)S(1)}, u32[]{:S(2)}, u32[]{:S(2)}) collective-permute-start(bf16[256,1024]{1,0:T(8,128)(2,1)} %add_convert_fusion), channel_id=1, source_target_pairs={{28,30},{12,14},{20,22},{4,6},{24,26},{8,10},{16,18},{0,2},{29,31}... | collective-permute-start | bytes 1572872 | tf_op jit(solution)/shard_map/ppermute | solution.py:154
  700.1 18.3 %collective-permute-start.72 = (bf16[2,3,256,256]{3,2,1,0:T(8,128)(2,1)S(1)}, bf16[2,3,256,256]{3,2,1,0:T(8,128)(2,1)S(1)}, u32[]{:S(2)}, u32[]{:S(2)}) collective-permute-start(bf16[2,3,256,256]{3,2,1,0:T(8,128)(2,1)S(1)} %dynamic-slice_bitcast_fusion.1), channel_id=1, source_target_pairs={{0,8},{4,12},{8,0},{12,4},{16,24},{20,28},{24,16},{28,20},{1,9},{5... | collective-permute-start | bytes 2359304 | tf_op jit(solution)/shard_map/ppermute | solution.py:77
  701.4 17.2 %collective-permute-start.67 = (bf16[256,1024]{1,0:T(8,128)(2,1)S(1)}, bf16[256,1024]{1,0:T(8,128)(2,1)S(1)}, u32[]{:S(2)}, u32[]{:S(2)}) collective-permute-start(bf16[256,1024]{1,0:T(8,128)(2,1)S(1)} %fusion.66), channel_id=1, source_target_pairs={{26,30},{10,14},{18,22},{2,6},{27,31},{11,15},{19,23},{3,7}} | collective-permute-start | bytes 1572872 | tf_op jit(solution)/shard_map/ppermute | solution.py:154
  718.5 17.2 %collective-permute-start.73 = (bf16[3,256,256]{2,1,0:T(8,128)(2,1)S(1)}, bf16[3,256,256]{2,1,0:T(8,128)(2,1)S(1)}, u32[]{:S(2)}, u32[]{:S(2)}) collective-permute-start(bf16[3,256,256]{2,1,0:T(8,128)(2,1)S(1)} %dynamic-slice_bitcast_fusion.2), channel_id=1, source_target_pairs={{0,16},{4,20},{8,24},{12,28},{16,0},{20,4},{24,8},{28,12},{1,17},{... | collective-permute-start | bytes 1179656 | tf_op jit(solution)/shard_map/ppermute | solution.py:77
  719.7 32.5 %collective-permute-start.68 = (bf16[256,1024]{1,0:T(8,128)(2,1)}, bf16[256,1024]{1,0:T(8,128)(2,1)}, u32[]{:S(2)}, u32[]{:S(2)}) collective-permute-start(bf16[256,1024]{1,0:T(8,128)(2,1)} %fusion.105), channel_id=1, source_target_pairs={{22,30},{6,14},{23,31},{7,15}} | collective-permute-start | bytes 1572872 | tf_op jit(solution)/shard_map/ppermute | solution.py:154
  747.1 36.7 %all-to-all-start.5 = ((bf16[8,2,5,32,256]{4,3,1,2,0:T(8,128)(2,1)}), bf16[8,2,5,32,256]{4,3,1,2,0:T(8,128)(2,1)}, u32[]{:S(2)}, u32[]{:S(2)}) async-start(bf16[8,2,5,32,256]{4,3,1,2,0:T(8,128)(2,1)} %copy_bitcast_fusion), calls=%async_computation.7 | async-start | bytes 2621440 | tf_op jit(solution)/shard_map/all_to_all | solution.py:914
  801.1 19.4 %collective-permute-start.77 = (f32[14337]{0:T(1024)S(1)}, f32[14337]{0:T(1024)S(1)}, u32[]{:S(2)}, u32[]{:S(2)}) collective-permute-start(f32[14337]{0:T(1024)S(1)} %add.1032), channel_id=1, source_target_pairs={{0,8},{4,12},{8,0},{12,4},{16,24},{20,28},{24,16},{28,20},{1,9},{5... | collective-permute-start | bytes 172052 | tf_op jit(solution)/shard_map/ppermute | solution.py:77
  820.5 9.4 %collective-permute-start.78 = (f32[14337]{0:T(1024)S(1)}, f32[14337]{0:T(1024)S(1)}, u32[]{:S(2)}, u32[]{:S(2)}) collective-permute-start(f32[14337]{0:T(1024)S(1)} %add.1033), channel_id=1, source_target_pairs={{0,16},{4,20},{8,24},{12,28},{16,0},{20,4},{24,8},{28,12},{1,17},{... | collective-permute-start | bytes 172052 | tf_op jit(solution)/shard_map/ppermute | solution.py:77
  824.9 24.2 %all-to-all-start.6 = ((bf16[8,2,3,32,256]{4,3,1,2,0:T(8,128)(2,1)}), bf16[8,2,3,32,256]{4,3,1,2,0:T(8,128)(2,1)S(1)}, u32[]{:S(2)}, u32[]{:S(2)}) async-start(bf16[8,2,3,32,256]{4,3,1,2,0:T(8,128)(2,1)} %maximum_bitcast_fusion), calls=%async_computation.8 | async-start | bytes 1572864 | tf_op jit(solution)/shard_map/all_to_all | solution.py:914
  (299 other events, 2586.5 us)
Sparse Core Ops, SparseCore 0:
  15.9 53.6 all-gather.11
  78.9 90.9 all-gather.5
  172.6 47.5 all-gather.7
  222.7 71.8 all-gather.9
  421.2 85.3 reduce-scatter.2
  542.9 144.4 reduce-scatter.4

commit v3 on v2

--- a/solution.py
+++ b/solution.py
@@ -50,16 +50,6 @@
     return pull(upstream)
 
 
-def contrast(pooled, log_scale, pair_index):
-    unit_rows = pooled * lax.rsqrt(jnp.sum(pooled * pooled, axis=-1, keepdims=True) + EPS_UNIT)
-    partner = jnp.take(unit_rows, pair_index, axis=0)
-    logits = jnp.exp(log_scale) * jnp.dot(unit_rows, partner.T, precision=PRECISE)
-    matched = jnp.diagonal(logits)
-    by_rows = jax.nn.logsumexp(logits, axis=1) - matched
-    by_cols = jax.nn.logsumexp(logits, axis=0) - matched
-    return 0.5 * (jnp.mean(by_rows) + jnp.mean(by_cols))
-
-
 def adamw(weight, first, second, grad, rate, decay):
     first = BETA_ONE * first + (1 - BETA_ONE) * grad
     second = BETA_TWO * second + (1 - BETA_TWO) * grad * grad
@@ -87,7 +77,7 @@
     return found
 
 
-def scatter_sum(slots):
+def scatter_sum(slots, after_first):
     masks = [1]
     while masks[-1] * 2 < lax.axis_size("dp"):
         masks.append(masks[-1] * 2)
@@ -98,6 +88,8 @@
         away = lax.dynamic_index_in_dim(slots, 1 - bit, dim, keepdims=False)
         keep = lax.dynamic_index_in_dim(slots, bit, dim, keepdims=False)
         slots = keep + from_peer(away, "dp", mask)
+        if at == 0:
+            slots = after_first(slots)
     return slots
 
 
@@ -124,7 +116,7 @@
 
 
 def tree():
-    count = lax.axis_size("dp") * lax.axis_size("x")
+    count = lax.axis_size("dp")
     holders = [count - 1]
     steps = []
     mask = count // 2
@@ -135,23 +127,47 @@
     return steps
 
 
+def last_to_near():
+    count = lax.axis_size("dp") * lax.axis_size("x")
+    return [(count - 1, count - 2)]
+
+
 def from_last(parts):
     last = lax.axis_size("core") - 1
-    return jnp.where(lax.axis_index("core") == last, parts[last], from_peer(parts[0], "core"))
+    value = jnp.where(lax.axis_index("core") == last, parts[last], from_peer(parts[0], "core"))
+    half = value.shape[0] // 2
+    near = lax.ppermute(value[:half], GROUP, last_to_near())
+    return jnp.where(lax.axis_index("x") == 0, near, value[half:])
 
 
 def spread_from(value, step):
-    at = lax.axis_index("dp") * lax.axis_size("x") + lax.axis_index("x")
-    found = lax.ppermute(value, GROUP, step)
-    reached = jnp.any(at == jnp.array([there for here, there in step]))
+    found = lax.ppermute(value, "dp", step)
+    reached = jnp.any(lax.axis_index("dp") == jnp.array([there for here, there in step]))
     return jnp.where(reached, found, value)
 
 
+def both_halves(value):
+    other = from_peer(value, "x")
+    first = lax.axis_index("x") == 0
+    return jnp.where(
+        first,
+        jnp.concatenate([value, other], axis=0),
+        jnp.concatenate([other, value], axis=0),
+    )
+
+
 def to_last(value):
-    total = value.astype(F32)
+    half = value.shape[0] // 2
+    first = lax.axis_index("x") == 0
+    away = jnp.where(first, value[half:], value[:half])
+    total = jnp.where(first, value[:half], value[half:]).astype(F32)
+    total = total + from_peer(away, "x").astype(F32)
     for step in reversed(tree()):
         back = [(there, here) for here, there in step]
-        total = total + lax.ppermute(total.astype(BF), GROUP, back).astype(F32)
+        total = total + lax.ppermute(total.astype(BF), "dp", back).astype(F32)
+    back = [(there, here) for here, there in last_to_near()]
+    near = lax.ppermute(total.astype(BF), GROUP, back).astype(F32)
+    total = jnp.concatenate([near, total], axis=0)
     return jnp.concatenate([from_peer(total.astype(BF), "core").astype(F32), total], axis=0)
 
 
@@ -619,6 +635,106 @@
         d_shift_two,
     )
     return d_residual, bias_grads
+
+
+def precise(left, right, dims):
+    return lax.dot_general(
+        left, right, (dims, ((), ())), precision=PRECISE, preferred_element_type=F32
+    )
+
+
+def contrast_kernel(scale_ref, pairs_ref, pooled_ref, loss_ref, d_scale_ref, d_pooled_ref):
+    pooled = pooled_ref[...]
+    count = pooled.shape[0]
+    norm = lax.rsqrt(jnp.sum(pooled * pooled, axis=-1, keepdims=True) + EPS_UNIT)
+    unit = pooled * norm
+    row_at = lax.broadcasted_iota(jnp.int32, (count, count), 0)
+    column_at = lax.broadcasted_iota(jnp.int32, (count, count), 1)
+    picks = (pairs_ref[...] == column_at).astype(F32)
+    same_at = (row_at == column_at).astype(F32)
+    scale = jnp.exp(scale_ref[...])
+    partner = precise(picks, unit, ((1,), (0,)))
+    logits = scale * precise(unit, partner, ((1,), (1,)))
+    total = 0.0
+    slope = -2.0 * same_at
+    for axis in (1, 0):
+        highest = jnp.max(logits, axis=axis, keepdims=True)
+        grown = jnp.exp(logits - highest)
+        each = jnp.sum(grown, axis=axis, keepdims=True)
+        total = total + jnp.sum(highest + jnp.log(each), keepdims=True)
+        slope = slope + grown / each
+    total = total - 2.0 * jnp.sum(logits * same_at, keepdims=True)
+    weight = 0.5 * CON_WEIGHT
+    loss_ref[...] = weight * total
+    slope = weight * slope
+    d_scale_ref[...] = jnp.sum(slope * logits, keepdims=True)
+    slope = slope * scale
+    d_partner = precise(slope, unit, ((0,), (0,)))
+    d_unit = precise(slope, partner, ((1,), (0,))) + precise(picks, d_partner, ((0,), (0,)))
+    along = jnp.sum(d_unit * pooled, axis=-1, keepdims=True)
+    d_pooled_ref[...] = norm * d_unit - pooled * (norm * norm * norm * along)
+
+
+def contrast(pooled, log_scale, pair_index):
+    loss, d_scale, d_pooled = pl.pallas_call(
+        contrast_kernel,
+        out_shape=[
+            jax.ShapeDtypeStruct((1, 1), F32),
+            jax.ShapeDtypeStruct((1, 1), F32),
+            jax.ShapeDtypeStruct(pooled.shape, F32),
+        ],
+        compiler_params=wide(),
+    )(log_scale.reshape(1, 1), pair_index.reshape(-1, 1), pooled)
+    return loss[0, 0], d_scale[0, 0], d_pooled
+
+
+def split_dot(left, right):
+    total = None
+    parts = []
+    for operand in (left, right):
+        if operand.dtype == BF:
+            parts.append((operand,))
+        else:
+            high = operand.astype(BF)
+            parts.append((high, (operand - high.astype(F32)).astype(BF)))
+    for at, first in enumerate(parts[0]):
+        for second in parts[1][: 2 - at]:
+            term = dot_nn(first, second)
+            total = term if total is None else total + term
+    return total
+
+
+def precondition(blocks, left_roots, right_roots, taken, owners):
+    count, side = blocks.shape[0], blocks.shape[-1]
+    rows = side // owners
+
+    def kernel(slots_ref, block_ref, left_ref, right_ref, out_ref):
+        block = block_ref[0]
+        result = split_dot(split_dot(left_ref[0], block), right_ref[0])
+        out_ref[:, 0, 0] = block.reshape(owners, rows, side)
+        out_ref[:, 1, 0] = result.astype(BF).reshape(owners, rows, side)
+
+    root_spec = pl.BlockSpec((1, side, side), lambda step, slots_ref: (slots_ref[step], 0, 0))
+    return pl.pallas_call(
+        kernel,
+        grid_spec=pltpu.PrefetchScalarGridSpec(
+            num_scalar_prefetch=1,
+            grid=(count,),
+            in_specs=[
+                pl.BlockSpec((1, side, side), lambda step, slots_ref: (step, 0, 0)),
+                root_spec,
+                root_spec,
+            ],
+            out_specs=pl.BlockSpec(
+                (owners, 2, 1, rows, side), lambda step, slots_ref: (0, 0, step, 0, 0)
+            ),
+        ),
+        out_shape=jax.ShapeDtypeStruct((owners, 2, count, rows, side), BF),
+        compiler_params=wide(),
+        cost_estimate=pl.CostEstimate(
+            flops=10 * count * side**3, bytes_accessed=14 * blocks.size, transcendentals=0
+        ),
+    )(jnp.array(taken, jnp.int32), blocks, left_roots, right_roots)
 
 
 def shards(
@@ -695,7 +811,6 @@
             ]
         )
         hops = tree()
-        place_rows = spread_from(place_rows, hops[0])
         all_ids, place_rows = lax.optimization_barrier((all_ids, place_rows))
     by_device = all_ids.reshape(devices, local_rows)
     holder = by_device // shard_rows
@@ -752,9 +867,9 @@
 
     fetched = [[fetch(rows) for rows in of_layer] for of_layer in rows_here]
     if places_last:
-        place_rows = spread_from(place_rows, hops[1])
+        place_rows = spread_from(place_rows, hops[0])
         filled, place_rows = lax.optimization_barrier((rows_to_send(0), place_rows))
-        for step in hops[2:]:
+        for step in hops[1:]:
             place_rows = spread_from(place_rows, step)
         reached, fetched[0][0] = lax.optimization_barrier((exchange(filled), fetched[0][0]))
         token_rows = lax.fori_loop(
@@ -763,7 +878,7 @@
             lambda at, rows: rows + rows_reached(at, exchange(rows_to_send(at))),
             rows_reached(0, reached),
         )
-        embedded = token_rows + place_rows.astype(F32)
+        embedded = token_rows + both_halves(place_rows).astype(F32)
     else:
         embedded = full_rows()
 
@@ -806,15 +921,13 @@
     pooled = gather_small(pooled_here + from_peer(pooled_here, "core"), (("x", 1),))
     global_sequence = owner_rank * seq_dev + my_sequence
 
-    def contrast_loss(pooled_in, log_scale):
-        return CON_WEIGHT * pooled_in.shape[0] * contrast(pooled_in, log_scale, pair_index)
-
-    scaled_con, con_pull = jax.vjp(contrast_loss, pooled, vectors[tail_at + 3 * D + 1])
-    d_pooled, d_scale = con_pull(jnp.ones_like(scaled_con))
+    scaled_con, d_scale, d_pooled = contrast(pooled, vectors[tail_at + 3 * D + 1], pair_index)
     d_logit = counted * (jax.nn.sigmoid(logits_tok) - my_labels)
-    upstream = d_logit[:, None] * head_weight[None, :] + token_weight[:, None] * jnp.take(
-        d_pooled, global_sequence, axis=0
-    )
+    if seqs == 1:
+        d_rows = lax.dynamic_slice_in_dim(d_pooled, owner_rank * seq_dev + rank, 1, axis=0)
+    else:
+        d_rows = jnp.take(d_pooled, global_sequence, axis=0)
+    upstream = d_logit[:, None] * head_weight[None, :] + token_weight[:, None] * d_rows
     d_head_weight = jnp.dot(d_logit, residual, precision=PRECISE)
     d_head_bias = jnp.sum(d_logit)
     leader = (device == 0).astype(F32)
@@ -884,7 +997,14 @@
                 outgoing.reshape((-1,) + outgoing.shape[2:]), "dp", scatter_dimension=0, tiled=True
             )
         else:
-            arrived = once_there(sends[-1], scatter_sum(outgoing))
+            before = sends[-1]
+            arrived = scatter_sum(
+                outgoing, lambda slots: send_back(before, once_there(before, slots), False)
+            )
+            back = returned[before[0]][0]
+            arrived, back = lax.optimization_barrier((arrived, back))
+            for at, slot in enumerate(before):
+                returned[slot] = (back, at)
         for at, slot in enumerate(taken):
             summed[slot] = arrived[at]
         sends.append(taken)
@@ -895,29 +1015,34 @@
     right_root = root_right.reshape(flat_stats)
     returned = [None] * slot_count
 
-    def send_back(taken, next_in=None):
+    def send_back(taken, next_in=None, wait=True):
         some = jnp.stack([summed[slot] for slot in taken])
-
-        def roots(array):
-            return jnp.stack([array[slot] for slot in taken])
-
-        direction = jnp.einsum(
-            "sij,sjk->sik",
-            jnp.einsum(
-                "sij,sjk->sik", roots(left_root), some.astype(F32), precision=lax.Precision.HIGH
-            ),
-            roots(right_root),
-            precision=lax.Precision.HIGH,
-        )
-        both = jnp.stack([some, direction.astype(BF)])
-        outgoing = both.reshape(2, len(taken), owners, rows_per, block_size)
-        back = lax.all_to_all(
-            outgoing.transpose(2, 0, 1, 3, 4), "dp", split_axis=0, concat_axis=0, tiled=True
-        )
-        if next_in is not None:
+        if rows_per % 16 == 0:
+            outgoing = precondition(some, left_root, right_root, taken, owners)
+        else:
+
+            def roots(array):
+                return jnp.stack([array[slot] for slot in taken])
+
+            direction = jnp.einsum(
+                "sij,sjk->sik",
+                jnp.einsum(
+                    "sij,sjk->sik", roots(left_root), some.astype(F32), precision=lax.Precision.HIGH
+                ),
+                roots(right_root),
+                precision=lax.Precision.HIGH,
+            )
+            both = jnp.stack([some, direction.astype(BF)])
+            outgoing = both.reshape(2, len(taken), owners, rows_per, block_size).transpose(
+                2, 0, 1, 3, 4
+            )
+        if not wait:
+            next_in, outgoing = lax.optimization_barrier((next_in, outgoing))
+        back = lax.all_to_all(outgoing, "dp", split_axis=0, concat_axis=0, tiled=True)
+        if next_in is not None and wait:
             next_in, back = lax.optimization_barrier((next_in, back))
         for at, slot in enumerate(taken):
-            returned[slot] = back[:, :, at]
+            returned[slot] = (back, at)
         return next_in
 
     def emit_of(layer_no):
@@ -935,11 +1060,7 @@
             if name == "up" or (name == "in" and layer_no == 0):
                 next_in = sum_ready(next_in)
             if name == "out" and layer_no == 0 and len(sends) > 1:
-                next_in = send_back(sends[0], next_in)
-                if layers in early_vectors:
-                    next_in, early_vectors[layers] = lax.optimization_barrier(
-                        (next_in, early_vectors[layers])
-                    )
+                next_in = send_back(sends[0], next_in, False)
             return next_in
 
         return emit
@@ -949,7 +1070,6 @@
         return lax.dynamic_update_slice(row, piece, ((rank * cores + core) * width,))
 
     bias_parts = [None] * layers
-    early_vectors = {}
 
     def vector_rows_of(layer_no):
         grad_items = bias_parts[layer_no]
@@ -960,12 +1080,6 @@
         ] + list(grad_items[3:])
 
     for layer_no in reversed(range(layers)):
-        if layer_no == 0:
-            rows = []
-            for done_no in range(1, layers):
-                rows = rows + vector_rows_of(done_no)
-            others = jnp.stack([d_head_bias, leader * d_scale, bce_part, count_part])
-            early_vectors[layers] = sum_over_all(jnp.concatenate(rows + [d_head_weight, others]))
         upstream, bias_parts[layer_no] = layer_backward(
             upstream,
             kept_all[layer_no],
@@ -978,7 +1092,10 @@
 
     d_embed, d_gain_embed, d_shift_embed = norm_back(embedded, gain_embed, shift_embed, upstream)
     d_embed = d_embed.astype(BF)
-
+    if returned[sends[0][0]] is not None:
+        d_embed, back = lax.optimization_barrier((d_embed, returned[sends[0][0]][0]))
+        for at, slot in enumerate(sends[0]):
+            returned[slot] = (back, at)
     if places_last:
         table_shard = lax.fori_loop(
             1, rounds, lambda at, total: total + return_rows(at, d_embed), return_rows(0, d_embed)
@@ -996,34 +1113,24 @@
         ).astype(BF)
         table_shard = product(picker, d_rows)
 
-    for at, taken in enumerate(sends):
-        if returned[taken[0]] is None:
-            last = summed[sends[-1][0]] if at < len(sends) - 1 else None
-            last = send_back(taken, last)
-            if last is not None:
-                summed[sends[-1][0]] = last
-
     blocks_low = jnp.stack([summed[slot] for slot in range(slot_count)])
     blocks = blocks_low.astype(F32)
     squares = jnp.sum(table_shard * table_shard) + jnp.sum(blocks * blocks)
-    late = sum_over_all(
-        jnp.concatenate(vector_rows_of(0) + [d_gain_embed, d_shift_embed, squares.reshape(1)])
-    )
-    early = early_vectors[layers]
-    vector_total = jnp.concatenate(
-        [late[:per_layer], early[: tail_at - per_layer], late[per_layer:-1], early[tail_at - per_layer : -2]]
-    )
-    bce_total, count_total, square_total = early[-2], early[-1], late[-1]
+    for taken in sends:
+        if returned[taken[0]] is None:
+            squares = send_back(taken, squares, False)
+    vector_rows = []
+    for layer_no in range(layers):
+        vector_rows = vector_rows + vector_rows_of(layer_no)
+    scalars = jnp.stack([d_head_bias, leader * d_scale, bce_part, count_part, squares])
+    totals = sum_over_all(
+        jnp.concatenate(vector_rows + [d_gain_embed, d_shift_embed, d_head_weight, scalars])
+    )
+    vector_total = totals[:-3]
+    bce_total, count_total, square_total = totals[-3], totals[-2], totals[-1]
     grad_norm = jnp.sqrt(square_total + jnp.sum(vector_total * vector_total))
     factor = CLIP_NORM / jnp.maximum(grad_norm, CLIP_NORM)
 
-    mine_back = (
-        jnp.stack(returned)
-        .transpose(2, 0, 1, 3, 4)
-        .reshape(2, slot_count * owners, rows_per, block_size)[:, :block_count]
-        .astype(F32)
-        * factor
-    )
     square_of = factor * factor * (1 - STAT_DECAY)
     new_left = STAT_DECAY * stats_left.reshape(blocks.shape) + square_of * jnp.einsum(
         "sij,skj->sik", blocks_low, blocks_low, preferred_element_type=F32
@@ -1038,9 +1145,18 @@
     rates = (RATE_MATRIX, RATE_OUT, RATE_MATRIX, RATE_MATRIX)
     for weight, rate in zip(matrices, rates):
         span_of = weight.size // (rows_per * block_size)
-        part = mine_back[:, begin_at : begin_at + span_of].reshape((2,) + weight.shape)
-        clipped.append(part[0])
-        new_weights.append(weight - rate * (part[1] + DECAY_MATRIX * weight))
+        numbers = range(begin_at, begin_at + span_of)
+        both = []
+        for kind in range(2):
+            pieces = []
+            for slot in range(numbers[0] // owners, numbers[-1] // owners + 1):
+                back, at = returned[slot]
+                low = max(numbers[0] - slot * owners, 0)
+                high = min(numbers[-1] + 1 - slot * owners, owners)
+                pieces.append(back[low:high, kind, at])
+            both.append(jnp.concatenate(pieces, axis=0).reshape(weight.shape).astype(F32) * factor)
+        clipped.append(both[0])
+        new_weights.append(weight - rate * (both[1] + DECAY_MATRIX * weight))
         begin_at = begin_at + span_of
     clipped_vectors = vector_total * factor
     new_table, table_one, table_two = adamw(

time: 886 us -> 833 us (0.940)
  local copies, waits for them, and re-layouts: 130 us -> 86.6 us
  starting transfers between devices: 134 us -> 103 us
  waiting for transfers between devices: 305 us -> 334 us
  Pallas kernels: 140 us -> 157 us
  matrix products: 32.4 us -> 19.1 us
    ppermute x8, waiting for transfers between devices: 0.02 us -> 86.7 us  [the longest x3 44.7 us: spread_from(): found = lax.ppermute(value, 'dp', step)]
    all_to_all x2, waiting for transfers between devices: 42.2 us -> 0.01 us  [exchange(): lax.all_to_all(filled, EVERY, split_axis=0, concat_axis=0, tiled=True)]
    ppermute x71 -> x68, waiting for transfers between devices: 229 us -> 197 us  [from_peer(): return lax.ppermute(values, axis, [(at, at ^ mask) for at in range(size)])]
    unnamed x565 -> x486, local copies, waits for them, and re-layouts: 74.8 us -> 45.1 us
    all_to_all x2, starting transfers between devices: 35.5 us -> 11.4 us  [exchange(): lax.all_to_all(filled, EVERY, split_axis=0, concat_axis=0, tiled=True)]
    all_gather x4, waiting for transfers between devices: 12.4 us -> 30.4 us  [fetch(): return lax.all_gather(pieces, 'dp', axis=0, tiled=False)[:, None]]
    ppermute x71 -> x68, starting transfers between devices: 72.1 us -> 54.6 us  [from_peer(): return lax.ppermute(values, axis, [(at, at ^ mask) for at in range(size)])]
    pallas_call x0 -> x4, Pallas kernels: none -> 15.7 us  [the longest x3 13.6 us: precondition(): pl.pallas_call(kernel, grid_spec=pltpu.PrefetchScalarGridSpec(num_scalar_...]
  transfers between devices with their start and end apart: 90 -> 87, of which waited for: 55 -> 55; matrix products, arithmetic and copies ran while one was open for 19% -> 17% of each run, Pallas kernels for 13% -> 16%
where the time goes in v3:
time: 833 us; the launch traced here: 823 us
  waiting for transfers between devices  334 us (40%)
  Pallas kernels  157 us (19%)
  starting transfers between devices  103 us (12%)
  other arithmetic  98.5 us (12%)
  local copies, waits for them, and re-layouts  86.6 us (10%)
  between operations  25.1 us (3%)
  matrix products  19.1 us (2%)
    ppermute x68, waiting for transfers between devices, from_peer(): return lax.ppermute(values, axis, [(at, at ^ mask) for at in range(size)])  197 us
    pallas_call x32, Pallas kernels, rows_product(): pl.pallas_call(kernel, grid=(steps,), in_specs=[whole(left.shape), pl.Blo...  84.1 us
    ppermute x68, starting transfers between devices, from_peer(): return lax.ppermute(values, axis, [(at, at ^ mask) for at in range(size)])  54.6 us
    unnamed x486, local copies, waits for them, and re-layouts  45.1 us
    ppermute x3, waiting for transfers between devices, spread_from(): found = lax.ppermute(value, 'dp', step)  44.7 us
    ppermute x3, waiting for transfers between devices, to_last(): total = total + lax.ppermute(total.astype(BF), 'dp', back).astype(F32)  42 us
    pallas_call x8, Pallas kernels, attend(): pl.pallas_call(body, grid=(seqs, pairs), in_specs=specs, out_specs=out_sp...  34.2 us
    all_gather x4, waiting for transfers between devices, fetch(): return lax.all_gather(pieces, 'dp', axis=0, tiled=False)[:, None]  30.4 us
  transfers between devices with their start and end apart: 87, of which 55 were waited for; matrix products, arithmetic and copies ran while one was open for 17% of the time, Pallas kernels for 16%

profile of v3, /device:TPU:0, one launch (start us, length us, event | category | flops | bytes accessed | tf_op | source)
XLA Modules:
  0.0 823.3 jit_solution(10029646330865341507)
XLA Ops:
  30.4 6.7 gather_fusion.1
  40.0 7.9 all-to-all-start.2
  58.6 44.7 %collective-permute-done.7 = bf16[128,1024]{1,0:T(8,128)(2,1)S(1)} collective-permute-done((bf16[128,1024]{1,0:T(8,128)(2,1)S(1)}, bf16[128,1024]{1,0:T(8,128)(2,1)S(1)}, u32[]{:S(2)}, u32[]{:S(2)}) %collective-permute-start.7) | collective-permute-done | bytes 262176 | tf_op jit(solution)/shard_map/ppermute | solution.py:144
  109.1 3.9 collective-permute-done.8
  126.8 4.7 collective-permute-done.10
  149.8 11.0 %collective-permute-done.14 = bf16[256,1024]{1,0:T(8,128)(2,1)S(1)} collective-permute-done((bf16[256,1024]{1,0:T(8,128)(2,1)S(1)}, bf16[256,1024]{1,0:T(8,128)(2,1)S(1)}, u32[]{:S(2)}, u32[]{:S(2)}) %collective-permute-start.14) | collective-permute-done | bytes 524320 | tf_op jit(solution)/shard_map/ppermute | solution.py:67
  166.6 4.1 shard_map.381
  172.0 6.0 collective-permute-done.16
  180.2 4.1 shard_map.382
  185.6 4.0 shard_map.383
  201.2 8.5 %collective-permute-done.20 = bf16[256,1024]{1,0:T(8,128)(2,1)S(1)} collective-permute-done((bf16[256,1024]{1,0:T(8,128)(2,1)S(1)}, bf16[256,1024]{1,0:T(8,128)(2,1)S(1)}, u32[]{:S(2)}, u32[]{:S(2)}) %collective-permute-start.20) | collective-permute-done | bytes 524320 | tf_op jit(solution)/shard_map/ppermute | solution.py:67
  221.8 4.6 collective-permute-done.22
  240.9 11.0 %collective-permute-done.26 = bf16[256,1024]{1,0:T(8,128)(2,1)S(1)} collective-permute-done((bf16[256,1024]{1,0:T(8,128)(2,1)S(1)}, bf16[256,1024]{1,0:T(8,128)(2,1)S(1)}, u32[]{:S(2)}, u32[]{:S(2)}) %collective-permute-start.26) | collective-permute-done | bytes 524320 | tf_op jit(solution)/shard_map/ppermute | solution.py:67
  257.6 30.3 %all-gather.10.cloned.1.call-done = bf16[8,8,4,32,256]{4,3,2,1,0:T(8,128)(2,1)} async-done(((bf16[1,8,4,32,256]{4,3,2,1,0:T(8,128)(2,1)}), bf16[8,8,4,32,256]{4,3,2,1,0:T(8,128)(2,1)}) %all-gather.10.cloned.1.call-update) | async-done | bytes 4194320 | tf_op jit(solution)/shard_map/all_gather | solution.py:204
  295.2 4.1 shard_map.392
  300.7 3.9 shard_map.393
  309.1 4.8 shard_map.394
  361.7 8.5 %collective-permute-done.39 = bf16[256,1024]{1,0:T(8,128)(2,1)S(1)} collective-permute-done((bf16[256,1024]{1,0:T(8,128)(2,1)S(1)}, bf16[256,1024]{1,0:T(8,128)(2,1)S(1)}, u32[]{:S(2)}, u32[]{:S(2)}) %collective-permute-start.39) | collective-permute-done | bytes 524320 | tf_op jit(solution)/shard_map/ppermute | solution.py:67
  376.0 4.0 shard_map.398
  384.5 3.9 shard_map.399
  388.4 3.9 shard_map.400
  412.6 5.5 shard_map.403.refs_2_.refs_0_
  418.2 5.5 collective-permute-done.45
  426.2 5.2 shard_map.405.refs_0_.refs_3_
  443.7 12.4 %collective-permute-done.49 = bf16[256,1024]{1,0:T(8,128)(2,1)S(1)} collective-permute-done((bf16[256,1024]{1,0:T(8,128)(2,1)S(1)}, bf16[256,1024]{1,0:T(8,128)(2,1)S(1)}, u32[]{:S(2)}, u32[]{:S(2)}) %collective-permute-start.49) | collective-permute-done | bytes 524320 | tf_op jit(solution)/shard_map/ppermute | solution.py:67
  465.3 7.5 collective-permute-done.51
  474.8 3.8 shard_map.411.refs_0_.refs_3_
  478.7 4.1 shard_map.412
  486.3 3.9 shard_map.413
  495.1 4.0 shard_map.414
  519.6 5.1 shard_map.417.refs_2_.refs_0_
  524.8 5.9 collective-permute-done.57
  533.1 5.2 shard_map.419.refs_0_.refs_3_
  541.7 4.2 shard_map.422
  560.7 4.5 all-to-all-start.3
  571.7 20.2 %all-to-all-done.3 = bf16[8,2,4,32,256]{4,3,2,1,0:T(8,128)(2,1)} async-done(((bf16[8,2,4,32,256]{4,3,2,1,0:T(8,128)(2,1)}), bf16[8,2,4,32,256]{4,3,2,1,0:T(8,128)(2,1)}, u32[]{:S(2)}, u32[]{:S(2)}) %all-to-all-start.3) | async-done | bytes 1048608 | tf_op jit(solution)/shard_map/all_to_all | solution.py:1041
  602.9 9.5 %collective-permute-done.62 = bf16[128,1024]{1,0:T(8,128)(2,1)S(1)} collective-permute-done((bf16[128,1024]{1,0:T(8,128)(2,1)S(1)}, bf16[128,1024]{1,0:T(8,128)(2,1)S(1)}, u32[]{:S(2)}, u32[]{:S(2)}) %collective-permute-start.62) | collective-permute-done | bytes 262176 | tf_op jit(solution)/shard_map/ppermute | solution.py:67
  612.5 4.6 collective-permute-start.63
  617.3 42.0 %collective-permute-done.63 = bf16[128,1024]{1,0:T(8,128)(2,1)S(1)} collective-permute-done((bf16[128,1024]{1,0:T(8,128)(2,1)S(1)}, bf16[128,1024]{1,0:T(8,128)(2,1)S(1)}, u32[]{:S(2)}, u32[]{:S(2)}) %collective-permute-start.63) | collective-permute-done | bytes 262176 | tf_op jit(solution)/shard_map/ppermute | solution.py:167
  663.8 5.3 fusion.14
  670.2 5.1 shard_map.425
  676.4 16.6 %all-to-all-start.5 = ((bf16[8,2,5,32,256]{4,3,2,1,0:T(8,128)(2,1)}), bf16[8,2,5,32,256]{4,3,2,1,0:T(8,128)(2,1)}, u32[]{:S(2)}, u32[]{:S(2)}) async-start(bf16[8,2,5,32,256]{4,3,2,1,0:T(8,128)(2,1)} %copy-done.18), calls=%async_computation.7 | async-start | bytes 2621440 | tf_op jit(solution)/shard_map/all_to_all | solution.py:1041
  700.9 31.5 %collective-permute-done.69 = bf16[2,3,256,256]{3,2,1,0:T(8,128)(2,1)S(1)} collective-permute-done((bf16[2,3,256,256]{3,2,1,0:T(8,128)(2,1)S(1)}, bf16[2,3,256,256]{3,2,1,0:T(8,128)(2,1)S(1)}, u32[]{:S(2)}, u32[]{:S(2)}) %collective-permute-start.69) | collective-permute-done | bytes 786464 | tf_op jit(solution)/shard_map/ppermute | solution.py:67
  737.7 12.9 %collective-permute-done.70 = bf16[3,256,256]{2,1,0:T(8,128)(2,1)S(1)} collective-permute-done((bf16[3,256,256]{2,1,0:T(8,128)(2,1)S(1)}, bf16[3,256,256]{2,1,0:T(8,128)(2,1)S(1)}, u32[]{:S(2)}, u32[]{:S(2)}) %collective-permute-start.70) | collective-permute-done | bytes 393248 | tf_op jit(solution)/shard_map/ppermute | solution.py:67
  750.7 4.4 shard_map.426
  782.3 4.2 all-to-all-start.6
  793.0 4.5 fusion.12
  805.5 5.8 multiply_subtract_fusion
  (909 shorter events, 370.5 us)
Async XLA Ops:
  7.2 99.8 %all-gather.12.cloned.1.call-start = ((), (), s32[]{:S(2)}) async-start(), calls=%async_computation.14 | async-start | bytes 2359296 | tf_op jit(solution)/shard_map/all_gather | solution.py:204
  10.6 8.8 %collective-permute-start.3 = (bf16[256,1024]{1,0:T(8,128)(2,1)}, bf16[256,1024]{1,0:T(8,128)(2,1)}, u32[]{:S(2)}, u32[]{:S(2)}) collective-permute-start(bf16[256,1024]{1,0:T(8,128)(2,1)} %slice.536), channel_id=1, source_target_pairs={{0,1},{1,0},{2,3},{3,2},{4,5},{5,4},{6,7},{7,6},{8,9},{9,8},{10,11... | collective-permute-start | bytes 1572872 | tf_op jit(solution)/shard_map/ppermute | solution.py:67
  20.6 5.4 collective-permute-start.4
  29.7 10.3 %collective-permute-start.5 = (bf16[128,1024]{1,0:T(8,128)(2,1)S(1)}, bf16[128,1024]{1,0:T(8,128)(2,1)S(1)}, u32[]{:S(2)}, u32[]{:S(2)}) collective-permute-start(bf16[128,1024]{1,0:T(8,128)(2,1)S(1)} %slice_select_fusion.1), channel_id=1, source_target_pairs={{28,12},{29,13},{30,14},{31,15}} | collective-permute-start | bytes 786440 | tf_op jit(solution)/shard_map/ppermute | solution.py:144
  40.0 67.0 %all-to-all-start.2 = ((bf16[32,24,1024]{2,1,0:T(8,128)(2,1)}), bf16[32,24,1024]{2,1,0:T(8,128)(2,1)}, u32[]{:S(2)}, u32[]{:S(2)}) async-start(bf16[32,24,1024]{2,1,0:T(8,128)(2,1)} %bitcast.255), calls=%async_computation.2 | async-start | bytes 3145728 | tf_op jit(solution)/shard_map/all_to_all | solution.py:838
  47.9 118.7 %all-gather.6.cloned.1.call-start = ((), (), s32[]{:S(2)}) async-start(), calls=%async_computation.9 | async-start | bytes 4718592 | tf_op jit(solution)/shard_map/all_gather | solution.py:204
  52.0 163.0 %all-gather.8.cloned.1.call-start = ((), (), s32[]{:S(2)}) async-start(), calls=%async_computation.10 | async-start | bytes 2359296 | tf_op jit(solution)/shard_map/all_gather | solution.py:204
  53.4 49.9 %collective-permute-start.7 = (bf16[128,1024]{1,0:T(8,128)(2,1)S(1)}, bf16[128,1024]{1,0:T(8,128)(2,1)S(1)}, u32[]{:S(2)}, u32[]{:S(2)}) collective-permute-start(bf16[128,1024]{1,0:T(8,128)(2,1)S(1)} %broadcast_select_fusion.1), channel_id=1, source_target_pairs={{28,24},{12,8},{20,16},{4,0},{29,25},{13,9},{21,17},{5,1},{30,26},... | collective-permute-start | bytes 786440 | tf_op jit(solution)/shard_map/ppermute | solution.py:144
  104.7 8.4 %collective-permute-start.8 = (bf16[128,1024]{1,0:T(8,128)(2,1)}, bf16[128,1024]{1,0:T(8,128)(2,1)S(1)}, u32[]{:S(2)}, u32[]{:S(2)}) collective-permute-start(bf16[128,1024]{1,0:T(8,128)(2,1)} %broadcast_select_fusion.2), channel_id=1, source_target_pairs={{0,2},{2,0},{1,3},{3,1},{4,6},{6,4},{5,7},{7,5},{8,10},{10,8},{9,1... | collective-permute-start | bytes 786440 | tf_op jit(solution)/shard_map/ppermute | solution.py:67
  117.1 14.4 %collective-permute-start.10 = (bf16[256,1024]{1,0:T(8,128)(2,1)S(1)}, bf16[256,1024]{1,0:T(8,128)(2,1)}, u32[]{:S(2)}, u32[]{:S(2)}) collective-permute-start(bf16[256,1024]{1,0:T(8,128)(2,1)S(1)} %fusion.53), channel_id=1, source_target_pairs={{0,2},{2,0},{1,3},{3,1},{4,6},{6,4},{5,7},{7,5},{8,10},{10,8},{9,1... | collective-permute-start | bytes 1572872 | tf_op jit(solution)/shard_map/ppermute | solution.py:67
  144.0 143.9 %all-gather.10.cloned.1.call-start = ((), (), s32[]{:S(2)}) async-start(), calls=%async_computation.11 | async-start | bytes 4718592 | tf_op jit(solution)/shard_map/all_gather | solution.py:204
  146.7 14.1 %collective-permute-start.14 = (bf16[256,1024]{1,0:T(8,128)(2,1)S(1)}, bf16[256,1024]{1,0:T(8,128)(2,1)S(1)}, u32[]{:S(2)}, u32[]{:S(2)}) collective-permute-start(bf16[256,1024]{1,0:T(8,128)(2,1)S(1)} %fusion.50), channel_id=1, source_target_pairs={{0,2},{2,0},{1,3},{3,1},{4,6},{6,4},{5,7},{7,5},{8,10},{10,8},{9,1... | collective-permute-start | bytes 1572872 | tf_op jit(solution)/shard_map/ppermute | solution.py:67
  149.7 11.0 %collective-permute-start.13 = (bf16[256,1024]{1,0:T(8,128)(2,1)S(1)}, bf16[256,1024]{1,0:T(8,128)(2,1)S(1)}, u32[]{:S(2)}, u32[]{:S(2)}) collective-permute-start(bf16[256,1024]{1,0:T(8,128)(2,1)S(1)} %slice.783), channel_id=1, source_target_pairs={{0,1},{1,0},{2,3},{3,2},{4,5},{5,4},{6,7},{7,6},{8,9},{9,8},{10,11... | collective-permute-start | bytes 1572872 | tf_op jit(solution)/shard_map/ppermute | solution.py:67
  163.3 14.7 %collective-permute-start.16 = (bf16[256,1024]{1,0:T(8,128)(2,1)}, bf16[256,1024]{1,0:T(8,128)(2,1)}, u32[]{:S(2)}, u32[]{:S(2)}) collective-permute-start(bf16[256,1024]{1,0:T(8,128)(2,1)} %fusion.54), channel_id=1, source_target_pairs={{0,2},{2,0},{1,3},{3,1},{4,6},{6,4},{5,7},{7,5},{8,10},{10,8},{9,1... | collective-permute-start | bytes 1572872 | tf_op jit(solution)/shard_map/ppermute | solution.py:67
  192.8 297.4 %reduce-scatter.3.cloned.1.call-start = ((), (), s32[]{:S(2)}) async-start(), calls=%async_computation.12 | async-start | bytes 4718592 | tf_op jit(solution)/shard_map/reduce_scatter | solution.py:996
  195.7 14.0 %collective-permute-start.20 = (bf16[256,1024]{1,0:T(8,128)(2,1)S(1)}, bf16[256,1024]{1,0:T(8,128)(2,1)S(1)}, u32[]{:S(2)}, u32[]{:S(2)}) collective-permute-start(bf16[256,1024]{1,0:T(8,128)(2,1)S(1)} %fusion.46), channel_id=1, source_target_pairs={{0,2},{2,0},{1,3},{3,1},{4,6},{6,4},{5,7},{7,5},{8,10},{10,8},{9,1... | collective-permute-start | bytes 1572872 | tf_op jit(solution)/shard_map/ppermute | solution.py:67
  201.1 8.6 %collective-permute-start.19 = (bf16[256,1024]{1,0:T(8,128)(2,1)S(1)}, bf16[256,1024]{1,0:T(8,128)(2,1)S(1)}, u32[]{:S(2)}, u32[]{:S(2)}) collective-permute-start(bf16[256,1024]{1,0:T(8,128)(2,1)S(1)} %slice.781), channel_id=1, source_target_pairs={{0,1},{1,0},{2,3},{3,2},{4,5},{5,4},{6,7},{7,6},{8,9},{9,8},{10,11... | collective-permute-start | bytes 1572872 | tf_op jit(solution)/shard_map/ppermute | solution.py:67
  211.7 14.7 %collective-permute-start.22 = (bf16[256,1024]{1,0:T(8,128)(2,1)}, bf16[256,1024]{1,0:T(8,128)(2,1)}, u32[]{:S(2)}, u32[]{:S(2)}) collective-permute-start(bf16[256,1024]{1,0:T(8,128)(2,1)} %fusion.55), channel_id=1, source_target_pairs={{0,2},{2,0},{1,3},{3,1},{4,6},{6,4},{5,7},{7,5},{8,10},{10,8},{9,1... | collective-permute-start | bytes 1572872 | tf_op jit(solution)/shard_map/ppermute | solution.py:67
  237.8 14.0 %collective-permute-start.26 = (bf16[256,1024]{1,0:T(8,128)(2,1)S(1)}, bf16[256,1024]{1,0:T(8,128)(2,1)S(1)}, u32[]{:S(2)}, u32[]{:S(2)}) collective-permute-start(bf16[256,1024]{1,0:T(8,128)(2,1)S(1)} %fusion.42), channel_id=1, source_target_pairs={{0,2},{2,0},{1,3},{3,1},{4,6},{6,4},{5,7},{7,5},{8,10},{10,8},{9,1... | collective-permute-start | bytes 1572872 | tf_op jit(solution)/shard_map/ppermute | solution.py:67
  240.8 11.0 %collective-permute-start.25 = (bf16[256,1024]{1,0:T(8,128)(2,1)S(1)}, bf16[256,1024]{1,0:T(8,128)(2,1)S(1)}, u32[]{:S(2)}, u32[]{:S(2)}) collective-permute-start(bf16[256,1024]{1,0:T(8,128)(2,1)S(1)} %slice.779), channel_id=1, source_target_pairs={{0,1},{1,0},{2,3},{3,2},{4,5},{5,4},{6,7},{7,6},{8,9},{9,8},{10,11... | collective-permute-start | bytes 1572872 | tf_op jit(solution)/shard_map/ppermute | solution.py:67
  254.4 38.6 %collective-permute-start.28 = (bf16[256,1024]{1,0:T(8,128)(2,1)}, bf16[256,1024]{1,0:T(8,128)(2,1)}, u32[]{:S(2)}, u32[]{:S(2)}) collective-permute-start(bf16[256,1024]{1,0:T(8,128)(2,1)} %fusion.56), channel_id=1, source_target_pairs={{0,2},{2,0},{1,3},{3,1},{4,6},{6,4},{5,7},{7,5},{8,10},{10,8},{9,1... | collective-permute-start | bytes 1572872 | tf_op jit(solution)/shard_map/ppermute | solution.py:67
  307.6 14.2 %collective-permute-start.32 = (bf16[256,1024]{1,0:T(8,128)(2,1)}, bf16[256,1024]{1,0:T(8,128)(2,1)S(1)}, u32[]{:S(2)}, u32[]{:S(2)}) collective-permute-start(bf16[256,1024]{1,0:T(8,128)(2,1)} %fusion.38), channel_id=1, source_target_pairs={{0,2},{2,0},{1,3},{3,1},{4,6},{6,4},{5,7},{7,5},{8,10},{10,8},{9,1... | collective-permute-start | bytes 1572872 | tf_op jit(solution)/shard_map/ppermute | solution.py:67
  316.0 5.8 collective-permute-start.31
  343.2 4.9 collective-permute-start.37
  355.9 14.3 %collective-permute-start.39 = (bf16[256,1024]{1,0:T(8,128)(2,1)S(1)}, bf16[256,1024]{1,0:T(8,128)(2,1)S(1)}, u32[]{:S(2)}, u32[]{:S(2)}) collective-permute-start(bf16[256,1024]{1,0:T(8,128)(2,1)S(1)} %get-tuple-element.516), channel_id=1, source_target_pairs={{0,2},{2,0},{1,3},{3,1},{4,6},{6,4},{5,7},{7,5},{8,10},{10,8},{9,1... | collective-permute-start | bytes 1572872 | tf_op jit(solution)/shard_map/ppermute | solution.py:67
  383.1 21.2 %collective-permute-start.43 = (bf16[256,1024]{1,0:T(8,128)(2,1)}, bf16[256,1024]{1,0:T(8,128)(2,1)}, u32[]{:S(2)}, u32[]{:S(2)}) collective-permute-start(bf16[256,1024]{1,0:T(8,128)(2,1)} %fusion.34), channel_id=1, source_target_pairs={{0,2},{2,0},{1,3},{3,1},{4,6},{6,4},{5,7},{7,5},{8,10},{10,8},{9,1... | collective-permute-start | bytes 1572872 | tf_op jit(solution)/shard_map/ppermute | solution.py:67
  404.2 264.9 %reduce-scatter.5.cloned.1.call-start = ((), (), s32[]{:S(2)}) async-start(), calls=%async_computation.13 | async-start | bytes 5898240 | tf_op jit(solution)/shard_map/reduce_scatter | solution.py:996
  409.9 13.8 %collective-permute-start.45 = (bf16[256,1024]{1,0:T(8,128)(2,1)S(1)}, bf16[256,1024]{1,0:T(8,128)(2,1)S(1)}, u32[]{:S(2)}, u32[]{:S(2)}) collective-permute-start(bf16[256,1024]{1,0:T(8,128)(2,1)S(1)} %get-tuple-element.518), channel_id=1, source_target_pairs={{0,2},{2,0},{1,3},{3,1},{4,6},{6,4},{5,7},{7,5},{8,10},{10,8},{9,1... | collective-permute-start | bytes 1572872 | tf_op jit(solution)/shard_map/ppermute | solution.py:67
  442.0 14.2 %collective-permute-start.49 = (bf16[256,1024]{1,0:T(8,128)(2,1)S(1)}, bf16[256,1024]{1,0:T(8,128)(2,1)S(1)}, u32[]{:S(2)}, u32[]{:S(2)}) collective-permute-start(bf16[256,1024]{1,0:T(8,128)(2,1)S(1)} %fusion.31), channel_id=1, source_target_pairs={{0,2},{2,0},{1,3},{3,1},{4,6},{6,4},{5,7},{7,5},{8,10},{10,8},{9,1... | collective-permute-start | bytes 1572872 | tf_op jit(solution)/shard_map/ppermute | solution.py:67
  458.5 14.3 %collective-permute-start.51 = (bf16[256,1024]{1,0:T(8,128)(2,1)S(1)}, bf16[256,1024]{1,0:T(8,128)(2,1)S(1)}, u32[]{:S(2)}, u32[]{:S(2)}) collective-permute-start(bf16[256,1024]{1,0:T(8,128)(2,1)S(1)} %get-tuple-element.520), channel_id=1, source_target_pairs={{0,2},{2,0},{1,3},{3,1},{4,6},{6,4},{5,7},{7,5},{8,10},{10,8},{9,1... | collective-permute-start | bytes 1572872 | tf_op jit(solution)/shard_map/ppermute | solution.py:67
  485.8 25.2 %collective-permute-start.55 = (bf16[256,1024]{1,0:T(8,128)(2,1)}, bf16[256,1024]{1,0:T(8,128)(2,1)}, u32[]{:S(2)}, u32[]{:S(2)}) collective-permute-start(bf16[256,1024]{1,0:T(8,128)(2,1)} %fusion.28), channel_id=1, source_target_pairs={{0,2},{2,0},{1,3},{3,1},{4,6},{6,4},{5,7},{7,5},{8,10},{10,8},{9,1... | collective-permute-start | bytes 1572872 | tf_op jit(solution)/shard_map/ppermute | solution.py:67
  516.9 13.8 %collective-permute-start.57 = (bf16[256,1024]{1,0:T(8,128)(2,1)S(1)}, bf16[256,1024]{1,0:T(8,128)(2,1)S(1)}, u32[]{:S(2)}, u32[]{:S(2)}) collective-permute-start(bf16[256,1024]{1,0:T(8,128)(2,1)S(1)} %get-tuple-element.522), channel_id=1, source_target_pairs={{0,2},{2,0},{1,3},{3,1},{4,6},{6,4},{5,7},{7,5},{8,10},{10,8},{9,1... | collective-permute-start | bytes 1572872 | tf_op jit(solution)/shard_map/ppermute | solution.py:67
  540.4 6.5 collective-permute-start.59
  552.1 15.4 %collective-permute-start.61 = (bf16[256,1024]{1,0:T(8,128)(2,1)}, bf16[256,1024]{1,0:T(8,128)(2,1)}, u32[]{:S(2)}, u32[]{:S(2)}) collective-permute-start(bf16[256,1024]{1,0:T(8,128)(2,1)} %fusion.22), channel_id=1, source_target_pairs={{0,2},{2,0},{1,3},{3,1},{4,6},{6,4},{5,7},{7,5},{8,10},{10,8},{9,1... | collective-permute-start | bytes 1572872 | tf_op jit(solution)/shard_map/ppermute | solution.py:67
  560.7 6.9 collective-permute-start.60
  560.7 31.2 %all-to-all-start.3 = ((bf16[8,2,4,32,256]{4,3,2,1,0:T(8,128)(2,1)}), bf16[8,2,4,32,256]{4,3,2,1,0:T(8,128)(2,1)}, u32[]{:S(2)}, u32[]{:S(2)}) async-start(bf16[8,2,4,32,256]{4,3,2,1,0:T(8,128)(2,1)} %copy-done.19), calls=%async_computation.4 | async-start | bytes 2097152 | tf_op jit(solution)/shard_map/all_to_all | solution.py:1041
  593.6 70.2 %all-to-all-start.4 = ((bf16[32,24,1024]{2,1,0:T(8,128)(2,1)}), bf16[32,24,1024]{2,1,0:T(8,128)(2,1)}, u32[]{:S(2)}, u32[]{:S(2)}) async-start(bf16[32,24,1024]{2,1,0:T(8,128)(2,1)} %bitcast.256), calls=%async_computation.5 | async-start | bytes 3145728 | tf_op jit(solution)/shard_map/all_to_all | solution.py:838
  599.3 60.9 %collective-permute-start.68 = (bf16[2,2,3,256,256]{4,3,2,1,0:T(8,128)(2,1)S(1)}, bf16[2,2,3,256,256]{4,3,2,1,0:T(8,128)(2,1)S(1)}, u32[]{:S(2)}, u32[]{:S(2)}) collective-permute-start(bf16[2,2,3,256,256]{4,3,2,1,0:T(8,128)(2,1)S(1)} %dynamic-slice_bitcast_fusion), channel_id=1, source_target_pairs={{0,4},{4,0},{8,12},{12,8},{16,20},{20,16},{24,28},{28,24},{1,5},{5... | collective-permute-start | bytes 4718600 | tf_op jit(solution)/shard_map/ppermute | solution.py:67
  601.0 11.3 %collective-permute-start.62 = (bf16[128,1024]{1,0:T(8,128)(2,1)S(1)}, bf16[128,1024]{1,0:T(8,128)(2,1)S(1)}, u32[]{:S(2)}, u32[]{:S(2)}) collective-permute-start(bf16[128,1024]{1,0:T(8,128)(2,1)S(1)} %broadcast_select_fusion.3), channel_id=1, source_target_pairs={{0,2},{2,0},{1,3},{3,1},{4,6},{6,4},{5,7},{7,5},{8,10},{10,8},{9,1... | collective-permute-start | bytes 786440 | tf_op jit(solution)/shard_map/ppermute | solution.py:67
  612.5 46.8 %collective-permute-start.63 = (bf16[128,1024]{1,0:T(8,128)(2,1)S(1)}, bf16[128,1024]{1,0:T(8,128)(2,1)S(1)}, u32[]{:S(2)}, u32[]{:S(2)}) collective-permute-start(bf16[128,1024]{1,0:T(8,128)(2,1)S(1)} %get-tuple-element.506), channel_id=1, source_target_pairs={{24,28},{8,12},{16,20},{0,4},{25,29},{9,13},{17,21},{1,5},{26,30},... | collective-permute-start | bytes 786440 | tf_op jit(solution)/shard_map/ppermute | solution.py:167
  662.4 30.6 %collective-permute-start.65 = (bf16[128,1024]{1,0:T(8,128)(2,1)}, bf16[128,1024]{1,0:T(8,128)(2,1)}, u32[]{:S(2)}, u32[]{:S(2)}) collective-permute-start(bf16[128,1024]{1,0:T(8,128)(2,1)} %fusion.77), channel_id=1, source_target_pairs={{12,28},{13,29},{14,30},{15,31}} | collective-permute-start | bytes 786440 | tf_op jit(solution)/shard_map/ppermute | solution.py:167
  676.4 74.3 %all-to-all-start.5 = ((bf16[8,2,5,32,256]{4,3,2,1,0:T(8,128)(2,1)}), bf16[8,2,5,32,256]{4,3,2,1,0:T(8,128)(2,1)}, u32[]{:S(2)}, u32[]{:S(2)}) async-start(bf16[8,2,5,32,256]{4,3,2,1,0:T(8,128)(2,1)} %copy-done.18), calls=%async_computation.7 | async-start | bytes 2621440 | tf_op jit(solution)/shard_map/all_to_all | solution.py:1041
  696.5 35.8 %collective-permute-start.69 = (bf16[2,3,256,256]{3,2,1,0:T(8,128)(2,1)S(1)}, bf16[2,3,256,256]{3,2,1,0:T(8,128)(2,1)S(1)}, u32[]{:S(2)}, u32[]{:S(2)}) collective-permute-start(bf16[2,3,256,256]{3,2,1,0:T(8,128)(2,1)S(1)} %dynamic-slice_bitcast_fusion.1), channel_id=1, source_target_pairs={{0,8},{4,12},{8,0},{12,4},{16,24},{20,28},{24,16},{28,20},{1,9},{5... | collective-permute-start | bytes 2359304 | tf_op jit(solution)/shard_map/ppermute | solution.py:67
  732.5 18.2 %collective-permute-start.70 = (bf16[3,256,256]{2,1,0:T(8,128)(2,1)S(1)}, bf16[3,256,256]{2,1,0:T(8,128)(2,1)S(1)}, u32[]{:S(2)}, u32[]{:S(2)}) collective-permute-start(bf16[3,256,256]{2,1,0:T(8,128)(2,1)S(1)} %dynamic-slice_bitcast_fusion.2), channel_id=1, source_target_pairs={{0,16},{4,20},{8,24},{12,28},{16,0},{20,4},{24,8},{28,12},{1,17},{... | collective-permute-start | bytes 1179656 | tf_op jit(solution)/shard_map/ppermute | solution.py:67
  762.8 5.3 collective-permute-start.72
  768.2 5.3 collective-permute-start.73
  778.4 8.1 collective-permute-start.75
  782.3 28.9 %all-to-all-start.6 = ((bf16[8,2,3,32,256]{4,3,2,1,0:T(8,128)(2,1)}), bf16[8,2,3,32,256]{4,3,2,1,0:T(8,128)(2,1)S(1)}, u32[]{:S(2)}, u32[]{:S(2)}) async-start(bf16[8,2,3,32,256]{4,3,2,1,0:T(8,128)(2,1)} %shard_map.426), calls=%async_computation.8 | async-start | bytes 1572864 | tf_op jit(solution)/shard_map/all_to_all | solution.py:1041
  (272 other events, 1748.3 us)
Sparse Core Ops, SparseCore 0:
  15.9 68.3 all-gather.11
  87.0 76.1 all-gather.5
  165.9 47.5 all-gather.7
  216.1 71.8 all-gather.9
  404.3 85.6 reduce-scatter.2
  511.0 136.9 reduce-scatter.4

commit v4 on v3

--- a/solution.py
+++ b/solution.py
@@ -77,20 +77,20 @@
     return found
 
 
-def scatter_sum(slots, after_first):
+def halving_steps():
     masks = [1]
     while masks[-1] * 2 < lax.axis_size("dp"):
         masks.append(masks[-1] * 2)
-    slots = slots.reshape((2,) * len(masks) + slots.shape[1:])
-    for at, mask in enumerate(masks):
-        bit = lax.axis_index("dp") // mask % 2
-        dim = len(masks) - 1 - at
-        away = lax.dynamic_index_in_dim(slots, 1 - bit, dim, keepdims=False)
-        keep = lax.dynamic_index_in_dim(slots, bit, dim, keepdims=False)
-        slots = keep + from_peer(away, "dp", mask)
-        if at == 0:
-            slots = after_first(slots)
-    return slots
+    return masks
+
+
+def halve(slots, step):
+    mask = halving_steps()[step]
+    dim = len(halving_steps()) - 1 - step
+    bit = lax.axis_index("dp") // mask % 2
+    away = lax.dynamic_index_in_dim(slots, 1 - bit, dim, keepdims=False)
+    keep = lax.dynamic_index_in_dim(slots, bit, dim, keepdims=False)
+    return keep + from_peer(away, "dp", mask)
 
 
 def sum_over_all(values):
@@ -844,9 +844,11 @@
     def rows_reached(round_no, reached):
         return product_tn(plan(round_no)[1], reached)
 
-    def return_rows(round_no, grads):
-        row_of_slot, slot_of_token = plan(round_no)
-        reached = exchange(product(slot_of_token, grads).astype(BF))
+    def rows_to_return(round_no, grads):
+        return product(plan(round_no)[1], grads).astype(BF)
+
+    def rows_returned(round_no, reached):
+        row_of_slot = plan(round_no)[0]
         picker = (row_of_slot[None, :] == 1 + jnp.arange(shard_rows)[:, None]).astype(BF)
         return product(picker, reached)
 
@@ -952,6 +954,7 @@
     ready_slots = {}
     summed = {}
     sends = []
+    halved = []
 
     def slot_parts(slot):
         if slot in ready_slots:
@@ -997,14 +1000,10 @@
                 outgoing.reshape((-1,) + outgoing.shape[2:]), "dp", scatter_dimension=0, tiled=True
             )
         else:
-            before = sends[-1]
-            arrived = scatter_sum(
-                outgoing, lambda slots: send_back(before, once_there(before, slots), False)
-            )
-            back = returned[before[0]][0]
-            arrived, back = lax.optimization_barrier((arrived, back))
-            for at, slot in enumerate(before):
-                returned[slot] = (back, at)
+            bits = (2,) * len(halving_steps())
+            halved.append(halve(outgoing.reshape(bits + outgoing.shape[1:]), 0))
+            sends.append(taken)
+            return next_in
         for at, slot in enumerate(taken):
             summed[slot] = arrived[at]
         sends.append(taken)
@@ -1093,12 +1092,26 @@
     d_embed, d_gain_embed, d_shift_embed = norm_back(embedded, gain_embed, shift_embed, upstream)
     d_embed = d_embed.astype(BF)
     if returned[sends[0][0]] is not None:
-        d_embed, back = lax.optimization_barrier((d_embed, returned[sends[0][0]][0]))
+        d_embed, back, halved = lax.optimization_barrier(
+            (d_embed, returned[sends[0][0]][0], halved)
+        )
         for at, slot in enumerate(sends[0]):
             returned[slot] = (back, at)
+    last_step = len(halving_steps()) - 1
+    halved = [halve(slots, 1) for slots in halved]
     if places_last:
+        reached = exchange(rows_to_return(0, d_embed))
+        if halved:
+            before = sends[-2]
+            sums = jnp.stack([summed[slot] for slot in before])
+            reached, halved, sums = lax.optimization_barrier((reached, halved, sums))
+            for at, slot in enumerate(before):
+                summed[slot] = sums[at]
         table_shard = lax.fori_loop(
-            1, rounds, lambda at, total: total + return_rows(at, d_embed), return_rows(0, d_embed)
+            1,
+            rounds,
+            lambda at, total: total + rows_returned(at, exchange(rows_to_return(at, d_embed))),
+            rows_returned(0, reached),
         )
         place_grads = to_last(d_embed)
         table_shard = table_shard.at[last_base : last_base + seq_slots].add(
@@ -1112,6 +1125,13 @@
             all_places[None, :] == held[:, None]
         ).astype(BF)
         table_shard = product(picker, d_rows)
+
+    for slots in halved:
+        for step in range(2, last_step + 1):
+            slots = halve(slots, step)
+        slots = send_back(sends[-2], slots, False)
+        for at, slot in enumerate(sends[-1]):
+            summed[slot] = slots[at]
 
     blocks_low = jnp.stack([summed[slot] for slot in range(slot_count)])
     blocks = blocks_low.astype(F32)
@@ -1123,9 +1143,8 @@
     for layer_no in range(layers):
         vector_rows = vector_rows + vector_rows_of(layer_no)
     scalars = jnp.stack([d_head_bias, leader * d_scale, bce_part, count_part, squares])
-    totals = sum_over_all(
-        jnp.concatenate(vector_rows + [d_gain_embed, d_shift_embed, d_head_weight, scalars])
-    )
+    totals = jnp.concatenate(vector_rows + [d_gain_embed, d_shift_embed, d_head_weight, scalars])
+    totals = sum_over_all(totals)
     vector_total = totals[:-3]
     bce_total, count_total, square_total = totals[-3], totals[-2], totals[-1]
     grad_norm = jnp.sqrt(square_total + jnp.sum(vector_total * vector_total))

time: 833 us -> 829 us (level)
    ppermute x3, waiting for transfers between devices: 42 us -> 13.8 us  [to_last(): total = total + lax.ppermute(total.astype(BF), 'dp', back).astype(F32)]
    ppermute x68, waiting for transfers between devices: 197 us -> 215 us  [from_peer(): return lax.ppermute(values, axis, [(at, at ^ mask) for at in range(size)])]
    ppermute x68, starting transfers between devices: 54.6 us -> 65 us  [from_peer(): return lax.ppermute(values, axis, [(at, at ^ mask) for at in range(size)])]
    all_to_all x3, starting transfers between devices: 25.3 us -> 15.3 us  [send_back(): lax.all_to_all(outgoing, 'dp', split_axis=0, concat_axis=0, tiled=True)]
    unnamed x486 -> x444, local copies, waits for them, and re-layouts: 45.1 us -> 44.9 us
  transfers between devices with their start and end apart: 87 -> 87, of which waited for: 55 -> 59; matrix products, arithmetic and copies ran while one was open for 17% -> 18% of each run, Pallas kernels for 16% -> 16%
where the time goes in v4:
time: 829 us; the launch traced here: 819 us
  waiting for transfers between devices  328 us (40%)
  Pallas kernels  157 us (19%)
  starting transfers between devices  102 us (12%)
  other arithmetic  102 us (12%)
  local copies, waits for them, and re-layouts  84.7 us (10%)
  between operations  24.5 us (3%)
  matrix products  20.2 us (2%)
    ppermute x68, waiting for transfers between devices, from_peer(): return lax.ppermute(values, axis, [(at, at ^ mask) for at in range(size)])  215 us
    pallas_call x32, Pallas kernels, rows_product(): pl.pallas_call(kernel, grid=(steps,), in_specs=[whole(left.shape), pl.Blo...  82.3 us
    ppermute x68, starting transfers between devices, from_peer(): return lax.ppermute(values, axis, [(at, at ^ mask) for at in range(size)])  65 us
    unnamed x444, local copies, waits for them, and re-layouts  44.9 us
    ppermute x3, waiting for transfers between devices, spread_from(): found = lax.ppermute(value, 'dp', step)  44.7 us
    pallas_call x8, Pallas kernels, attend(): pl.pallas_call(body, grid=(seqs, pairs), in_specs=specs, out_specs=out_sp...  34 us
    all_gather x4, waiting for transfers between devices, fetch(): return lax.all_gather(pieces, 'dp', axis=0, tiled=False)[:, None]  32.8 us
    pallas_call x8, Pallas kernels, block_grads(): pl.pallas_call(kernel, grid=(high,), in_specs=[whole(member.shape) for me...  22.7 us
  transfers between devices with their start and end apart: 87, of which 59 were waited for; matrix products, arithmetic and copies ran while one was open for 18% of the time, Pallas kernels for 16%

profile of v4, /device:TPU:0, one launch (start us, length us, event | category | flops | bytes accessed | tf_op | source)
XLA Modules:
  0.0 818.9 jit_solution(279695118074577832)
XLA Ops:
  30.4 6.7 gather_fusion.1
  40.0 7.9 all-to-all-start.2
  58.6 44.7 %collective-permute-done.7 = bf16[128,1024]{1,0:T(8,128)(2,1)S(1)} collective-permute-done((bf16[128,1024]{1,0:T(8,128)(2,1)S(1)}, bf16[128,1024]{1,0:T(8,128)(2,1)S(1)}, u32[]{:S(2)}, u32[]{:S(2)}) %collective-permute-start.7) | collective-permute-done | bytes 262176 | tf_op jit(solution)/shard_map/ppermute | solution.py:144
  125.0 4.9 collective-permute-done.10
  146.9 11.0 %collective-permute-done.14 = bf16[256,1024]{1,0:T(8,128)(2,1)S(1)} collective-permute-done((bf16[256,1024]{1,0:T(8,128)(2,1)S(1)}, bf16[256,1024]{1,0:T(8,128)(2,1)S(1)}, u32[]{:S(2)}, u32[]{:S(2)}) %collective-permute-start.14) | collective-permute-done | bytes 524320 | tf_op jit(solution)/shard_map/ppermute | solution.py:67
  163.7 4.1 shard_map.381
  169.1 6.0 collective-permute-done.16
  177.2 4.1 shard_map.382
  182.7 4.0 shard_map.383
  198.3 8.5 %collective-permute-done.20 = bf16[256,1024]{1,0:T(8,128)(2,1)S(1)} collective-permute-done((bf16[256,1024]{1,0:T(8,128)(2,1)S(1)}, bf16[256,1024]{1,0:T(8,128)(2,1)S(1)}, u32[]{:S(2)}, u32[]{:S(2)}) %collective-permute-start.20) | collective-permute-done | bytes 524320 | tf_op jit(solution)/shard_map/ppermute | solution.py:67
  220.0 3.9 collective-permute-done.22
  238.4 10.9 %collective-permute-done.26 = bf16[256,1024]{1,0:T(8,128)(2,1)S(1)} collective-permute-done((bf16[256,1024]{1,0:T(8,128)(2,1)S(1)}, bf16[256,1024]{1,0:T(8,128)(2,1)S(1)}, u32[]{:S(2)}, u32[]{:S(2)}) %collective-permute-start.26) | collective-permute-done | bytes 524320 | tf_op jit(solution)/shard_map/ppermute | solution.py:67
  256.3 31.8 %all-gather.10.cloned.1.call-done = bf16[8,8,4,32,256]{4,3,2,1,0:T(8,128)(2,1)} async-done(((bf16[1,8,4,32,256]{4,3,2,1,0:T(8,128)(2,1)}), bf16[8,8,4,32,256]{4,3,2,1,0:T(8,128)(2,1)}) %all-gather.10.cloned.1.call-update) | async-done | bytes 4194320 | tf_op jit(solution)/shard_map/all_gather | solution.py:204
  296.5 4.1 shard_map.392
  301.9 3.9 shard_map.393
  359.7 8.5 %collective-permute-done.39 = bf16[256,1024]{1,0:T(8,128)(2,1)S(1)} collective-permute-done((bf16[256,1024]{1,0:T(8,128)(2,1)S(1)}, bf16[256,1024]{1,0:T(8,128)(2,1)S(1)}, u32[]{:S(2)}, u32[]{:S(2)}) %collective-permute-start.39) | collective-permute-done | bytes 524320 | tf_op jit(solution)/shard_map/ppermute | solution.py:67
  374.0 4.0 shard_map.398
  382.5 3.9 shard_map.399
  386.4 3.9 shard_map.400
  408.4 5.3 shard_map.403.refs_2_.refs_0_
  413.7 5.8 collective-permute-done.45
  422.0 5.2 shard_map.405.refs_0_.refs_3_
  440.1 12.4 %collective-permute-done.49 = bf16[256,1024]{1,0:T(8,128)(2,1)S(1)} collective-permute-done((bf16[256,1024]{1,0:T(8,128)(2,1)S(1)}, bf16[256,1024]{1,0:T(8,128)(2,1)S(1)}, u32[]{:S(2)}, u32[]{:S(2)}) %collective-permute-start.49) | collective-permute-done | bytes 524320 | tf_op jit(solution)/shard_map/ppermute | solution.py:67
  459.7 8.5 %collective-permute-done.51 = bf16[256,1024]{1,0:T(8,128)(2,1)S(1)} collective-permute-done((bf16[256,1024]{1,0:T(8,128)(2,1)S(1)}, bf16[256,1024]{1,0:T(8,128)(2,1)S(1)}, u32[]{:S(2)}, u32[]{:S(2)}) %collective-permute-start.51) | collective-permute-done | bytes 524320 | tf_op jit(solution)/shard_map/ppermute | solution.py:67
  470.1 3.8 shard_map.411.refs_0_.refs_3_
  474.0 4.1 shard_map.412
  481.6 3.9 shard_map.413
  490.4 4.3 shard_map.414
  513.2 5.1 shard_map.417.refs_2_.refs_0_
  519.2 5.0 collective-permute-done.57
  529.0 5.1 shard_map.419.refs_0_.refs_3_
  545.0 5.1 shard_map.422
  564.7 4.4 all-to-all-start.3
  574.3 48.3 %collective-permute-done.62 = bf16[2,2,3,256,256]{4,3,2,1,0:T(8,128)(2,1)} collective-permute-done((bf16[2,2,3,256,256]{4,3,2,1,0:T(8,128)(2,1)}, bf16[2,2,3,256,256]{4,3,2,1,0:T(8,128)(2,1)}, u32[]{:S(2)}, u32[]{:S(2)}) %collective-permute-start.62) | collective-permute-done | bytes 1572896 | tf_op jit(solution)/shard_map/ppermute | solution.py:67
  628.6 4.0 all-to-all-start.4
  637.0 13.8 %collective-permute-done.65 = bf16[128,1024]{1,0:T(8,128)(2,1)S(1)} collective-permute-done((bf16[128,1024]{1,0:T(8,128)(2,1)S(1)}, bf16[128,1024]{1,0:T(8,128)(2,1)S(1)}, u32[]{:S(2)}, u32[]{:S(2)}) %collective-permute-start.65) | collective-permute-done | bytes 262176 | tf_op jit(solution)/shard_map/ppermute | solution.py:167
  656.5 23.3 %collective-permute-done.63 = bf16[2,3,256,256]{3,2,1,0:T(8,128)(2,1)S(1)} collective-permute-done((bf16[2,3,256,256]{3,2,1,0:T(8,128)(2,1)S(1)}, bf16[2,3,256,256]{3,2,1,0:T(8,128)(2,1)S(1)}, u32[]{:S(2)}, u32[]{:S(2)}) %collective-permute-start.63) | collective-permute-done | bytes 786464 | tf_op jit(solution)/shard_map/ppermute | solution.py:67
  683.2 5.1 fusion.14
  688.4 4.3 fusion.17
  692.7 6.6 shard_map.425
  703.1 4.4 shard_map.426
  720.7 14.6 %collective-permute-start.73 = (f32[27653]{0:T(1024)S(1)}, f32[27653]{0:T(1024)S(1)}, u32[]{:S(2)}, u32[]{:S(2)}) collective-permute-start(f32[27653]{0:T(1024)S(1)} %add.913), channel_id=1, source_target_pairs={{0,4},{4,0},{8,12},{12,8},{16,20},{20,16},{24,28},{28,24},{1,5},{5... | collective-permute-start | bytes 331844 | tf_op jit(solution)/shard_map/ppermute | solution.py:67
  745.8 7.3 all-to-all-start.5
  758.4 4.2 fusion.13
  762.6 6.7 all-to-all-done.5
  773.8 4.5 fusion.12
  779.2 8.2 multiply_subtract_fusion
  789.7 13.6 %all-to-all-done.6 = bf16[8,2,5,32,256]{4,3,2,1,0:T(8,128)(2,1)S(1)} async-done(((bf16[8,2,5,32,256]{4,3,2,1,0:T(8,128)(2,1)}), bf16[8,2,5,32,256]{4,3,2,1,0:T(8,128)(2,1)S(1)}, u32[]{:S(2)}, u32[]{:S(2)}) %all-to-all-start.6) | async-done | bytes 1310752 | tf_op jit(solution)/shard_map/all_to_all | solution.py:1040
  (867 shorter events, 370.9 us)
Async XLA Ops:
  7.2 99.3 %all-gather.12.cloned.1.call-start = ((), (), s32[]{:S(2)}) async-start(), calls=%async_computation.14 | async-start | bytes 2359296 | tf_op jit(solution)/shard_map/all_gather | solution.py:204
  10.6 8.8 %collective-permute-start.3 = (bf16[256,1024]{1,0:T(8,128)(2,1)}, bf16[256,1024]{1,0:T(8,128)(2,1)}, u32[]{:S(2)}, u32[]{:S(2)}) collective-permute-start(bf16[256,1024]{1,0:T(8,128)(2,1)} %slice.536), channel_id=1, source_target_pairs={{0,1},{1,0},{2,3},{3,2},{4,5},{5,4},{6,7},{7,6},{8,9},{9,8},{10,11... | collective-permute-start | bytes 1572872 | tf_op jit(solution)/shard_map/ppermute | solution.py:67
  20.6 5.4 collective-permute-start.4
  29.7 10.3 %collective-permute-start.5 = (bf16[128,1024]{1,0:T(8,128)(2,1)S(1)}, bf16[128,1024]{1,0:T(8,128)(2,1)S(1)}, u32[]{:S(2)}, u32[]{:S(2)}) collective-permute-start(bf16[128,1024]{1,0:T(8,128)(2,1)S(1)} %slice_select_fusion.1), channel_id=1, source_target_pairs={{28,12},{29,13},{30,14},{31,15}} | collective-permute-start | bytes 786440 | tf_op jit(solution)/shard_map/ppermute | solution.py:144
  40.0 66.5 %all-to-all-start.2 = ((bf16[32,24,1024]{2,1,0:T(8,128)(2,1)}), bf16[32,24,1024]{2,1,0:T(8,128)(2,1)}, u32[]{:S(2)}, u32[]{:S(2)}) async-start(bf16[32,24,1024]{2,1,0:T(8,128)(2,1)} %bitcast.275), calls=%async_computation.2 | async-start | bytes 3145728 | tf_op jit(solution)/shard_map/all_to_all | solution.py:838
  47.9 115.8 %all-gather.6.cloned.1.call-start = ((), (), s32[]{:S(2)}) async-start(), calls=%async_computation.9 | async-start | bytes 4718592 | tf_op jit(solution)/shard_map/all_gather | solution.py:204
  51.9 161.6 %all-gather.8.cloned.1.call-start = ((), (), s32[]{:S(2)}) async-start(), calls=%async_computation.10 | async-start | bytes 2359296 | tf_op jit(solution)/shard_map/all_gather | solution.py:204
  53.3 49.9 %collective-permute-start.7 = (bf16[128,1024]{1,0:T(8,128)(2,1)S(1)}, bf16[128,1024]{1,0:T(8,128)(2,1)S(1)}, u32[]{:S(2)}, u32[]{:S(2)}) collective-permute-start(bf16[128,1024]{1,0:T(8,128)(2,1)S(1)} %broadcast_select_fusion.1), channel_id=1, source_target_pairs={{28,24},{12,8},{20,16},{4,0},{29,25},{13,9},{21,17},{5,1},{30,26},... | collective-permute-start | bytes 786440 | tf_op jit(solution)/shard_map/ppermute | solution.py:144
  104.0 8.3 %collective-permute-start.8 = (bf16[128,1024]{1,0:T(8,128)(2,1)S(1)}, bf16[128,1024]{1,0:T(8,128)(2,1)}, u32[]{:S(2)}, u32[]{:S(2)}) collective-permute-start(bf16[128,1024]{1,0:T(8,128)(2,1)S(1)} %broadcast_select_fusion.2), channel_id=1, source_target_pairs={{0,2},{2,0},{1,3},{3,1},{4,6},{6,4},{5,7},{7,5},{8,10},{10,8},{9,1... | collective-permute-start | bytes 786440 | tf_op jit(solution)/shard_map/ppermute | solution.py:67
  115.5 14.4 %collective-permute-start.10 = (bf16[256,1024]{1,0:T(8,128)(2,1)S(1)}, bf16[256,1024]{1,0:T(8,128)(2,1)}, u32[]{:S(2)}, u32[]{:S(2)}) collective-permute-start(bf16[256,1024]{1,0:T(8,128)(2,1)S(1)} %fusion.53), channel_id=1, source_target_pairs={{0,2},{2,0},{1,3},{3,1},{4,6},{6,4},{5,7},{7,5},{8,10},{10,8},{9,1... | collective-permute-start | bytes 1572872 | tf_op jit(solution)/shard_map/ppermute | solution.py:67
  141.4 146.6 %all-gather.10.cloned.1.call-start = ((), (), s32[]{:S(2)}) async-start(), calls=%async_computation.11 | async-start | bytes 4718592 | tf_op jit(solution)/shard_map/all_gather | solution.py:204
  143.8 14.1 %collective-permute-start.14 = (bf16[256,1024]{1,0:T(8,128)(2,1)S(1)}, bf16[256,1024]{1,0:T(8,128)(2,1)S(1)}, u32[]{:S(2)}, u32[]{:S(2)}) collective-permute-start(bf16[256,1024]{1,0:T(8,128)(2,1)S(1)} %fusion.50), channel_id=1, source_target_pairs={{0,2},{2,0},{1,3},{3,1},{4,6},{6,4},{5,7},{7,5},{8,10},{10,8},{9,1... | collective-permute-start | bytes 1572872 | tf_op jit(solution)/shard_map/ppermute | solution.py:67
  146.8 11.1 %collective-permute-start.13 = (bf16[256,1024]{1,0:T(8,128)(2,1)S(1)}, bf16[256,1024]{1,0:T(8,128)(2,1)S(1)}, u32[]{:S(2)}, u32[]{:S(2)}) collective-permute-start(bf16[256,1024]{1,0:T(8,128)(2,1)S(1)} %slice.783), channel_id=1, source_target_pairs={{0,1},{1,0},{2,3},{3,2},{4,5},{5,4},{6,7},{7,6},{8,9},{9,8},{10,11... | collective-permute-start | bytes 1572872 | tf_op jit(solution)/shard_map/ppermute | solution.py:67
  160.4 14.7 %collective-permute-start.16 = (bf16[256,1024]{1,0:T(8,128)(2,1)}, bf16[256,1024]{1,0:T(8,128)(2,1)}, u32[]{:S(2)}, u32[]{:S(2)}) collective-permute-start(bf16[256,1024]{1,0:T(8,128)(2,1)} %fusion.54), channel_id=1, source_target_pairs={{0,2},{2,0},{1,3},{3,1},{4,6},{6,4},{5,7},{7,5},{8,10},{10,8},{9,1... | collective-permute-start | bytes 1572872 | tf_op jit(solution)/shard_map/ppermute | solution.py:67
  189.9 296.8 %reduce-scatter.3.cloned.1.call-start = ((), (), s32[]{:S(2)}) async-start(), calls=%async_computation.12 | async-start | bytes 4718592 | tf_op jit(solution)/shard_map/reduce_scatter | solution.py:999
  192.7 14.0 %collective-permute-start.20 = (bf16[256,1024]{1,0:T(8,128)(2,1)S(1)}, bf16[256,1024]{1,0:T(8,128)(2,1)S(1)}, u32[]{:S(2)}, u32[]{:S(2)}) collective-permute-start(bf16[256,1024]{1,0:T(8,128)(2,1)S(1)} %fusion.46), channel_id=1, source_target_pairs={{0,2},{2,0},{1,3},{3,1},{4,6},{6,4},{5,7},{7,5},{8,10},{10,8},{9,1... | collective-permute-start | bytes 1572872 | tf_op jit(solution)/shard_map/ppermute | solution.py:67
  198.2 8.6 %collective-permute-start.19 = (bf16[256,1024]{1,0:T(8,128)(2,1)S(1)}, bf16[256,1024]{1,0:T(8,128)(2,1)S(1)}, u32[]{:S(2)}, u32[]{:S(2)}) collective-permute-start(bf16[256,1024]{1,0:T(8,128)(2,1)S(1)} %slice.781), channel_id=1, source_target_pairs={{0,1},{1,0},{2,3},{3,2},{4,5},{5,4},{6,7},{7,6},{8,9},{9,8},{10,11... | collective-permute-start | bytes 1572872 | tf_op jit(solution)/shard_map/ppermute | solution.py:67
  209.3 14.7 %collective-permute-start.22 = (bf16[256,1024]{1,0:T(8,128)(2,1)}, bf16[256,1024]{1,0:T(8,128)(2,1)}, u32[]{:S(2)}, u32[]{:S(2)}) collective-permute-start(bf16[256,1024]{1,0:T(8,128)(2,1)} %fusion.55), channel_id=1, source_target_pairs={{0,2},{2,0},{1,3},{3,1},{4,6},{6,4},{5,7},{7,5},{8,10},{10,8},{9,1... | collective-permute-start | bytes 1572872 | tf_op jit(solution)/shard_map/ppermute | solution.py:67
  235.3 14.0 %collective-permute-start.26 = (bf16[256,1024]{1,0:T(8,128)(2,1)S(1)}, bf16[256,1024]{1,0:T(8,128)(2,1)S(1)}, u32[]{:S(2)}, u32[]{:S(2)}) collective-permute-start(bf16[256,1024]{1,0:T(8,128)(2,1)S(1)} %fusion.42), channel_id=1, source_target_pairs={{0,2},{2,0},{1,3},{3,1},{4,6},{6,4},{5,7},{7,5},{8,10},{10,8},{9,1... | collective-permute-start | bytes 1572872 | tf_op jit(solution)/shard_map/ppermute | solution.py:67
  238.3 11.0 %collective-permute-start.25 = (bf16[256,1024]{1,0:T(8,128)(2,1)S(1)}, bf16[256,1024]{1,0:T(8,128)(2,1)S(1)}, u32[]{:S(2)}, u32[]{:S(2)}) collective-permute-start(bf16[256,1024]{1,0:T(8,128)(2,1)S(1)} %slice.779), channel_id=1, source_target_pairs={{0,1},{1,0},{2,3},{3,2},{4,5},{5,4},{6,7},{7,6},{8,9},{9,8},{10,11... | collective-permute-start | bytes 1572872 | tf_op jit(solution)/shard_map/ppermute | solution.py:67
  252.0 42.3 %collective-permute-start.28 = (bf16[256,1024]{1,0:T(8,128)(2,1)}, bf16[256,1024]{1,0:T(8,128)(2,1)}, u32[]{:S(2)}, u32[]{:S(2)}) collective-permute-start(bf16[256,1024]{1,0:T(8,128)(2,1)} %fusion.56), channel_id=1, source_target_pairs={{0,2},{2,0},{1,3},{3,1},{4,6},{6,4},{5,7},{7,5},{8,10},{10,8},{9,1... | collective-permute-start | bytes 1572872 | tf_op jit(solution)/shard_map/ppermute | solution.py:67
  308.9 14.3 %collective-permute-start.32 = (bf16[256,1024]{1,0:T(8,128)(2,1)}, bf16[256,1024]{1,0:T(8,128)(2,1)}, u32[]{:S(2)}, u32[]{:S(2)}) collective-permute-start(bf16[256,1024]{1,0:T(8,128)(2,1)} %fusion.38), channel_id=1, source_target_pairs={{0,2},{2,0},{1,3},{3,1},{4,6},{6,4},{5,7},{7,5},{8,10},{10,8},{9,1... | collective-permute-start | bytes 1572872 | tf_op jit(solution)/shard_map/ppermute | solution.py:67
  316.3 6.8 collective-permute-start.31
  353.8 14.3 %collective-permute-start.39 = (bf16[256,1024]{1,0:T(8,128)(2,1)S(1)}, bf16[256,1024]{1,0:T(8,128)(2,1)S(1)}, u32[]{:S(2)}, u32[]{:S(2)}) collective-permute-start(bf16[256,1024]{1,0:T(8,128)(2,1)S(1)} %get-tuple-element.516), channel_id=1, source_target_pairs={{0,2},{2,0},{1,3},{3,1},{4,6},{6,4},{5,7},{7,5},{8,10},{10,8},{9,1... | collective-permute-start | bytes 1572872 | tf_op jit(solution)/shard_map/ppermute | solution.py:67
  381.0 20.0 %collective-permute-start.43 = (bf16[256,1024]{1,0:T(8,128)(2,1)}, bf16[256,1024]{1,0:T(8,128)(2,1)}, u32[]{:S(2)}, u32[]{:S(2)}) collective-permute-start(bf16[256,1024]{1,0:T(8,128)(2,1)} %fusion.34), channel_id=1, source_target_pairs={{0,2},{2,0},{1,3},{3,1},{4,6},{6,4},{5,7},{7,5},{8,10},{10,8},{9,1... | collective-permute-start | bytes 1572872 | tf_op jit(solution)/shard_map/ppermute | solution.py:67
  401.0 280.9 %reduce-scatter.5.cloned.1.call-start = ((), (), s32[]{:S(2)}) async-start(), calls=%async_computation.13 | async-start | bytes 5898240 | tf_op jit(solution)/shard_map/reduce_scatter | solution.py:999
  405.6 13.9 %collective-permute-start.45 = (bf16[256,1024]{1,0:T(8,128)(2,1)S(1)}, bf16[256,1024]{1,0:T(8,128)(2,1)S(1)}, u32[]{:S(2)}, u32[]{:S(2)}) collective-permute-start(bf16[256,1024]{1,0:T(8,128)(2,1)S(1)} %get-tuple-element.518), channel_id=1, source_target_pairs={{0,2},{2,0},{1,3},{3,1},{4,6},{6,4},{5,7},{7,5},{8,10},{10,8},{9,1... | collective-permute-start | bytes 1572872 | tf_op jit(solution)/shard_map/ppermute | solution.py:67
  438.3 14.2 %collective-permute-start.49 = (bf16[256,1024]{1,0:T(8,128)(2,1)S(1)}, bf16[256,1024]{1,0:T(8,128)(2,1)S(1)}, u32[]{:S(2)}, u32[]{:S(2)}) collective-permute-start(bf16[256,1024]{1,0:T(8,128)(2,1)S(1)} %copy-done.138), channel_id=1, source_target_pairs={{0,2},{2,0},{1,3},{3,1},{4,6},{6,4},{5,7},{7,5},{8,10},{10,8},{9,1... | collective-permute-start | bytes 1572872 | tf_op jit(solution)/shard_map/ppermute | solution.py:67
  453.8 14.3 %collective-permute-start.51 = (bf16[256,1024]{1,0:T(8,128)(2,1)S(1)}, bf16[256,1024]{1,0:T(8,128)(2,1)S(1)}, u32[]{:S(2)}, u32[]{:S(2)}) collective-permute-start(bf16[256,1024]{1,0:T(8,128)(2,1)S(1)} %get-tuple-element.520), channel_id=1, source_target_pairs={{0,2},{2,0},{1,3},{3,1},{4,6},{6,4},{5,7},{7,5},{8,10},{10,8},{9,1... | collective-permute-start | bytes 1572872 | tf_op jit(solution)/shard_map/ppermute | solution.py:67
  481.1 24.3 %collective-permute-start.55 = (bf16[256,1024]{1,0:T(8,128)(2,1)}, bf16[256,1024]{1,0:T(8,128)(2,1)}, u32[]{:S(2)}, u32[]{:S(2)}) collective-permute-start(bf16[256,1024]{1,0:T(8,128)(2,1)} %fusion.28), channel_id=1, source_target_pairs={{0,2},{2,0},{1,3},{3,1},{4,6},{6,4},{5,7},{7,5},{8,10},{10,8},{9,1... | collective-permute-start | bytes 1572872 | tf_op jit(solution)/shard_map/ppermute | solution.py:67
  510.2 14.0 %collective-permute-start.57 = (bf16[256,1024]{1,0:T(8,128)(2,1)S(1)}, bf16[256,1024]{1,0:T(8,128)(2,1)}, u32[]{:S(2)}, u32[]{:S(2)}) collective-permute-start(bf16[256,1024]{1,0:T(8,128)(2,1)S(1)} %get-tuple-element.522), channel_id=1, source_target_pairs={{0,2},{2,0},{1,3},{3,1},{4,6},{6,4},{5,7},{7,5},{8,10},{10,8},{9,1... | collective-permute-start | bytes 1572872 | tf_op jit(solution)/shard_map/ppermute | solution.py:67
  538.3 11.8 %collective-permute-start.59 = (bf16[256,1024]{1,0:T(8,128)(2,1)}, bf16[256,1024]{1,0:T(8,128)(2,1)}, u32[]{:S(2)}, u32[]{:S(2)}) collective-permute-start(bf16[256,1024]{1,0:T(8,128)(2,1)} %slice.770), channel_id=1, source_target_pairs={{0,1},{1,0},{2,3},{3,2},{4,5},{5,4},{6,7},{7,6},{8,9},{9,8},{10,11... | collective-permute-start | bytes 1572872 | tf_op jit(solution)/shard_map/ppermute | solution.py:67
  556.8 14.5 %collective-permute-start.61 = (bf16[256,1024]{1,0:T(8,128)(2,1)}, bf16[256,1024]{1,0:T(8,128)(2,1)S(1)}, u32[]{:S(2)}, u32[]{:S(2)}) collective-permute-start(bf16[256,1024]{1,0:T(8,128)(2,1)} %fusion.22), channel_id=1, source_target_pairs={{0,2},{2,0},{1,3},{3,1},{4,6},{6,4},{5,7},{7,5},{8,10},{10,8},{9,1... | collective-permute-start | bytes 1572872 | tf_op jit(solution)/shard_map/ppermute | solution.py:67
  561.8 8.6 %collective-permute-start.60 = (bf16[256,1024]{1,0:T(8,128)(2,1)}, bf16[256,1024]{1,0:T(8,128)(2,1)}, u32[]{:S(2)}, u32[]{:S(2)}) collective-permute-start(bf16[256,1024]{1,0:T(8,128)(2,1)} %slice.769), channel_id=1, source_target_pairs={{0,1},{1,0},{2,3},{3,2},{4,5},{5,4},{6,7},{7,6},{8,9},{9,8},{10,11... | collective-permute-start | bytes 1572872 | tf_op jit(solution)/shard_map/ppermute | solution.py:67
  563.2 59.4 %collective-permute-start.62 = (bf16[2,2,3,256,256]{4,3,2,1,0:T(8,128)(2,1)}, bf16[2,2,3,256,256]{4,3,2,1,0:T(8,128)(2,1)}, u32[]{:S(2)}, u32[]{:S(2)}) collective-permute-start(bf16[2,2,3,256,256]{4,3,2,1,0:T(8,128)(2,1)} %dynamic-slice_bitcast_fusion), channel_id=1, source_target_pairs={{0,4},{4,0},{8,12},{12,8},{16,20},{20,16},{24,28},{28,24},{1,5},{5... | collective-permute-start | bytes 4718600 | tf_op jit(solution)/shard_map/ppermute | solution.py:67
  564.7 60.6 %all-to-all-start.3 = ((bf16[8,2,4,32,256]{4,3,2,1,0:T(8,128)(2,1)}), bf16[8,2,4,32,256]{4,3,2,1,0:T(8,128)(2,1)}, u32[]{:S(2)}, u32[]{:S(2)}) async-start(bf16[8,2,4,32,256]{4,3,2,1,0:T(8,128)(2,1)} %shard_map.422), calls=%async_computation.4 | async-start | bytes 2097152 | tf_op jit(solution)/shard_map/all_to_all | solution.py:1040
  625.4 7.9 collective-permute-start.64
  628.6 53.3 %all-to-all-start.4 = ((bf16[32,24,1024]{2,1,0:T(8,128)(2,1)}), bf16[32,24,1024]{2,1,0:T(8,128)(2,1)}, u32[]{:S(2)}, u32[]{:S(2)}) async-start(bf16[32,24,1024]{2,1,0:T(8,128)(2,1)} %bitcast.276), calls=%async_computation.5 | async-start | bytes 3145728 | tf_op jit(solution)/shard_map/all_to_all | solution.py:838
  633.5 17.4 %collective-permute-start.65 = (bf16[128,1024]{1,0:T(8,128)(2,1)S(1)}, bf16[128,1024]{1,0:T(8,128)(2,1)S(1)}, u32[]{:S(2)}, u32[]{:S(2)}) collective-permute-start(bf16[128,1024]{1,0:T(8,128)(2,1)S(1)} %get-tuple-element.506), channel_id=1, source_target_pairs={{24,28},{8,12},{16,20},{0,4},{25,29},{9,13},{17,21},{1,5},{26,30},... | collective-permute-start | bytes 786440 | tf_op jit(solution)/shard_map/ppermute | solution.py:167
  653.3 26.5 %collective-permute-start.63 = (bf16[2,3,256,256]{3,2,1,0:T(8,128)(2,1)S(1)}, bf16[2,3,256,256]{3,2,1,0:T(8,128)(2,1)S(1)}, u32[]{:S(2)}, u32[]{:S(2)}) collective-permute-start(bf16[2,3,256,256]{3,2,1,0:T(8,128)(2,1)S(1)} %dynamic-slice_bitcast_fusion.1), channel_id=1, source_target_pairs={{0,8},{4,12},{8,0},{12,4},{16,24},{20,28},{24,16},{28,20},{1,9},{5... | collective-permute-start | bytes 2359304 | tf_op jit(solution)/shard_map/ppermute | solution.py:67
  656.2 24.5 %collective-permute-start.69 = (bf16[256,1024]{1,0:T(8,128)(2,1)S(1)}, bf16[256,1024]{1,0:T(8,128)(2,1)S(1)}, u32[]{:S(2)}, u32[]{:S(2)}) collective-permute-start(bf16[256,1024]{1,0:T(8,128)(2,1)S(1)} %pad_maximum_fusion.11), channel_id=1, source_target_pairs={{0,1},{1,0},{2,3},{3,2},{4,5},{5,4},{6,7},{7,6},{8,9},{9,8},{10,11... | collective-permute-start | bytes 1572872 | tf_op jit(solution)/shard_map/ppermute | solution.py:67
  682.6 19.4 %collective-permute-start.70 = (bf16[3,256,256]{2,1,0:T(8,128)(2,1)}, bf16[3,256,256]{2,1,0:T(8,128)(2,1)}, u32[]{:S(2)}, u32[]{:S(2)}) collective-permute-start(bf16[3,256,256]{2,1,0:T(8,128)(2,1)} %dynamic-slice_bitcast_fusion.2), channel_id=1, source_target_pairs={{0,16},{4,20},{8,24},{12,28},{16,0},{20,4},{24,8},{28,12},{1,17},{... | collective-permute-start | bytes 1179656 | tf_op jit(solution)/shard_map/ppermute | solution.py:67
  714.8 5.9 collective-permute-start.72
  720.7 17.3 %collective-permute-start.73 = (f32[27653]{0:T(1024)S(1)}, f32[27653]{0:T(1024)S(1)}, u32[]{:S(2)}, u32[]{:S(2)}) collective-permute-start(f32[27653]{0:T(1024)S(1)} %add.913), channel_id=1, source_target_pairs={{0,4},{4,0},{8,12},{12,8},{16,20},{20,16},{24,28},{28,24},{1,5},{5... | collective-permute-start | bytes 331844 | tf_op jit(solution)/shard_map/ppermute | solution.py:67
  738.1 6.1 collective-permute-start.74
  744.2 9.0 %collective-permute-start.75 = (f32[27653]{0:T(1024)S(1)}, f32[27653]{0:T(1024)S(1)}, u32[]{:S(2)}, u32[]{:S(2)}) collective-permute-start(f32[27653]{0:T(1024)S(1)} %add.915), channel_id=1, source_target_pairs={{0,16},{4,20},{8,24},{12,28},{16,0},{20,4},{24,8},{28,12},{1,17},{... | collective-permute-start | bytes 331844 | tf_op jit(solution)/shard_map/ppermute | solution.py:67
  745.8 23.5 %all-to-all-start.5 = ((bf16[8,2,3,32,256]{4,3,2,1,0:T(8,128)(2,1)}), bf16[8,2,3,32,256]{4,3,2,1,0:T(8,128)(2,1)S(1)}, u32[]{:S(2)}, u32[]{:S(2)}) async-start(bf16[8,2,3,32,256]{4,3,2,1,0:T(8,128)(2,1)} %shard_map.426), calls=%async_computation.7 | async-start | bytes 1572864 | tf_op jit(solution)/shard_map/all_to_all | solution.py:1040
  770.2 33.1 %all-to-all-start.6 = ((bf16[8,2,5,32,256]{4,3,2,1,0:T(8,128)(2,1)}), bf16[8,2,5,32,256]{4,3,2,1,0:T(8,128)(2,1)S(1)}, u32[]{:S(2)}, u32[]{:S(2)}) async-start(bf16[8,2,5,32,256]{4,3,2,1,0:T(8,128)(2,1)} %shard_map.425), calls=%async_computation.8 | async-start | bytes 2621440 | tf_op jit(solution)/shard_map/all_to_all | solution.py:1040
  (251 other events, 1541.1 us)
Sparse Core Ops, SparseCore 0:
  15.9 68.3 all-gather.11
  87.0 76.2 all-gather.5
  165.9 47.5 all-gather.7
  216.1 71.8 all-gather.9
  401.1 85.6 reduce-scatter.2
  505.4 122.7 reduce-scatter.4

commit v5 on v4

--- a/solution.py
+++ b/solution.py
@@ -212,21 +212,21 @@
         in_proj[layer_no].reshape(row_blocks, 3, rows, width).transpose(1, 0, 2, 3),
         out_proj[layer_no].reshape(1, row_blocks, rows, width),
     ]
-    feed_rows = [
-        up_proj[layer_no].reshape(row_blocks, feed, rows, width),
-        down_proj[layer_no].reshape(feed, row_blocks, rows, width),
+    return [
+        jnp.concatenate(attend_rows, axis=0).astype(BF),
+        up_proj[layer_no].reshape(row_blocks, feed, rows, width).astype(BF),
+        down_proj[layer_no].reshape(feed, row_blocks, rows, width).astype(BF),
     ]
-    return [jnp.concatenate(rows, axis=0).astype(BF) for rows in (attend_rows, feed_rows)]
-
-
-def named_layer(attend_all, feed_all, row_blocks, feed):
+
+
+def named_layer(attend_all, up_all, down_all, row_blocks, feed):
     of_x = (1, attend_all.shape[1], 0)
     second = (3, row_blocks, 0)
     return (
         (attend_all, {"x": of_x, "low": (2, 3, 0), "high": second}),
         (attend_all, {"x": of_x, "low": second, "high": (2, 1, 3)}),
-        (feed_all, {"x": of_x, "low": second, "high": (2, row_blocks, 0)}),
-        (feed_all, {"x": of_x, "low": second, "high": (2, feed, row_blocks)}),
+        (up_all[0], {"x": of_x, "low": second, "high": (2, row_blocks, up_all[1])}),
+        (down_all[0], {"x": of_x, "low": second, "high": (2, feed, down_all[1])}),
     )
 
 
@@ -794,10 +794,14 @@
         for which in (rank, rank ^ 1)
     ]
 
-    rows_here = [
+    (attend_0, up_0, down_0), (attend_1, up_1, down_1) = [
         layer_rows(in_proj, out_proj, up_proj, down_proj, layer_no) for layer_no in range(layers)
     ]
-    rows_here[0][0], token_ids = lax.optimization_barrier((rows_here[0][0], token_ids))
+    rows_here = [
+        jnp.concatenate(members, axis=0)
+        for members in ((attend_0, up_0), (attend_1, down_0), (up_1, down_1))
+    ]
+    rows_here[0], token_ids = lax.optimization_barrier((rows_here[0], token_ids))
 
     shard_rows = embed_table.shape[0]
     last_base = VOCAB - (devices - 1) * shard_rows
@@ -867,13 +871,13 @@
         rows = rows + lookup(VOCAB + jnp.arange(rows.shape[0]) % seq_slots)
         return lax.psum_scatter(rows, ("x", "core"), scatter_dimension=0, tiled=True).astype(F32)
 
-    fetched = [[fetch(rows) for rows in of_layer] for of_layer in rows_here]
+    fetched = [fetch(rows) for rows in rows_here]
     if places_last:
         place_rows = spread_from(place_rows, hops[0])
         filled, place_rows = lax.optimization_barrier((rows_to_send(0), place_rows))
         for step in hops[1:]:
             place_rows = spread_from(place_rows, step)
-        reached, fetched[0][0] = lax.optimization_barrier((exchange(filled), fetched[0][0]))
+        reached, fetched[0] = lax.optimization_barrier((exchange(filled), fetched[0]))
         token_rows = lax.fori_loop(
             1,
             rounds,
@@ -905,8 +909,13 @@
     residual = layer_norm(embedded, gain_embed, shift_embed)
     kept_all = []
     weights_all = []
+    first, middle, last = fetched
+    placed_at = (
+        (first, (first, 4), (middle, 4)),
+        (middle, (last, 0), (last, row_blocks)),
+    )
     for layer_no in range(layers):
-        weights = named_layer(*fetched[layer_no], row_blocks, feed_blocks)
+        weights = named_layer(*placed_at[layer_no], row_blocks, feed_blocks)
         residual, kept_values = layer_forward(
             residual, weights, pieces_of(layer_no), keys_live
         )

time: 829 us -> 820 us (0.989)
  local copies, waits for them, and re-layouts: 84.7 us -> 72.1 us
  Pallas kernels: 157 us -> 169 us
    all_gather x4 -> x3, waiting for transfers between devices: 32.8 us -> 20 us  [fetch(): return lax.all_gather(pieces, 'dp', axis=0, tiled=False)[:, None]]
    pallas_call x32, Pallas kernels: 82.3 us -> 94.8 us  [rows_product(): pl.pallas_call(kernel, grid=(steps,), in_specs=[whole(left.shape), pl.Blo...]
    unnamed x444 -> x402, local copies, waits for them, and re-layouts: 44.9 us -> 33.6 us
    ppermute x3, waiting for transfers between devices: 44.7 us -> 55.8 us  [spread_from(): found = lax.ppermute(value, 'dp', step)]
    ppermute x68, waiting for transfers between devices: 215 us -> 206 us  [from_peer(): return lax.ppermute(values, axis, [(at, at ^ mask) for at in range(size)])]
  transfers between devices with their start and end apart: 87 -> 86, of which waited for: 59 -> 57; matrix products, arithmetic and copies ran while one was open for 18% -> 17% of each run, Pallas kernels for 16% -> 18%
where the time goes in v5:
time: 820 us; the launch traced here: 811 us
  waiting for transfers between devices  323 us (39%)
  Pallas kernels  169 us (21%)
  starting transfers between devices  101 us (12%)
  other arithmetic  99.3 us (12%)
  local copies, waits for them, and re-layouts  72.1 us (9%)
  between operations  24.2 us (3%)
  matrix products  21.2 us (3%)
    ppermute x68, waiting for transfers between devices, from_peer(): return lax.ppermute(values, axis, [(at, at ^ mask) for at in range(size)])  206 us
    pallas_call x32, Pallas kernels, rows_product(): pl.pallas_call(kernel, grid=(steps,), in_specs=[whole(left.shape), pl.Blo...  94.8 us
    ppermute x68, starting transfers between devices, from_peer(): return lax.ppermute(values, axis, [(at, at ^ mask) for at in range(size)])  62.5 us
    ppermute x3, waiting for transfers between devices, spread_from(): found = lax.ppermute(value, 'dp', step)  55.8 us
    pallas_call x8, Pallas kernels, attend(): pl.pallas_call(body, grid=(seqs, pairs), in_specs=specs, out_specs=out_sp...  34 us
    unnamed x402, local copies, waits for them, and re-layouts  33.6 us
    pallas_call x8, Pallas kernels, block_grads(): pl.pallas_call(kernel, grid=(high,), in_specs=[whole(member.shape) for me...  22.7 us
    all_gather x3, waiting for transfers between devices, fetch(): return lax.all_gather(pieces, 'dp', axis=0, tiled=False)[:, None]  20 us
  transfers between devices with their start and end apart: 86, of which 57 were waited for; matrix products, arithmetic and copies ran while one was open for 17% of the time, Pallas kernels for 18%

profile of v5, /device:TPU:0, one launch (start us, length us, event | category | flops | bytes accessed | tf_op | source)
XLA Modules:
  0.0 810.7 jit_solution(13487718440631360372)
XLA Ops:
  33.8 6.7 gather_fusion.1
  43.5 9.1 %all-to-all-start.2 = ((bf16[32,24,1024]{2,1,0:T(8,128)(2,1)}), bf16[32,24,1024]{2,1,0:T(8,128)(2,1)}, u32[]{:S(2)}, u32[]{:S(2)}) async-start(bf16[32,24,1024]{2,1,0:T(8,128)(2,1)} %bitcast.282), calls=%async_computation.2 | async-start | bytes 3145728 | tf_op jit(solution)/shard_map/all_to_all | solution.py:842
  60.8 55.8 %collective-permute-done.7 = bf16[128,1024]{1,0:T(8,128)(2,1)S(1)} collective-permute-done((bf16[128,1024]{1,0:T(8,128)(2,1)S(1)}, bf16[128,1024]{1,0:T(8,128)(2,1)S(1)}, u32[]{:S(2)}, u32[]{:S(2)}) %collective-permute-start.7) | collective-permute-done | bytes 262176 | tf_op jit(solution)/shard_map/ppermute | solution.py:144
  159.4 9.7 %collective-permute-done.14 = bf16[256,1024]{1,0:T(8,128)(2,1)S(1)} collective-permute-done((bf16[256,1024]{1,0:T(8,128)(2,1)S(1)}, bf16[256,1024]{1,0:T(8,128)(2,1)S(1)}, u32[]{:S(2)}, u32[]{:S(2)}) %collective-permute-start.14) | collective-permute-done | bytes 524320 | tf_op jit(solution)/shard_map/ppermute | solution.py:67
  177.4 7.3 collective-permute-done.16
  193.7 5.7 all-gather.9.cloned.1.call-done
  213.9 8.8 %collective-permute-done.20 = bf16[256,1024]{1,0:T(8,128)(2,1)S(1)} collective-permute-done((bf16[256,1024]{1,0:T(8,128)(2,1)S(1)}, bf16[256,1024]{1,0:T(8,128)(2,1)S(1)}, u32[]{:S(2)}, u32[]{:S(2)}) %collective-permute-start.20) | collective-permute-done | bytes 524320 | tf_op jit(solution)/shard_map/ppermute | solution.py:67
  231.7 6.5 collective-permute-done.22
  254.4 9.7 %collective-permute-done.26 = bf16[256,1024]{1,0:T(8,128)(2,1)S(1)} collective-permute-done((bf16[256,1024]{1,0:T(8,128)(2,1)S(1)}, bf16[256,1024]{1,0:T(8,128)(2,1)S(1)}, u32[]{:S(2)}, u32[]{:S(2)}) %collective-permute-start.26) | collective-permute-done | bytes 524320 | tf_op jit(solution)/shard_map/ppermute | solution.py:67
  267.6 14.0 %all-gather.11.cloned.1.call-done = bf16[64,4,32,256]{3,2,1,0:T(8,128)(2,1)} async-done(((bf16[8,4,32,256]{3,2,1,0:T(8,128)(2,1)}), bf16[64,4,32,256]{3,2,1,0:T(8,128)(2,1)}) %all-gather.11.cloned.1.call-update) | async-done | bytes 4194320 | tf_op jit(solution)/shard_map/all_gather | solution.py:204
  288.6 4.1 shard_map.392
  294.1 3.9 shard_map.393
  309.6 5.7 collective-permute-done.32
  350.2 8.5 %collective-permute-done.39 = bf16[256,1024]{1,0:T(8,128)(2,1)S(1)} collective-permute-done((bf16[256,1024]{1,0:T(8,128)(2,1)S(1)}, bf16[256,1024]{1,0:T(8,128)(2,1)S(1)}, u32[]{:S(2)}, u32[]{:S(2)}) %collective-permute-start.39) | collective-permute-done | bytes 524320 | tf_op jit(solution)/shard_map/ppermute | solution.py:67
  364.5 4.0 shard_map.398
  373.0 3.9 shard_map.399
  376.9 3.9 shard_map.400
  398.4 5.3 shard_map.403.refs_2_.refs_0_
  403.7 5.8 collective-permute-done.45
  412.6 5.1 shard_map.405.refs_0_.refs_3_
  428.7 3.9 shard_map.409
  432.8 5.0 collective-permute-done.49
  445.0 8.5 %collective-permute-done.51 = bf16[256,1024]{1,0:T(8,128)(2,1)S(1)} collective-permute-done((bf16[256,1024]{1,0:T(8,128)(2,1)S(1)}, bf16[256,1024]{1,0:T(8,128)(2,1)S(1)}, u32[]{:S(2)}, u32[]{:S(2)}) %collective-permute-start.51) | collective-permute-done | bytes 524320 | tf_op jit(solution)/shard_map/ppermute | solution.py:67
  459.3 4.1 shard_map.412
  467.1 3.9 shard_map.413
  471.0 6.2 reduce-scatter.3.cloned.1.call-done.block_ref
  478.4 4.3 shard_map.414
  500.9 5.1 shard_map.417.refs_2_.refs_0_
  507.0 4.6 collective-permute-done.57
  517.3 5.1 shard_map.419.refs_0_.refs_3_
  534.1 4.5 shard_map.422
  548.2 3.9 shard_map.424
  555.8 4.2 all-to-all-start.3
  566.6 43.7 %collective-permute-done.62 = bf16[2,2,3,256,256]{4,3,2,1,0:T(8,128)(2,1)} collective-permute-done((bf16[2,2,3,256,256]{4,3,2,1,0:T(8,128)(2,1)}, bf16[2,2,3,256,256]{4,3,2,1,0:T(8,128)(2,1)}, u32[]{:S(2)}, u32[]{:S(2)}) %collective-permute-start.62) | collective-permute-done | bytes 1572896 | tf_op jit(solution)/shard_map/ppermute | solution.py:67
  619.2 3.8 all-to-all-start.4
  628.3 13.1 %collective-permute-done.65 = bf16[128,1024]{1,0:T(8,128)(2,1)S(1)} collective-permute-done((bf16[128,1024]{1,0:T(8,128)(2,1)S(1)}, bf16[128,1024]{1,0:T(8,128)(2,1)S(1)}, u32[]{:S(2)}, u32[]{:S(2)}) %collective-permute-start.65) | collective-permute-done | bytes 262176 | tf_op jit(solution)/shard_map/ppermute | solution.py:167
  647.0 23.3 %collective-permute-done.63 = bf16[2,3,256,256]{3,2,1,0:T(8,128)(2,1)S(1)} collective-permute-done((bf16[2,3,256,256]{3,2,1,0:T(8,128)(2,1)S(1)}, bf16[2,3,256,256]{3,2,1,0:T(8,128)(2,1)S(1)}, u32[]{:S(2)}, u32[]{:S(2)}) %collective-permute-start.63) | collective-permute-done | bytes 786464 | tf_op jit(solution)/shard_map/ppermute | solution.py:67
  675.7 5.1 fusion.14
  680.9 4.2 fusion.17
  685.1 6.6 shard_map.425
  695.6 4.4 shard_map.426
  713.1 14.4 %collective-permute-start.73 = (f32[27653]{0:T(1024)S(1)}, f32[27653]{0:T(1024)S(1)}, u32[]{:S(2)}, u32[]{:S(2)}) collective-permute-start(f32[27653]{0:T(1024)S(1)} %add.913), channel_id=1, source_target_pairs={{0,4},{4,0},{8,12},{12,8},{16,20},{20,16},{24,28},{28,24},{1,5},{5... | collective-permute-start | bytes 331844 | tf_op jit(solution)/shard_map/ppermute | solution.py:67
  738.0 7.5 all-to-all-start.5
  752.6 4.2 fusion.13
  756.8 4.7 all-to-all-done.5
  766.0 4.5 fusion.12
  771.5 8.2 %multiply_subtract_fusion = (f32[976,1024]{1,0:T(8,128)}, f32[976,1024]{1,0:T(8,128)}, f32[976,1024]{1,0:T(8,128)}) fusion(f32[976,1024]{1,0:T(8,128)S(1)} %copy-done.84, f32[976,1024]{1,0:T(8,128)S(1)} %copy-done.100, f32[]{:T(128)S(6)} %div.257, f32[976,1024]{1,0:T(8,128)} %param.35, f32[976,1024]{1,0:T(8,128)} %param.36), kind=kLoop, calls=%fused_computation.36 | loop fusion | flops 15990784 | bytes 27983876 | tf_op jit(solution)/shard_map/sub | solution.py:59
  781.9 13.6 %all-to-all-done.6 = bf16[8,2,5,32,256]{4,3,2,1,0:T(8,128)(2,1)S(1)} async-done(((bf16[8,2,5,32,256]{4,3,2,1,0:T(8,128)(2,1)}), bf16[8,2,5,32,256]{4,3,2,1,0:T(8,128)(2,1)S(1)}, u32[]{:S(2)}, u32[]{:S(2)}) %all-to-all-start.6) | async-done | bytes 1310752 | tf_op jit(solution)/shard_map/all_to_all | solution.py:1049
  (821 shorter events, 378.2 us)
Async XLA Ops:
  7.2 117.0 %all-gather.7.cloned.1.call-start = ((), (), s32[]{:S(2)}) async-start(), calls=%async_computation.11 | async-start | bytes 4718592 | tf_op jit(solution)/shard_map/all_gather | solution.py:204
  14.0 6.9 collective-permute-start.3
  22.0 6.5 collective-permute-start.4
  33.1 10.3 %collective-permute-start.5 = (bf16[128,1024]{1,0:T(8,128)(2,1)S(1)}, bf16[128,1024]{1,0:T(8,128)(2,1)S(1)}, u32[]{:S(2)}, u32[]{:S(2)}) collective-permute-start(bf16[128,1024]{1,0:T(8,128)(2,1)S(1)} %slice_select_fusion.1), channel_id=1, source_target_pairs={{28,12},{29,13},{30,14},{31,15}} | collective-permute-start | bytes 786440 | tf_op jit(solution)/shard_map/ppermute | solution.py:144
  43.5 80.3 %all-to-all-start.2 = ((bf16[32,24,1024]{2,1,0:T(8,128)(2,1)}), bf16[32,24,1024]{2,1,0:T(8,128)(2,1)}, u32[]{:S(2)}, u32[]{:S(2)}) async-start(bf16[32,24,1024]{2,1,0:T(8,128)(2,1)} %bitcast.282), calls=%async_computation.2 | async-start | bytes 3145728 | tf_op jit(solution)/shard_map/all_to_all | solution.py:842
  52.6 146.8 %all-gather.9.cloned.1.call-start = ((), (), s32[]{:S(2)}) async-start(), calls=%async_computation.12 | async-start | bytes 4718592 | tf_op jit(solution)/shard_map/all_gather | solution.py:204
  54.2 227.4 %all-gather.11.cloned.1.call-start = ((), (), s32[]{:S(2)}) async-start(), calls=%async_computation.13 | async-start | bytes 4718592 | tf_op jit(solution)/shard_map/all_gather | solution.py:204
  55.6 61.0 %collective-permute-start.7 = (bf16[128,1024]{1,0:T(8,128)(2,1)S(1)}, bf16[128,1024]{1,0:T(8,128)(2,1)S(1)}, u32[]{:S(2)}, u32[]{:S(2)}) collective-permute-start(bf16[128,1024]{1,0:T(8,128)(2,1)S(1)} %broadcast_select_fusion.1), channel_id=1, source_target_pairs={{28,24},{12,8},{20,16},{4,0},{29,25},{13,9},{21,17},{5,1},{30,26},... | collective-permute-start | bytes 786440 | tf_op jit(solution)/shard_map/ppermute | solution.py:144
  118.0 8.2 %collective-permute-start.8 = (bf16[128,1024]{1,0:T(8,128)(2,1)}, bf16[128,1024]{1,0:T(8,128)(2,1)}, u32[]{:S(2)}, u32[]{:S(2)}) collective-permute-start(bf16[128,1024]{1,0:T(8,128)(2,1)} %broadcast_select_fusion.2), channel_id=1, source_target_pairs={{0,2},{2,0},{1,3},{3,1},{4,6},{6,4},{5,7},{7,5},{8,10},{10,8},{9,1... | collective-permute-start | bytes 786440 | tf_op jit(solution)/shard_map/ppermute | solution.py:67
  128.9 14.3 %collective-permute-start.10 = (bf16[256,1024]{1,0:T(8,128)(2,1)S(1)}, bf16[256,1024]{1,0:T(8,128)(2,1)S(1)}, u32[]{:S(2)}, u32[]{:S(2)}) collective-permute-start(bf16[256,1024]{1,0:T(8,128)(2,1)S(1)} %fusion.53), channel_id=1, source_target_pairs={{0,2},{2,0},{1,3},{3,1},{4,6},{6,4},{5,7},{7,5},{8,10},{10,8},{9,1... | collective-permute-start | bytes 1572872 | tf_op jit(solution)/shard_map/ppermute | solution.py:67
  155.1 14.0 %collective-permute-start.14 = (bf16[256,1024]{1,0:T(8,128)(2,1)S(1)}, bf16[256,1024]{1,0:T(8,128)(2,1)S(1)}, u32[]{:S(2)}, u32[]{:S(2)}) collective-permute-start(bf16[256,1024]{1,0:T(8,128)(2,1)S(1)} %fusion.50), channel_id=1, source_target_pairs={{0,2},{2,0},{1,3},{3,1},{4,6},{6,4},{5,7},{7,5},{8,10},{10,8},{9,1... | collective-permute-start | bytes 1572872 | tf_op jit(solution)/shard_map/ppermute | solution.py:67
  159.3 9.8 %collective-permute-start.13 = (bf16[256,1024]{1,0:T(8,128)(2,1)S(1)}, bf16[256,1024]{1,0:T(8,128)(2,1)S(1)}, u32[]{:S(2)}, u32[]{:S(2)}) collective-permute-start(bf16[256,1024]{1,0:T(8,128)(2,1)S(1)} %slice.788), channel_id=1, source_target_pairs={{0,1},{1,0},{2,3},{3,2},{4,5},{5,4},{6,7},{7,6},{8,9},{9,8},{10,11... | collective-permute-start | bytes 1572872 | tf_op jit(solution)/shard_map/ppermute | solution.py:67
  170.4 14.3 %collective-permute-start.16 = (bf16[256,1024]{1,0:T(8,128)(2,1)S(1)}, bf16[256,1024]{1,0:T(8,128)(2,1)S(1)}, u32[]{:S(2)}, u32[]{:S(2)}) collective-permute-start(bf16[256,1024]{1,0:T(8,128)(2,1)S(1)} %fusion.54), channel_id=1, source_target_pairs={{0,2},{2,0},{1,3},{3,1},{4,6},{6,4},{5,7},{7,5},{8,10},{10,8},{9,1... | collective-permute-start | bytes 1572872 | tf_op jit(solution)/shard_map/ppermute | solution.py:67
  206.0 271.2 %reduce-scatter.3.cloned.1.call-start = ((), (), s32[]{:S(2)}) async-start(), calls=%async_computation.9 | async-start | bytes 4718592 | tf_op jit(solution)/shard_map/reduce_scatter | solution.py:1008
  208.6 14.0 %collective-permute-start.20 = (bf16[256,1024]{1,0:T(8,128)(2,1)S(1)}, bf16[256,1024]{1,0:T(8,128)(2,1)S(1)}, u32[]{:S(2)}, u32[]{:S(2)}) collective-permute-start(bf16[256,1024]{1,0:T(8,128)(2,1)S(1)} %fusion.46), channel_id=1, source_target_pairs={{0,2},{2,0},{1,3},{3,1},{4,6},{6,4},{5,7},{7,5},{8,10},{10,8},{9,1... | collective-permute-start | bytes 1572872 | tf_op jit(solution)/shard_map/ppermute | solution.py:67
  213.8 8.9 %collective-permute-start.19 = (bf16[256,1024]{1,0:T(8,128)(2,1)S(1)}, bf16[256,1024]{1,0:T(8,128)(2,1)S(1)}, u32[]{:S(2)}, u32[]{:S(2)}) collective-permute-start(bf16[256,1024]{1,0:T(8,128)(2,1)S(1)} %slice.786), channel_id=1, source_target_pairs={{0,1},{1,0},{2,3},{3,2},{4,5},{5,4},{6,7},{7,6},{8,9},{9,8},{10,11... | collective-permute-start | bytes 1572872 | tf_op jit(solution)/shard_map/ppermute | solution.py:67
  223.9 14.3 %collective-permute-start.22 = (bf16[256,1024]{1,0:T(8,128)(2,1)S(1)}, bf16[256,1024]{1,0:T(8,128)(2,1)S(1)}, u32[]{:S(2)}, u32[]{:S(2)}) collective-permute-start(bf16[256,1024]{1,0:T(8,128)(2,1)S(1)} %fusion.55), channel_id=1, source_target_pairs={{0,2},{2,0},{1,3},{3,1},{4,6},{6,4},{5,7},{7,5},{8,10},{10,8},{9,1... | collective-permute-start | bytes 1572872 | tf_op jit(solution)/shard_map/ppermute | solution.py:67
  250.1 14.0 %collective-permute-start.26 = (bf16[256,1024]{1,0:T(8,128)(2,1)S(1)}, bf16[256,1024]{1,0:T(8,128)(2,1)S(1)}, u32[]{:S(2)}, u32[]{:S(2)}) collective-permute-start(bf16[256,1024]{1,0:T(8,128)(2,1)S(1)} %fusion.42), channel_id=1, source_target_pairs={{0,2},{2,0},{1,3},{3,1},{4,6},{6,4},{5,7},{7,5},{8,10},{10,8},{9,1... | collective-permute-start | bytes 1572872 | tf_op jit(solution)/shard_map/ppermute | solution.py:67
  254.3 9.8 %collective-permute-start.25 = (bf16[256,1024]{1,0:T(8,128)(2,1)S(1)}, bf16[256,1024]{1,0:T(8,128)(2,1)S(1)}, u32[]{:S(2)}, u32[]{:S(2)}) collective-permute-start(bf16[256,1024]{1,0:T(8,128)(2,1)S(1)} %slice.784), channel_id=1, source_target_pairs={{0,1},{1,0},{2,3},{3,2},{4,5},{5,4},{6,7},{7,6},{8,9},{9,8},{10,11... | collective-permute-start | bytes 1572872 | tf_op jit(solution)/shard_map/ppermute | solution.py:67
  265.6 21.0 %collective-permute-start.28 = (bf16[256,1024]{1,0:T(8,128)(2,1)S(1)}, bf16[256,1024]{1,0:T(8,128)(2,1)S(1)}, u32[]{:S(2)}, u32[]{:S(2)}) collective-permute-start(bf16[256,1024]{1,0:T(8,128)(2,1)S(1)} %fusion.56), channel_id=1, source_target_pairs={{0,2},{2,0},{1,3},{3,1},{4,6},{6,4},{5,7},{7,5},{8,10},{10,8},{9,1... | collective-permute-start | bytes 1572872 | tf_op jit(solution)/shard_map/ppermute | solution.py:67
  301.0 14.3 %collective-permute-start.32 = (bf16[256,1024]{1,0:T(8,128)(2,1)}, bf16[256,1024]{1,0:T(8,128)(2,1)}, u32[]{:S(2)}, u32[]{:S(2)}) collective-permute-start(bf16[256,1024]{1,0:T(8,128)(2,1)} %fusion.38), channel_id=1, source_target_pairs={{0,2},{2,0},{1,3},{3,1},{4,6},{6,4},{5,7},{7,5},{8,10},{10,8},{9,1... | collective-permute-start | bytes 1572872 | tf_op jit(solution)/shard_map/ppermute | solution.py:67
  307.1 8.2 %collective-permute-start.31 = (bf16[256,1024]{1,0:T(8,128)(2,1)}, bf16[256,1024]{1,0:T(8,128)(2,1)}, u32[]{:S(2)}, u32[]{:S(2)}) collective-permute-start(bf16[256,1024]{1,0:T(8,128)(2,1)} %slice.782), channel_id=1, source_target_pairs={{0,1},{1,0},{2,3},{3,2},{4,5},{5,4},{6,7},{7,6},{8,9},{9,8},{10,11... | collective-permute-start | bytes 1572872 | tf_op jit(solution)/shard_map/ppermute | solution.py:67
  344.3 14.3 %collective-permute-start.39 = (bf16[256,1024]{1,0:T(8,128)(2,1)S(1)}, bf16[256,1024]{1,0:T(8,128)(2,1)S(1)}, u32[]{:S(2)}, u32[]{:S(2)}) collective-permute-start(bf16[256,1024]{1,0:T(8,128)(2,1)S(1)} %get-tuple-element.516), channel_id=1, source_target_pairs={{0,2},{2,0},{1,3},{3,1},{4,6},{6,4},{5,7},{7,5},{8,10},{10,8},{9,1... | collective-permute-start | bytes 1572872 | tf_op jit(solution)/shard_map/ppermute | solution.py:67
  371.5 19.9 %collective-permute-start.43 = (bf16[256,1024]{1,0:T(8,128)(2,1)}, bf16[256,1024]{1,0:T(8,128)(2,1)}, u32[]{:S(2)}, u32[]{:S(2)}) collective-permute-start(bf16[256,1024]{1,0:T(8,128)(2,1)} %fusion.34), channel_id=1, source_target_pairs={{0,2},{2,0},{1,3},{3,1},{4,6},{6,4},{5,7},{7,5},{8,10},{10,8},{9,1... | collective-permute-start | bytes 1572872 | tf_op jit(solution)/shard_map/ppermute | solution.py:67
  391.3 281.9 %reduce-scatter.5.cloned.1.call-start = ((), (), s32[]{:S(2)}) async-start(), calls=%async_computation.10 | async-start | bytes 5898240 | tf_op jit(solution)/shard_map/reduce_scatter | solution.py:1008
  395.6 13.9 %collective-permute-start.45 = (bf16[256,1024]{1,0:T(8,128)(2,1)S(1)}, bf16[256,1024]{1,0:T(8,128)(2,1)S(1)}, u32[]{:S(2)}, u32[]{:S(2)}) collective-permute-start(bf16[256,1024]{1,0:T(8,128)(2,1)S(1)} %get-tuple-element.518), channel_id=1, source_target_pairs={{0,2},{2,0},{1,3},{3,1},{4,6},{6,4},{5,7},{7,5},{8,10},{10,8},{9,1... | collective-permute-start | bytes 1572872 | tf_op jit(solution)/shard_map/ppermute | solution.py:67
  423.7 14.1 %collective-permute-start.49 = (bf16[256,1024]{1,0:T(8,128)(2,1)S(1)}, bf16[256,1024]{1,0:T(8,128)(2,1)S(1)}, u32[]{:S(2)}, u32[]{:S(2)}) collective-permute-start(bf16[256,1024]{1,0:T(8,128)(2,1)S(1)} %fusion.31), channel_id=1, source_target_pairs={{0,2},{2,0},{1,3},{3,1},{4,6},{6,4},{5,7},{7,5},{8,10},{10,8},{9,1... | collective-permute-start | bytes 1572872 | tf_op jit(solution)/shard_map/ppermute | solution.py:67
  432.7 5.1 collective-permute-start.48
  439.2 14.3 %collective-permute-start.51 = (bf16[256,1024]{1,0:T(8,128)(2,1)S(1)}, bf16[256,1024]{1,0:T(8,128)(2,1)S(1)}, u32[]{:S(2)}, u32[]{:S(2)}) collective-permute-start(bf16[256,1024]{1,0:T(8,128)(2,1)S(1)} %get-tuple-element.520), channel_id=1, source_target_pairs={{0,2},{2,0},{1,3},{3,1},{4,6},{6,4},{5,7},{7,5},{8,10},{10,8},{9,1... | collective-permute-start | bytes 1572872 | tf_op jit(solution)/shard_map/ppermute | solution.py:67
  466.4 26.8 %collective-permute-start.55 = (bf16[256,1024]{1,0:T(8,128)(2,1)}, bf16[256,1024]{1,0:T(8,128)(2,1)}, u32[]{:S(2)}, u32[]{:S(2)}) collective-permute-start(bf16[256,1024]{1,0:T(8,128)(2,1)} %fusion.28), channel_id=1, source_target_pairs={{0,2},{2,0},{1,3},{3,1},{4,6},{6,4},{5,7},{7,5},{8,10},{10,8},{9,1... | collective-permute-start | bytes 1572872 | tf_op jit(solution)/shard_map/ppermute | solution.py:67
  497.7 13.9 %collective-permute-start.57 = (bf16[256,1024]{1,0:T(8,128)(2,1)S(1)}, bf16[256,1024]{1,0:T(8,128)(2,1)S(1)}, u32[]{:S(2)}, u32[]{:S(2)}) collective-permute-start(bf16[256,1024]{1,0:T(8,128)(2,1)S(1)} %get-tuple-element.522), channel_id=1, source_target_pairs={{0,2},{2,0},{1,3},{3,1},{4,6},{6,4},{5,7},{7,5},{8,10},{10,8},{9,1... | collective-permute-start | bytes 1572872 | tf_op jit(solution)/shard_map/ppermute | solution.py:67
  527.1 12.5 %collective-permute-start.59 = (bf16[256,1024]{1,0:T(8,128)(2,1)}, bf16[256,1024]{1,0:T(8,128)(2,1)}, u32[]{:S(2)}, u32[]{:S(2)}) collective-permute-start(bf16[256,1024]{1,0:T(8,128)(2,1)} %slice.775), channel_id=1, source_target_pairs={{0,1},{1,0},{2,3},{3,2},{4,5},{5,4},{6,7},{7,6},{8,9},{9,8},{10,11... | collective-permute-start | bytes 1572872 | tf_op jit(solution)/shard_map/ppermute | solution.py:67
  546.3 16.0 %collective-permute-start.61 = (bf16[256,1024]{1,0:T(8,128)(2,1)}, bf16[256,1024]{1,0:T(8,128)(2,1)}, u32[]{:S(2)}, u32[]{:S(2)}) collective-permute-start(bf16[256,1024]{1,0:T(8,128)(2,1)} %fusion.22), channel_id=1, source_target_pairs={{0,2},{2,0},{1,3},{3,1},{4,6},{6,4},{5,7},{7,5},{8,10},{10,8},{9,1... | collective-permute-start | bytes 1572872 | tf_op jit(solution)/shard_map/ppermute | solution.py:67
  553.0 9.3 %collective-permute-start.60 = (bf16[256,1024]{1,0:T(8,128)(2,1)}, bf16[256,1024]{1,0:T(8,128)(2,1)}, u32[]{:S(2)}, u32[]{:S(2)}) collective-permute-start(bf16[256,1024]{1,0:T(8,128)(2,1)} %slice.774), channel_id=1, source_target_pairs={{0,1},{1,0},{2,3},{3,2},{4,5},{5,4},{6,7},{7,6},{8,9},{9,8},{10,11... | collective-permute-start | bytes 1572872 | tf_op jit(solution)/shard_map/ppermute | solution.py:67
  554.3 56.0 %collective-permute-start.62 = (bf16[2,2,3,256,256]{4,3,2,1,0:T(8,128)(2,1)}, bf16[2,2,3,256,256]{4,3,2,1,0:T(8,128)(2,1)}, u32[]{:S(2)}, u32[]{:S(2)}) collective-permute-start(bf16[2,2,3,256,256]{4,3,2,1,0:T(8,128)(2,1)} %dynamic-slice_bitcast_fusion), channel_id=1, source_target_pairs={{0,4},{4,0},{8,12},{12,8},{16,20},{20,16},{24,28},{28,24},{1,5},{5... | collective-permute-start | bytes 4718600 | tf_op jit(solution)/shard_map/ppermute | solution.py:67
  555.8 57.3 %all-to-all-start.3 = ((bf16[8,2,4,32,256]{4,3,2,1,0:T(8,128)(2,1)}), bf16[8,2,4,32,256]{4,3,2,1,0:T(8,128)(2,1)}, u32[]{:S(2)}, u32[]{:S(2)}) async-start(bf16[8,2,4,32,256]{4,3,2,1,0:T(8,128)(2,1)} %copy-done.20), calls=%async_computation.4 | async-start | bytes 2097152 | tf_op jit(solution)/shard_map/all_to_all | solution.py:1049
  614.9 8.3 %collective-permute-start.64 = (bf16[128,1024]{1,0:T(8,128)(2,1)}, bf16[128,1024]{1,0:T(8,128)(2,1)S(1)}, u32[]{:S(2)}, u32[]{:S(2)}) collective-permute-start(bf16[128,1024]{1,0:T(8,128)(2,1)} %broadcast_select_fusion.3), channel_id=1, source_target_pairs={{0,2},{2,0},{1,3},{3,1},{4,6},{6,4},{5,7},{7,5},{8,10},{10,8},{9,1... | collective-permute-start | bytes 786440 | tf_op jit(solution)/shard_map/ppermute | solution.py:67
  619.2 54.0 %all-to-all-start.4 = ((bf16[32,24,1024]{2,1,0:T(8,128)(2,1)}), bf16[32,24,1024]{2,1,0:T(8,128)(2,1)}, u32[]{:S(2)}, u32[]{:S(2)}) async-start(bf16[32,24,1024]{2,1,0:T(8,128)(2,1)} %bitcast.283), calls=%async_computation.5 | async-start | bytes 3145728 | tf_op jit(solution)/shard_map/all_to_all | solution.py:842
  624.4 16.9 %collective-permute-start.65 = (bf16[128,1024]{1,0:T(8,128)(2,1)S(1)}, bf16[128,1024]{1,0:T(8,128)(2,1)S(1)}, u32[]{:S(2)}, u32[]{:S(2)}) collective-permute-start(bf16[128,1024]{1,0:T(8,128)(2,1)S(1)} %get-tuple-element.506), channel_id=1, source_target_pairs={{24,28},{8,12},{16,20},{0,4},{25,29},{9,13},{17,21},{1,5},{26,30},... | collective-permute-start | bytes 786440 | tf_op jit(solution)/shard_map/ppermute | solution.py:167
  643.8 26.5 %collective-permute-start.63 = (bf16[2,3,256,256]{3,2,1,0:T(8,128)(2,1)S(1)}, bf16[2,3,256,256]{3,2,1,0:T(8,128)(2,1)S(1)}, u32[]{:S(2)}, u32[]{:S(2)}) collective-permute-start(bf16[2,3,256,256]{3,2,1,0:T(8,128)(2,1)S(1)} %dynamic-slice_bitcast_fusion.1), channel_id=1, source_target_pairs={{0,8},{4,12},{8,0},{12,4},{16,24},{20,28},{24,16},{28,20},{1,9},{5... | collective-permute-start | bytes 2359304 | tf_op jit(solution)/shard_map/ppermute | solution.py:67
  646.7 25.4 %collective-permute-start.69 = (bf16[256,1024]{1,0:T(8,128)(2,1)S(1)}, bf16[256,1024]{1,0:T(8,128)(2,1)S(1)}, u32[]{:S(2)}, u32[]{:S(2)}) collective-permute-start(bf16[256,1024]{1,0:T(8,128)(2,1)S(1)} %pad_maximum_fusion.12), channel_id=1, source_target_pairs={{0,1},{1,0},{2,3},{3,2},{4,5},{5,4},{6,7},{7,6},{8,9},{9,8},{10,11... | collective-permute-start | bytes 1572872 | tf_op jit(solution)/shard_map/ppermute | solution.py:67
  675.0 19.4 %collective-permute-start.70 = (bf16[3,256,256]{2,1,0:T(8,128)(2,1)}, bf16[3,256,256]{2,1,0:T(8,128)(2,1)}, u32[]{:S(2)}, u32[]{:S(2)}) collective-permute-start(bf16[3,256,256]{2,1,0:T(8,128)(2,1)} %dynamic-slice_bitcast_fusion.2), channel_id=1, source_target_pairs={{0,16},{4,20},{8,24},{12,28},{16,0},{20,4},{24,8},{28,12},{1,17},{... | collective-permute-start | bytes 1179656 | tf_op jit(solution)/shard_map/ppermute | solution.py:67
  707.2 5.9 collective-permute-start.72
  713.1 17.2 %collective-permute-start.73 = (f32[27653]{0:T(1024)S(1)}, f32[27653]{0:T(1024)S(1)}, u32[]{:S(2)}, u32[]{:S(2)}) collective-permute-start(f32[27653]{0:T(1024)S(1)} %add.913), channel_id=1, source_target_pairs={{0,4},{4,0},{8,12},{12,8},{16,20},{20,16},{24,28},{28,24},{1,5},{5... | collective-permute-start | bytes 331844 | tf_op jit(solution)/shard_map/ppermute | solution.py:67
  730.3 5.9 collective-permute-start.74
  736.3 9.2 %collective-permute-start.75 = (f32[27653]{0:T(1024)S(1)}, f32[27653]{0:T(1024)}, u32[]{:S(2)}, u32[]{:S(2)}) collective-permute-start(f32[27653]{0:T(1024)S(1)} %add.915), channel_id=1, source_target_pairs={{0,16},{4,20},{8,24},{12,28},{16,0},{20,4},{24,8},{28,12},{1,17},{... | collective-permute-start | bytes 331844 | tf_op jit(solution)/shard_map/ppermute | solution.py:67
  738.0 23.6 %all-to-all-start.5 = ((bf16[8,2,3,32,256]{4,3,2,1,0:T(8,128)(2,1)}), bf16[8,2,3,32,256]{4,3,2,1,0:T(8,128)(2,1)S(1)}, u32[]{:S(2)}, u32[]{:S(2)}) async-start(bf16[8,2,3,32,256]{4,3,2,1,0:T(8,128)(2,1)} %shard_map.426), calls=%async_computation.7 | async-start | bytes 1572864 | tf_op jit(solution)/shard_map/all_to_all | solution.py:1049
  762.4 33.1 %all-to-all-start.6 = ((bf16[8,2,5,32,256]{4,3,2,1,0:T(8,128)(2,1)}), bf16[8,2,5,32,256]{4,3,2,1,0:T(8,128)(2,1)S(1)}, u32[]{:S(2)}, u32[]{:S(2)}) async-start(bf16[8,2,5,32,256]{4,3,2,1,0:T(8,128)(2,1)} %shard_map.425), calls=%async_computation.8 | async-start | bytes 2621440 | tf_op jit(solution)/shard_map/all_to_all | solution.py:1049
  (229 other events, 1641.0 us)
Sparse Core Ops, SparseCore 0:
  11.6 112.5 all-gather.6
  126.9 72.4 all-gather.8
  206.1 75.4 all-gather.10
  391.4 85.6 reduce-scatter.2
  493.3 117.5 reduce-scatter.4
